TPU v7x, 32 devices: a whole 2x2x4 slice. The times are simulated.
32 devices in a mesh: groups: 2 (over y), ctx: 4 (over z), heads: 2 (over x), rep: 2 (over core).
Axes of the slice: x: 2, y: 2, z: 4, core: 2. Of those that a mesh axis runs over, the one named last changes fastest.
Arguments:
- queries: bfloat16 [24576, 32, 128], P(('groups', 'ctx'), ('heads', 'rep')), parts along dimension 0, may hold values from -14 to 14
- keys: bfloat16 [24576, 8, 128], P(('groups', 'ctx'), 'heads'), parts along dimension 0, may hold values from -14 to 14
- values: bfloat16 [24576, 8, 128], P(('groups', 'ctx'), 'heads'), parts along dimension 0, may hold values from -6 to 6
- chosen: int32 [8, 192, 8], P('heads', ('groups', 'ctx')), parts along dimension 1, may hold values from 0 to 95, as said below
Outputs:
- attended: bfloat16 [24576, 32, 128], P(('groups', 'ctx'), ('heads', 'rep')), parts along dimension 0
There are 2 independent parts, one for each index of `groups`. A program takes and returns all parts, laid end to end along the dimension named above; each array names one. Nothing has to cross between parts.
Inputs may be any that keep to these rules, and one draw needn't show every extreme that they name: chosen[h, b, 0] = b. The other entries of a list are at most b and differ from each other, except that b itself may be repeated. For one key-value head, the 24 query blocks of one sequence shard list at most 2 distinct blocks of any other shard.
All inputs are finite; a program needn't handle non-finite values.
Results may differ from a plain program's by a relative error of at most 0.0046.
Values may be sent and summed in bfloat16 or wider, within the bound.
No kernel may reach another device: no remote copies, remote signals or barrier semaphores. Data moves between devices by JAX's collectives and lax.ppermute only.
A program may use at most 128 MiB of HBM per device.

v0:
```python
import jax
import jax.numpy as jnp
from jax import lax
from jax.sharding import PartitionSpec as P

QUERY_HEADS = 32
KEY_VALUE_HEADS = 8
REMOTE_BLOCK_MAX = 2


def attend(query_part, key_part, value_part, chosen_part):
    block_len = query_part.shape[1]
    head_dim = query_part.shape[-1]
    picks = chosen_part.shape[-1]
    scores = jnp.einsum(
        "gqeah,egkh->egaqk", query_part, key_part, preferred_element_type=jnp.float32
    ) * head_dim ** (-0.5)
    earlier = chosen_part[..., :, None] == chosen_part[..., None, :]
    before_slot = jnp.arange(picks)[:, None] > jnp.arange(picks)[None, :]
    repeated = jnp.any(earlier & before_slot[None, None], axis=-1)
    slot_open = jnp.repeat(jnp.logical_not(repeated), block_len, axis=-1)
    key_slot = jnp.arange(picks * block_len) // block_len
    key_place = jnp.arange(picks * block_len) % block_len
    query_place = jnp.arange(block_len)
    causal = (key_slot[None, :] > 0) | (key_place[None, :] <= query_place[:, None])
    visible = slot_open[:, :, None, None, :] & causal[None, None, None]
    highest = jnp.max(jnp.where(visible, scores, -jnp.inf), axis=-1, keepdims=True)
    weights = jnp.where(visible, jnp.exp(scores - highest), jnp.float32(0.0))
    totals = jnp.sum(weights, axis=-1)
    probabilities = weights.astype(jnp.bfloat16)
    attended = jnp.einsum(
        "egaqk,egkh->gqeah", probabilities, value_part, preferred_element_type=jnp.float32
    )
    scaled = attended / jnp.transpose(totals, (1, 3, 0, 2))[..., None]
    return scaled.astype(jnp.bfloat16)


def on_device(queries, keys, values, chosen):
    tokens_dev, query_heads, head_dim = queries.shape
    blocks = chosen.shape[1]
    picks = chosen.shape[2]
    block_len = tokens_dev // blocks
    heads_per_group = QUERY_HEADS // KEY_VALUE_HEADS
    used_heads = max(1, query_heads // heads_per_group)
    per_head = query_heads // used_heads
    shard_count = lax.axis_size("ctx")
    position = lax.axis_index("ctx")
    rep_index = lax.axis_index("rep")
    first_head = rep_index * query_heads // heads_per_group
    chosen_used = lax.dynamic_slice_in_dim(chosen, first_head, used_heads, 0)
    fetch_keys = lax.dynamic_slice_in_dim(keys, first_head, used_heads, 1)
    fetch_values = lax.dynamic_slice_in_dim(values, first_head, used_heads, 1)
    fetch_heads = chosen_used.shape[0]
    flat_chosen = chosen_used.reshape(fetch_heads, blocks * picks)
    needed = jnp.any(
        flat_chosen[:, :, None] == jnp.arange(shard_count * blocks, dtype=jnp.int32)[None, None, :],
        axis=1,
    )
    needed = (
        needed.reshape(fetch_heads, shard_count, blocks)
        & (jnp.arange(shard_count, dtype=jnp.int32) != position)[None, :, None]
    )
    ranking = jnp.cumsum(needed.astype(jnp.int32), axis=2) - 1
    matches = needed[..., None] & (
        ranking[..., None] == jnp.arange(REMOTE_BLOCK_MAX, dtype=jnp.int32)[None, None, None, :]
    )
    request = jnp.sum(
        matches.astype(jnp.int32) * jnp.arange(blocks, dtype=jnp.int32)[None, None, :, None], axis=2
    )
    requests_in = lax.all_to_all(request, "ctx", split_axis=1, concat_axis=1, tiled=True)
    key_blocks = jnp.transpose(fetch_keys, (1, 0, 2)).reshape(
        fetch_heads, blocks, block_len, head_dim
    )
    value_blocks = jnp.transpose(fetch_values, (1, 0, 2)).reshape(
        fetch_heads, blocks, block_len, head_dim
    )
    fetch_index = jnp.arange(fetch_heads, dtype=jnp.int32)[:, None, None]
    send_keys = key_blocks[fetch_index, requests_in].reshape(
        fetch_heads, shard_count, REMOTE_BLOCK_MAX * block_len, head_dim
    )
    send_values = value_blocks[fetch_index, requests_in].reshape(
        fetch_heads, shard_count, REMOTE_BLOCK_MAX * block_len, head_dim
    )
    got_keys, got_values = (
        lax.all_to_all(send_keys, "ctx", split_axis=1, concat_axis=1, tiled=True),
        lax.all_to_all(send_values, "ctx", split_axis=1, concat_axis=1, tiled=True),
    )
    remote_keys = got_keys.reshape(used_heads, shard_count * REMOTE_BLOCK_MAX, block_len, head_dim)
    remote_values = got_values.reshape(
        used_heads, shard_count * REMOTE_BLOCK_MAX, block_len, head_dim
    )
    rank_used = ranking.reshape(used_heads, shard_count * blocks)
    key_table = jnp.concatenate([key_blocks, remote_keys], axis=1)
    value_table = jnp.concatenate([value_blocks, remote_values], axis=1)
    source = chosen_used // blocks
    within = chosen_used % blocks
    slot_rank = jnp.take_along_axis(
        rank_used, chosen_used.reshape(used_heads, blocks * picks), axis=1
    ).reshape(used_heads, blocks, picks)
    slot_index = jnp.where(
        source == position, within, blocks + source * REMOTE_BLOCK_MAX + slot_rank
    )
    group_size = 4
    query_groups = queries.reshape(
        blocks // group_size, group_size, block_len, used_heads, per_head, head_dim
    )
    index_groups = jnp.transpose(
        slot_index.reshape(used_heads, blocks // group_size, group_size, picks), (1, 0, 2, 3)
    )
    chosen_groups = jnp.transpose(
        chosen_used.reshape(used_heads, blocks // group_size, group_size, picks), (1, 0, 2, 3)
    )
    head_index = jnp.arange(used_heads, dtype=jnp.int32)[:, None, None]

    def block_group(operands):
        query_part, index_part, chosen_part = operands
        key_part = key_table[head_index, index_part].reshape(
            used_heads, group_size, picks * block_len, head_dim
        )
        value_part = value_table[head_index, index_part].reshape(
            used_heads, group_size, picks * block_len, head_dim
        )
        return attend(query_part, key_part, value_part, chosen_part)

    result = lax.map(block_group, (query_groups, index_groups, chosen_groups))
    return result.reshape(tokens_dev, query_heads, head_dim)


def solution(mesh):
    placed = (
        P(("groups", "ctx"), ("heads", "rep"), None),
        P(("groups", "ctx"), "heads", None),
        P(("groups", "ctx"), "heads", None),
        P("heads", ("groups", "ctx"), None),
    )
    return jax.shard_map(
        on_device,
        mesh=mesh,
        in_specs=placed,
        out_specs=P(("groups", "ctx"), ("heads", "rep"), None),
        check_vma=False,
    )
```

profile of v0, /device:TPU:18, one launch (start us, length us, event | category | flops | bytes accessed | tf_op | source)
XLA Modules:
  0.0 317.8 jit_solution(5121647006889984484)
XLA Ops:
  2.5 5.2 %all-to-all-start = ((s32[2,4,2]{2,0,1:T(2,128)}), s32[2,4,2]{2,0,1:T(2,128)S(1)}, u32[]{:S(2)}, u32[]{:S(2)}) async-start(s32[2,4,2]{2,0,1:T(2,128)} %copy.57), calls=%async_computation | async-start | bytes 8192 | tf_op jit(solution)/shard_map/all_to_all | solution.py:70
  7.7 6.2 %dynamic-slice_bitcast_fusion.1 = (bf16[2,3072,128]{2,0,1:T(2,128)(2,1)}, bf16[2,3072,128]{2,0,1:T(2,128)(2,1)S(1)}) fusion(bf16[3072,4,128]{2,1,0:T(4,128)(2,1)} %param.7, s32[]{:T(128)S(6)} %select_n.118, bf16[3072,4,128]{2,1,0:T(4,128)(2,1)} %param.8), kind=kLoop, calls=%fused_computation.54 | loop fusion | bytes 6291460 | tf_op jit(solution)/shard_map/transpose | solution.py:71
  15.9 5.1 %all-to-all-start.1 = ((bf16[2,4,256,128]{3,2,0,1:T(8,128)(2,1)}), bf16[2,4,256,128]{3,2,0,1:T(8,128)(2,1)}, u32[]{:S(2)}, u32[]{:S(2)}) async-start(bf16[2,4,256,128]{3,2,0,1:T(8,128)(2,1)} %copy.60), calls=%async_computation.1 | async-start | bytes 1048576 | tf_op jit(solution)/shard_map/all_to_all | solution.py:86
  25.9 5.8 %all-to-all-done.1 = bf16[2,4,256,128]{3,2,0,1:T(8,128)(2,1)} async-done(((bf16[2,4,256,128]{3,2,0,1:T(8,128)(2,1)}), bf16[2,4,256,128]{3,2,0,1:T(8,128)(2,1)}, u32[]{:S(2)}, u32[]{:S(2)}) %all-to-all-start.1) | async-done | bytes 524320 | tf_op jit(solution)/shard_map/all_to_all | solution.py:86
  31.7 7.5 %all-to-all-start.2 = ((bf16[2,4,256,128]{3,2,0,1:T(8,128)(2,1)}), bf16[2,4,256,128]{3,2,0,1:T(8,128)(2,1)}, u32[]{:S(2)}, u32[]{:S(2)}) async-start(bf16[2,4,256,128]{3,2,0,1:T(8,128)(2,1)} %copy.63), calls=%async_computation.2 | async-start | bytes 1048576 | tf_op jit(solution)/shard_map/all_to_all | solution.py:85
  52.4 264.6 %while.13 = (s32[]{:T(128)}, bf16[6,4,128,2,4,128]{5,4,3,2,1,0:T(4,128)(2,1)}, s32[6,2,4,8]{3,2,0,1:T(4,128)S(1)}, bf16[2,32,128,128]{3,2,1,0:T(8,128)(2,1)}, s3...) while((s32[]{:T(128)}, ...), condition=%wide.region_7.8_spmd.clone, body=%wide.region_3.7_spmd.clone.sunk | while | flops 2179221504 | bytes 82130696 | solution.py:125
  56.8 8.1 %fusion.69 = f32[2,4,1024,128,4]{3,2,4,1,0:T(8,128)} fusion(bf16[2,4,1024,128,1]{3,2,4,1,0:T(8,128)(2,1)S(1)} %bitcast.94, bf16[1,4,128,2,4,128]{5,4,3,2,1,0:T(4,128)(2,1)S(1)} %constant_dynamic-slice_fusion.3), kind=kOutput, calls=%fused_computation.23.clone.1 | convolution fusion | flops 1073741824 | bytes 19922944 | tf_op jit(solution)/shard_map/while/body/eval_jaxpr/gqeah,egkh->egaqk/dot_general | solution.py:15
  67.0 19.8 %fusion.73 = (bf16[2,4,4,128,1024]{3,4,2,1,0:T(8,128)(2,1)}, f32[2,4,4,128]{3,2,1,0:T(4,128)S(1)}) fusion(f32[2,4,1024,128,4]{3,2,4,1,0:T(8,128)} %fusion.69, pred[2,4,128,1024]{2,3,1,0:T(8,128)(4,1)S(1)} %broadcast_and_fusion.4), kind=kOutput, calls=%fused_computation.81.clone.1 | output fusion | flops 29361152 | bytes 26230784 | tf_op jit(solution)/shard_map/while/body/eval_jaxpr/sub | solution.py:28
  89.0 5.4 %fusion.74 = bf16[1,4,128,2,4,128]{2,5,4,3,1,0:T(8,128)(2,1)S(1)} fusion(bf16[2,4,4,128,1024]{3,4,2,1,0:T(8,128)(2,1)} %get-tuple-element.220, bf16[2,4,1024,128,1]{3,2,1,0,4:T(8,128)(2,1)} %bitcast.95, f32[2,4,4,128]{3,2,1,0:T(4,128)S(1)} %get-tuple-element.221), kind=kOutput, calls=%fused_computation.24.clone.1 | convolution fusion | flops 1074790400 | bytes 11550720 | tf_op jit(solution)/shard_map/while/body/eval_jaxpr/egaqk,egkh->gqeah/dot_general | solution.py:31
  100.9 8.1 %fusion.69 = f32[2,4,1024,128,4]{3,2,4,1,0:T(8,128)} fusion(bf16[2,4,1024,128,1]{3,2,4,1,0:T(8,128)(2,1)S(1)} %bitcast.94, bf16[1,4,128,2,4,128]{5,4,3,2,1,0:T(4,128)(2,1)S(1)} %constant_dynamic-slice_fusion.3), kind=kOutput, calls=%fused_computation.23.clone.1 | convolution fusion | flops 1073741824 | bytes 19922944 | tf_op jit(solution)/shard_map/while/body/eval_jaxpr/gqeah,egkh->egaqk/dot_general | solution.py:15
  111.1 19.8 %fusion.73 = (bf16[2,4,4,128,1024]{3,4,2,1,0:T(8,128)(2,1)}, f32[2,4,4,128]{3,2,1,0:T(4,128)S(1)}) fusion(f32[2,4,1024,128,4]{3,2,4,1,0:T(8,128)} %fusion.69, pred[2,4,128,1024]{2,3,1,0:T(8,128)(4,1)S(1)} %broadcast_and_fusion.4), kind=kOutput, calls=%fused_computation.81.clone.1 | output fusion | flops 29361152 | bytes 26230784 | tf_op jit(solution)/shard_map/while/body/eval_jaxpr/sub | solution.py:28
  133.1 5.4 %fusion.74 = bf16[1,4,128,2,4,128]{2,5,4,3,1,0:T(8,128)(2,1)S(1)} fusion(bf16[2,4,4,128,1024]{3,4,2,1,0:T(8,128)(2,1)} %get-tuple-element.220, bf16[2,4,1024,128,1]{3,2,1,0,4:T(8,128)(2,1)} %bitcast.95, f32[2,4,4,128]{3,2,1,0:T(4,128)S(1)} %get-tuple-element.221), kind=kOutput, calls=%fused_computation.24.clone.1 | convolution fusion | flops 1074790400 | bytes 11550720 | tf_op jit(solution)/shard_map/while/body/eval_jaxpr/egaqk,egkh->gqeah/dot_general | solution.py:31
  145.0 8.1 %fusion.69 = f32[2,4,1024,128,4]{3,2,4,1,0:T(8,128)} fusion(bf16[2,4,1024,128,1]{3,2,4,1,0:T(8,128)(2,1)S(1)} %bitcast.94, bf16[1,4,128,2,4,128]{5,4,3,2,1,0:T(4,128)(2,1)S(1)} %constant_dynamic-slice_fusion.3), kind=kOutput, calls=%fused_computation.23.clone.1 | convolution fusion | flops 1073741824 | bytes 19922944 | tf_op jit(solution)/shard_map/while/body/eval_jaxpr/gqeah,egkh->egaqk/dot_general | solution.py:15
  155.2 19.8 %fusion.73 = (bf16[2,4,4,128,1024]{3,4,2,1,0:T(8,128)(2,1)}, f32[2,4,4,128]{3,2,1,0:T(4,128)S(1)}) fusion(f32[2,4,1024,128,4]{3,2,4,1,0:T(8,128)} %fusion.69, pred[2,4,128,1024]{2,3,1,0:T(8,128)(4,1)S(1)} %broadcast_and_fusion.4), kind=kOutput, calls=%fused_computation.81.clone.1 | output fusion | flops 29361152 | bytes 26230784 | tf_op jit(solution)/shard_map/while/body/eval_jaxpr/sub | solution.py:28
  177.2 5.4 %fusion.74 = bf16[1,4,128,2,4,128]{2,5,4,3,1,0:T(8,128)(2,1)S(1)} fusion(bf16[2,4,4,128,1024]{3,4,2,1,0:T(8,128)(2,1)} %get-tuple-element.220, bf16[2,4,1024,128,1]{3,2,1,0,4:T(8,128)(2,1)} %bitcast.95, f32[2,4,4,128]{3,2,1,0:T(4,128)S(1)} %get-tuple-element.221), kind=kOutput, calls=%fused_computation.24.clone.1 | convolution fusion | flops 1074790400 | bytes 11550720 | tf_op jit(solution)/shard_map/while/body/eval_jaxpr/egaqk,egkh->gqeah/dot_general | solution.py:31
  189.1 8.1 %fusion.69 = f32[2,4,1024,128,4]{3,2,4,1,0:T(8,128)} fusion(bf16[2,4,1024,128,1]{3,2,4,1,0:T(8,128)(2,1)S(1)} %bitcast.94, bf16[1,4,128,2,4,128]{5,4,3,2,1,0:T(4,128)(2,1)S(1)} %constant_dynamic-slice_fusion.3), kind=kOutput, calls=%fused_computation.23.clone.1 | convolution fusion | flops 1073741824 | bytes 19922944 | tf_op jit(solution)/shard_map/while/body/eval_jaxpr/gqeah,egkh->egaqk/dot_general | solution.py:15
  199.3 19.8 %fusion.73 = (bf16[2,4,4,128,1024]{3,4,2,1,0:T(8,128)(2,1)}, f32[2,4,4,128]{3,2,1,0:T(4,128)S(1)}) fusion(f32[2,4,1024,128,4]{3,2,4,1,0:T(8,128)} %fusion.69, pred[2,4,128,1024]{2,3,1,0:T(8,128)(4,1)S(1)} %broadcast_and_fusion.4), kind=kOutput, calls=%fused_computation.81.clone.1 | output fusion | flops 29361152 | bytes 26230784 | tf_op jit(solution)/shard_map/while/body/eval_jaxpr/sub | solution.py:28
  221.3 5.4 %fusion.74 = bf16[1,4,128,2,4,128]{2,5,4,3,1,0:T(8,128)(2,1)S(1)} fusion(bf16[2,4,4,128,1024]{3,4,2,1,0:T(8,128)(2,1)} %get-tuple-element.220, bf16[2,4,1024,128,1]{3,2,1,0,4:T(8,128)(2,1)} %bitcast.95, f32[2,4,4,128]{3,2,1,0:T(4,128)S(1)} %get-tuple-element.221), kind=kOutput, calls=%fused_computation.24.clone.1 | convolution fusion | flops 1074790400 | bytes 11550720 | tf_op jit(solution)/shard_map/while/body/eval_jaxpr/egaqk,egkh->gqeah/dot_general | solution.py:31
  233.2 8.1 %fusion.69 = f32[2,4,1024,128,4]{3,2,4,1,0:T(8,128)} fusion(bf16[2,4,1024,128,1]{3,2,4,1,0:T(8,128)(2,1)S(1)} %bitcast.94, bf16[1,4,128,2,4,128]{5,4,3,2,1,0:T(4,128)(2,1)S(1)} %constant_dynamic-slice_fusion.3), kind=kOutput, calls=%fused_computation.23.clone.1 | convolution fusion | flops 1073741824 | bytes 19922944 | tf_op jit(solution)/shard_map/while/body/eval_jaxpr/gqeah,egkh->egaqk/dot_general | solution.py:15
  243.4 19.8 %fusion.73 = (bf16[2,4,4,128,1024]{3,4,2,1,0:T(8,128)(2,1)}, f32[2,4,4,128]{3,2,1,0:T(4,128)S(1)}) fusion(f32[2,4,1024,128,4]{3,2,4,1,0:T(8,128)} %fusion.69, pred[2,4,128,1024]{2,3,1,0:T(8,128)(4,1)S(1)} %broadcast_and_fusion.4), kind=kOutput, calls=%fused_computation.81.clone.1 | output fusion | flops 29361152 | bytes 26230784 | tf_op jit(solution)/shard_map/while/body/eval_jaxpr/sub | solution.py:28
  265.4 5.4 %fusion.74 = bf16[1,4,128,2,4,128]{2,5,4,3,1,0:T(8,128)(2,1)S(1)} fusion(bf16[2,4,4,128,1024]{3,4,2,1,0:T(8,128)(2,1)} %get-tuple-element.220, bf16[2,4,1024,128,1]{3,2,1,0,4:T(8,128)(2,1)} %bitcast.95, f32[2,4,4,128]{3,2,1,0:T(4,128)S(1)} %get-tuple-element.221), kind=kOutput, calls=%fused_computation.24.clone.1 | convolution fusion | flops 1074790400 | bytes 11550720 | tf_op jit(solution)/shard_map/while/body/eval_jaxpr/egaqk,egkh->gqeah/dot_general | solution.py:31
  277.3 8.1 %fusion.69 = f32[2,4,1024,128,4]{3,2,4,1,0:T(8,128)} fusion(bf16[2,4,1024,128,1]{3,2,4,1,0:T(8,128)(2,1)S(1)} %bitcast.94, bf16[1,4,128,2,4,128]{5,4,3,2,1,0:T(4,128)(2,1)S(1)} %constant_dynamic-slice_fusion.3), kind=kOutput, calls=%fused_computation.23.clone.1 | convolution fusion | flops 1073741824 | bytes 19922944 | tf_op jit(solution)/shard_map/while/body/eval_jaxpr/gqeah,egkh->egaqk/dot_general | solution.py:15
  287.5 19.8 %fusion.73 = (bf16[2,4,4,128,1024]{3,4,2,1,0:T(8,128)(2,1)}, f32[2,4,4,128]{3,2,1,0:T(4,128)S(1)}) fusion(f32[2,4,1024,128,4]{3,2,4,1,0:T(8,128)} %fusion.69, pred[2,4,128,1024]{2,3,1,0:T(8,128)(4,1)S(1)} %broadcast_and_fusion.4), kind=kOutput, calls=%fused_computation.81.clone.1 | output fusion | flops 29361152 | bytes 26230784 | tf_op jit(solution)/shard_map/while/body/eval_jaxpr/sub | solution.py:28
  309.6 5.4 %fusion.74 = bf16[1,4,128,2,4,128]{2,5,4,3,1,0:T(8,128)(2,1)S(1)} fusion(bf16[2,4,4,128,1024]{3,4,2,1,0:T(8,128)(2,1)} %get-tuple-element.220, bf16[2,4,1024,128,1]{3,2,1,0,4:T(8,128)(2,1)} %bitcast.95, f32[2,4,4,128]{3,2,1,0:T(4,128)S(1)} %get-tuple-element.221), kind=kOutput, calls=%fused_computation.24.clone.1 | convolution fusion | flops 1074790400 | bytes 11550720 | tf_op jit(solution)/shard_map/while/body/eval_jaxpr/egaqk,egkh->gqeah/dot_general | solution.py:31
  (160 shorter events, 87.4 us)
Async XLA Ops:
  0.0 0.7 copy-start
  2.5 11.6 %all-to-all-start = ((s32[2,4,2]{2,0,1:T(2,128)}), s32[2,4,2]{2,0,1:T(2,128)S(1)}, u32[]{:S(2)}, u32[]{:S(2)}) async-start(s32[2,4,2]{2,0,1:T(2,128)} %copy.57), calls=%async_computation | async-start | bytes 8192 | tf_op jit(solution)/shard_map/all_to_all | solution.py:70
  15.9 15.7 %all-to-all-start.1 = ((bf16[2,4,256,128]{3,2,0,1:T(8,128)(2,1)}), bf16[2,4,256,128]{3,2,0,1:T(8,128)(2,1)}, u32[]{:S(2)}, u32[]{:S(2)}) async-start(bf16[2,4,256,128]{3,2,0,1:T(8,128)(2,1)} %copy.60), calls=%async_computation.1 | async-start | bytes 1048576 | tf_op jit(solution)/shard_map/all_to_all | solution.py:86
  31.7 18.2 %all-to-all-start.2 = ((bf16[2,4,256,128]{3,2,0,1:T(8,128)(2,1)}), bf16[2,4,256,128]{3,2,0,1:T(8,128)(2,1)}, u32[]{:S(2)}, u32[]{:S(2)}) async-start(bf16[2,4,256,128]{3,2,0,1:T(8,128)(2,1)} %copy.63), calls=%async_computation.2 | async-start | bytes 1048576 | tf_op jit(solution)/shard_map/all_to_all | solution.py:85
  67.0 19.9 %copy-start.2 = (bf16[2,32,128,128]{3,2,1,0:T(8,128)(2,1)S(1)}, bf16[2,32,128,128]{3,2,1,0:T(8,128)(2,1)}, u32[]{:S(2)}) copy-start(bf16[2,32,128,128]{3,2,1,0:T(8,128)(2,1)} %get-tuple-element.241) | copy-start | bytes 6291460 | tf_op jit(solution)/shard_map/while
  111.1 19.9 %copy-start.2 = (bf16[2,32,128,128]{3,2,1,0:T(8,128)(2,1)S(1)}, bf16[2,32,128,128]{3,2,1,0:T(8,128)(2,1)}, u32[]{:S(2)}) copy-start(bf16[2,32,128,128]{3,2,1,0:T(8,128)(2,1)} %get-tuple-element.241) | copy-start | bytes 6291460 | tf_op jit(solution)/shard_map/while
  155.2 19.9 %copy-start.2 = (bf16[2,32,128,128]{3,2,1,0:T(8,128)(2,1)S(1)}, bf16[2,32,128,128]{3,2,1,0:T(8,128)(2,1)}, u32[]{:S(2)}) copy-start(bf16[2,32,128,128]{3,2,1,0:T(8,128)(2,1)} %get-tuple-element.241) | copy-start | bytes 6291460 | tf_op jit(solution)/shard_map/while
  199.3 19.9 %copy-start.2 = (bf16[2,32,128,128]{3,2,1,0:T(8,128)(2,1)S(1)}, bf16[2,32,128,128]{3,2,1,0:T(8,128)(2,1)}, u32[]{:S(2)}) copy-start(bf16[2,32,128,128]{3,2,1,0:T(8,128)(2,1)} %get-tuple-element.241) | copy-start | bytes 6291460 | tf_op jit(solution)/shard_map/while
  243.4 19.9 %copy-start.2 = (bf16[2,32,128,128]{3,2,1,0:T(8,128)(2,1)S(1)}, bf16[2,32,128,128]{3,2,1,0:T(8,128)(2,1)}, u32[]{:S(2)}) copy-start(bf16[2,32,128,128]{3,2,1,0:T(8,128)(2,1)} %get-tuple-element.241) | copy-start | bytes 6291460 | tf_op jit(solution)/shard_map/while
  287.5 19.9 %copy-start.2 = (bf16[2,32,128,128]{3,2,1,0:T(8,128)(2,1)S(1)}, bf16[2,32,128,128]{3,2,1,0:T(8,128)(2,1)}, u32[]{:S(2)}) copy-start(bf16[2,32,128,128]{3,2,1,0:T(8,128)(2,1)} %get-tuple-element.241) | copy-start | bytes 6291460 | tf_op jit(solution)/shard_map/while
  317.1 0.7 copy-start.1
where the time goes:
time: 323 us; the launch traced here: 318 us
  other arithmetic  136 us (42%)
  matrix products  81 us (25%)
  local copies, waits for them, and re-layouts  72.9 us (23%)
  starting transfers between devices  17.8 us (6%)
  waiting for transfers between devices  9.86 us (3%)
    sub x6, other arithmetic, attend(): weights = jnp.where(visible, jnp.exp(scores - highest), jnp.float32(0.0))  119 us
    dot_general x6, matrix products, attend(): jnp.einsum('gqeah,egkh->egaqk', query_part, key_part, preferred_element_t...  48.4 us
    dot_general x6, matrix products, attend(): jnp.einsum('egaqk,egkh->gqeah', probabilities, value_part, preferred_elem...  32.6 us
    gather x6, local copies, waits for them, and re-layouts, block_group(): key_table[head_index, index_part]  15.3 us
    gather x6, local copies, waits for them, and re-layouts, block_group(): value_table[head_index, index_part]  13 us
    dynamic_update_slice x12, local copies, waits for them, and re-layouts, on_device(): result = lax.map(block_group, (query_groups, index_groups, chosen_groups))  12.3 us
    dynamic_slice x6, local copies, waits for them, and re-layouts, on_device(): result = lax.map(block_group, (query_groups, index_groups, chosen_groups))  9.55 us
    and x6, other arithmetic, attend(): visible = slot_open[:, :, None, None, :] & causal[None, None, None]  8.44 us
  transfers between devices with their start and end apart: 3, of which 2 were waited for; matrix products, arithmetic and copies ran while one was open for 6% of the time, Pallas kernels for 0%

commit v1 on v0

v1 whole, which is shorter than its diff:
```python
import functools

import jax
import jax.numpy as jnp
from jax import lax
from jax.experimental import pallas as pl
from jax.experimental.pallas import tpu as pltpu
from jax.sharding import PartitionSpec as P

QUERY_HEADS = 32
KEY_VALUE_HEADS = 8
REMOTE_BLOCK_MAX = 2
GROUP = QUERY_HEADS // KEY_VALUE_HEADS
LOG2E = 1.4426950408889634
MASKED = -1e30
CLOSED = 3e38
SAFE_TOTAL = 2.0**100


def block_rows(index, block_len):
    return pl.ds(pl.multiple_of(index * block_len, block_len), block_len)


def relayout_kernel(
    first_ref, keys_ref, values_ref, keys_out, values_out, keys_wide, values_wide,
    *, step_blocks, kv_heads, used, block_len,
):
    first = first_ref[0]
    keys_wide[...] = keys_ref[...].astype(jnp.float32)
    values_wide[...] = values_ref[...].astype(jnp.float32)
    for block in range(step_blocks):
        rows = slice(block * block_len, (block + 1) * block_len)
        for head in range(used):
            picked = pl.ds(block * block_len * kv_heads + first + head, block_len, stride=kv_heads)
            keys_out[head, rows, :] = keys_wide[picked, :].astype(jnp.bfloat16)
            values_out[head, rows, :] = values_wide[picked, :].T.astype(jnp.bfloat16)


def relayout(first, keys, values, used, block_len, step_blocks):
    tokens, kv_heads, head_dim = keys.shape
    rows = step_blocks * block_len
    taken = pl.BlockSpec((rows * kv_heads, head_dim), lambda g, *_: (g, 0))
    given = pl.BlockSpec((used, rows, head_dim), lambda g, *_: (0, g, 0))
    table = jax.ShapeDtypeStruct((used, tokens, head_dim), jnp.bfloat16)
    return pl.pallas_call(
        functools.partial(
            relayout_kernel, step_blocks=step_blocks, kv_heads=kv_heads, used=used,
            block_len=block_len,
        ),
        grid_spec=pltpu.PrefetchScalarGridSpec(
            num_scalar_prefetch=1,
            grid=(tokens // rows,),
            in_specs=[taken, taken],
            out_specs=[given, given],
            scratch_shapes=[pltpu.VMEM((rows * kv_heads, head_dim), jnp.float32)] * 2,
        ),
        out_shape=[table, table],
        compiler_params=pltpu.CompilerParams(vmem_limit_bytes=32 * 2**20),
        name="relayout",
    )(
        first,
        keys.reshape(tokens * kv_heads, head_dim),
        values.reshape(tokens * kv_heads, head_dim),
    )


def pack_kernel(request, keys_ref, values_ref, *rest, shifts, used, block_len):
    outs, (clear_ref, sems) = rest[:shifts], rest[shifts:]
    clear_ref[...] = jnp.zeros_like(clear_ref)
    copies = []
    for shift in range(shifts):
        for head in range(used):
            for turn in range(REMOTE_BLOCK_MAX):
                at = (shift * used + head) * REMOTE_BLOCK_MAX + turn
                source = block_rows(request[at], block_len)
                target = pl.ds(turn * block_len, block_len)
                for kind, table in enumerate((keys_ref, values_ref)):
                    copies.append(
                        pltpu.make_async_copy(
                            table.at[head, source],
                            outs[shift].at[kind, head, target],
                            sems.at[2 * at + kind],
                        )
                    )
    for copy in copies:
        copy.start()
    for copy in copies:
        copy.wait()


def pack(request, key_table, value_table, shifts, block_len, row_shape):
    used, _, head_dim = key_table.shape
    anywhere = pl.BlockSpec(memory_space=pl.ANY)
    parcel = jax.ShapeDtypeStruct(
        (2, used, REMOTE_BLOCK_MAX * block_len, head_dim), jnp.bfloat16
    )
    return pl.pallas_call(
        functools.partial(pack_kernel, shifts=shifts, used=used, block_len=block_len),
        grid_spec=pltpu.PrefetchScalarGridSpec(
            num_scalar_prefetch=1,
            grid=(1,),
            in_specs=[anywhere, anywhere],
            out_specs=[anywhere] * shifts + [pl.BlockSpec(row_shape, lambda g, *_: (0, 0))],
            scratch_shapes=[pltpu.SemaphoreType.DMA((2 * shifts * used * REMOTE_BLOCK_MAX,))],
        ),
        out_shape=[parcel] * shifts + [jax.ShapeDtypeStruct(row_shape, jnp.float32)],
        name="pack",
    )(request, key_table, value_table)


def split_heads(rows, used):
    count, head_dim = rows.shape
    if used == 1:
        return (rows,)
    wide = rows.astype(jnp.float32).reshape(count // 16, 2, 8, head_dim)
    even, odd = wide[:, 0], wide[:, 1]
    upper = lax.broadcasted_iota(jnp.int32, even.shape, 1) < GROUP
    first = jnp.where(upper, even, pltpu.roll(odd, GROUP, 1))
    second = jnp.where(upper, pltpu.roll(even, GROUP, 1), odd)
    return tuple(x.reshape(count // 2, head_dim).astype(jnp.bfloat16) for x in (first, second))


def join_heads(first, *others):
    count, head_dim = first.shape
    if not others:
        return first.astype(jnp.bfloat16)
    (second,) = others
    first = first.reshape(count // 8, 8, head_dim)
    second = second.reshape(count // 8, 8, head_dim)
    upper = lax.broadcasted_iota(jnp.int32, first.shape, 1) < GROUP
    even = jnp.where(upper, first, pltpu.roll(second, GROUP, 1))
    odd = jnp.where(upper, pltpu.roll(first, GROUP, 1), second)
    return jnp.stack([even, odd], axis=1).reshape(count * 2, head_dim).astype(jnp.bfloat16)


def score(key_rows, query):
    return lax.dot_general(
        key_rows, query, (((1,), (1,)), ((), ())), preferred_element_type=jnp.float32
    )


def causal(scores):
    key = lax.broadcasted_iota(jnp.int32, scores.shape, 0)
    per_head = scores.shape[1] // scores.shape[0]
    token = lax.broadcasted_iota(jnp.int32, scores.shape, 1) // per_head
    return jnp.where(key <= token, scores, MASKED)


def fold(weights):
    return jnp.sum(weights.reshape(weights.shape[0] // 8, 8, weights.shape[1]), axis=0)


def weigh(scores, highest, slots, scale, block_len):
    parts = []
    for turn, slot in enumerate(slots):
        shift = jnp.where(slot < 0, CLOSED, highest)
        parts.append(
            jnp.exp2(scores[turn * block_len : (turn + 1) * block_len] * scale - shift)
        )
    return jnp.concatenate(parts, axis=0)


def local_kernel(
    slots_ref, counts_ref, queries_ref, keys_ref, values_ref, clear_ref,
    sums_ref, totals_ref, highest_ref, bad_ref,
    *, step_blocks, used, picks, block_len, scale,
):
    step = pl.program_id(0)

    def gather(ref, head, slots, axis):
        return jnp.concatenate(
            [ref[head, block_rows(jnp.maximum(s, 0), block_len), :] for s in slots], axis=axis
        )

    def query_rows(block):
        rows = queries_ref.shape[0] // step_blocks
        return queries_ref[pl.ds(pl.multiple_of(block * rows, rows), rows), :]

    def attend(block, count):
        for head, query in enumerate(split_heads(query_rows(block), used)):
            item = block * used + head
            at = ((step * step_blocks + block) * used + head) * picks
            slots = [slots_ref[at + turn] for turn in range(count)]
            scores = score(gather(keys_ref, head, slots, 0), query)
            own = causal(scores[:block_len])
            highest = jnp.max(own, axis=0, keepdims=True) * scale
            scores = jnp.concatenate([own, scores[block_len:]], axis=0) if count > 1 else own
            weights = weigh(scores, highest, slots, scale, block_len)
            totals = fold(weights)
            highest_ref[item] = jnp.broadcast_to(highest, totals.shape)
            totals_ref[item] = totals
            bad_ref[...] = jnp.maximum(bad_ref[...], jnp.where(totals < SAFE_TOTAL, 0.0, 1.0))
            sums_ref[item] = jnp.dot(
                gather(values_ref, head, slots, 1),
                weights.astype(jnp.bfloat16),
                preferred_element_type=jnp.float32,
            )

    def one_block(block, carry):
        count = counts_ref[step * step_blocks + block]
        lax.switch(
            count - 1, [functools.partial(attend, block, n) for n in range(1, picks + 1)]
        )
        return carry

    def mend(block, carry):
        for head, query in enumerate(split_heads(query_rows(block), used)):
            item = block * used + head
            at = ((step * step_blocks + block) * used + head) * picks

            def slot_scores(turn, query=query, head=head, at=at):
                slot = slots_ref[at + turn]
                scores = score(gather(keys_ref, head, [slot], 0), query)
                return slot, jnp.where(turn == 0, causal(scores), scores)

            def raise_highest(turn, highest, slot_scores=slot_scores):
                slot, scores = slot_scores(turn)
                found = jnp.max(scores, axis=0, keepdims=True) * scale
                return jnp.where(slot < 0, highest, jnp.maximum(highest, found))

            highest = lax.fori_loop(
                0, picks, raise_highest, jnp.full((1, query.shape[0]), MASKED, jnp.float32)
            )
            highest_ref[item] = jnp.broadcast_to(highest, highest_ref.shape[1:])
            totals_ref[item] = jnp.zeros(totals_ref.shape[1:], jnp.float32)
            sums_ref[item] = jnp.zeros(sums_ref.shape[1:], jnp.float32)

            def add(turn, carry, slot_scores=slot_scores, item=item, head=head):
                slot, scores = slot_scores(turn)
                weights = weigh(scores, highest_ref[item][:1], [slot], scale, block_len)
                totals_ref[item] += fold(weights)
                sums_ref[item] += jnp.dot(
                    gather(values_ref, head, [slot], 1),
                    weights.astype(jnp.bfloat16),
                    preferred_element_type=jnp.float32,
                )
                return carry

            lax.fori_loop(0, picks, add, 0)
        return carry

    bad_ref[...] = clear_ref[...]
    lax.fori_loop(0, step_blocks, one_block, 0)

    @pl.when(jnp.max(bad_ref[...]) > 0.0)
    def _():
        lax.fori_loop(0, step_blocks, mend, 0)


def remote_kernel(
    slots_ref, counts_ref, queries_ref, sums_ref, totals_ref, highest_ref, *rest,
    shifts, step_blocks, used, picks, block_len, scale,
):
    parcels, (out_ref, keys_ref, values_ref, bad_ref, sems) = rest[:shifts], rest[shifts:]
    step = pl.program_id(0)
    parcel_rows = REMOTE_BLOCK_MAX * block_len

    @pl.when(step == 0)
    def _():
        copies = []
        for shift in range(shifts):
            place = pl.ds(shift * parcel_rows, parcel_rows)
            for head in range(used):
                for kind, table in enumerate((keys_ref, values_ref)):
                    copies.append(
                        pltpu.make_async_copy(
                            parcels[shift].at[kind, head],
                            table.at[head, place],
                            sems.at[(shift * used + head) * 2 + kind],
                        )
                    )
        for copy in copies:
            copy.start()
        for copy in copies:
            copy.wait()

    def gather(ref, head, slots, axis):
        return jnp.concatenate(
            [ref[head, block_rows(jnp.maximum(s, 0), block_len), :] for s in slots], axis=axis
        )

    def block_rows_of(block):
        rows = queries_ref.shape[0] // step_blocks
        return pl.ds(pl.multiple_of(block * rows, rows), rows)

    def finish(block, shares):
        parts = []
        for sums, totals in shares:
            parts.append((sums * (1.0 / jnp.sum(totals, axis=0, keepdims=True))).T)
        out_ref[block_rows_of(block), :] = join_heads(*parts)

    def attend(block, count):
        shares = []
        for head, query in enumerate(split_heads(queries_ref[block_rows_of(block), :], used)):
            item = block * used + head
            sums, totals = sums_ref[item], totals_ref[item]
            if count:
                at = ((step * step_blocks + block) * used + head) * picks
                slots = [slots_ref[at + turn] for turn in range(count)]
                scores = score(gather(keys_ref, head, slots, 0), query)
                weights = weigh(scores, highest_ref[item][:1], slots, scale, block_len)
                totals = totals + fold(weights)
                bad_ref[...] = jnp.maximum(
                    bad_ref[...], jnp.where(totals < 2 * SAFE_TOTAL, 0.0, 1.0)
                )
                sums = sums + jnp.dot(
                    gather(values_ref, head, slots, 1),
                    weights.astype(jnp.bfloat16),
                    preferred_element_type=jnp.float32,
                )
            shares.append((sums, totals))
        finish(block, shares)

    def one_block(block, carry):
        count = counts_ref[step * step_blocks + block]
        lax.switch(count, [functools.partial(attend, block, n) for n in range(picks)])
        return carry

    def mend(block, carry):
        shares = []
        for head, query in enumerate(split_heads(queries_ref[block_rows_of(block), :], used)):
            item = block * used + head
            at = ((step * step_blocks + block) * used + head) * picks
            before = highest_ref[item][:1]

            def slot_scores(turn, query=query, head=head, at=at):
                slot = slots_ref[at + turn]
                return slot, score(gather(keys_ref, head, [slot], 0), query)

            def raise_highest(turn, highest, slot_scores=slot_scores):
                slot, scores = slot_scores(turn)
                found = jnp.max(scores, axis=0, keepdims=True) * scale
                return jnp.where(slot < 0, highest, jnp.maximum(highest, found))

            highest = lax.fori_loop(0, picks - 1, raise_highest, before)
            shrink = jnp.exp2(before - highest)

            def add(turn, carry, slot_scores=slot_scores, head=head, highest=highest):
                sums, totals = carry
                slot, scores = slot_scores(turn)
                weights = weigh(scores, highest, [slot], scale, block_len)
                sums = sums + jnp.dot(
                    gather(values_ref, head, [slot], 1),
                    weights.astype(jnp.bfloat16),
                    preferred_element_type=jnp.float32,
                )
                return sums, totals + fold(weights)

            shares.append(
                lax.fori_loop(
                    0, picks - 1, add, (sums_ref[item] * shrink, totals_ref[item] * shrink)
                )
            )
        finish(block, shares)
        return carry

    bad_ref[...] = jnp.zeros_like(bad_ref)
    lax.fori_loop(0, step_blocks, one_block, 0)

    @pl.when(jnp.max(bad_ref[...]) > 0.0)
    def _():
        lax.fori_loop(0, step_blocks, mend, 0)


def compact(open_slot, index):
    picks = index.shape[-1]
    before = jnp.arange(picks)[:, None] < jnp.arange(picks)[None, :]
    place = jnp.sum(open_slot[..., :, None] & before, axis=-2)
    here = open_slot[..., :, None] & (place[..., :, None] == jnp.arange(picks))
    packed = jnp.sum(jnp.where(here, index[..., :, None] + 1, 0), axis=-2) - 1
    return packed, jnp.sum(open_slot, axis=-1)


def on_device(queries, keys, values, chosen):
    tokens, query_heads, head_dim = queries.shape
    blocks, picks = chosen.shape[1:]
    block_len = tokens // blocks
    used = max(1, query_heads // GROUP)
    per_head = query_heads // used
    shards = lax.axis_size("ctx")
    shifts = shards - 1
    position = lax.axis_index("ctx")
    base = position * blocks
    first = lax.axis_index("rep") * query_heads // GROUP
    scale = LOG2E * head_dim**-0.5
    step_blocks = next(n for n in (6, 4, 3, 2, 1) if blocks % n == 0)
    steps = blocks // step_blocks
    item_rows = per_head * block_len

    lists = lax.dynamic_slice_in_dim(chosen, first, used, 0)
    wanted = jnp.stack(
        [
            lax.ppermute(lists, "ctx", [(j, j - d) for j in range(d, shards)])
            for d in range(1, shards)
        ]
    )
    key_table, value_table = relayout(
        first.reshape(1), keys, values, used, block_len, step_blocks
    )
    within = wanted - base
    mine = (within >= 0) & (within < blocks)
    request = jnp.stack(
        [
            jnp.min(jnp.where(mine, within, blocks - 1), axis=(2, 3)),
            jnp.max(jnp.where(mine, within, 0), axis=(2, 3)),
        ],
        axis=-1,
    )
    *parcels, clear = pack(
        request.reshape(-1), key_table, value_table, shifts, block_len, (8, item_rows)
    )
    arrived = [
        lax.ppermute(parcel, "ctx", [(i, i + d) for i in range(shards - d)])
        for d, parcel in zip(range(1, shards), parcels)
    ]

    local = lists >= base
    repeated = (lists == (base + jnp.arange(blocks))[None, :, None]) & (jnp.arange(picks) > 0)
    local_slots, local_count = compact(local & ~repeated, lists - base)
    shard_of = lists // blocks
    from_shard = shard_of[..., None] == jnp.arange(shards)
    lowest = jnp.min(
        jnp.where(from_shard, lists[..., None], shards * blocks), axis=(1, 2), keepdims=True
    )
    is_lowest = jnp.any(from_shard & (lists[..., None] == lowest), axis=-1)
    remote_index = (position - 1 - shard_of) * REMOTE_BLOCK_MAX + jnp.where(is_lowest, 0, 1)
    remote_slots, remote_count = compact(~local, remote_index)

    def table(slots):
        return jnp.transpose(slots, (1, 0, 2)).reshape(-1)

    query_spec = pl.BlockSpec(
        (step_blocks * block_len * query_heads, head_dim), lambda g, *_: (g, 0)
    )
    table_spec = pl.BlockSpec(key_table.shape, lambda g, *_: (0, 0, 0))
    sums_spec = pl.BlockSpec((step_blocks * used, head_dim, item_rows), lambda g, *_: (g, 0, 0))
    row_spec = pl.BlockSpec((step_blocks * used, 8, item_rows), lambda g, *_: (g, 0, 0))
    sums_shape = jax.ShapeDtypeStruct((blocks * used, head_dim, item_rows), jnp.float32)
    row_shape = jax.ShapeDtypeStruct((blocks * used, 8, item_rows), jnp.float32)
    sizes = dict(
        step_blocks=step_blocks, used=used, picks=picks, block_len=block_len, scale=scale
    )
    query_rows = queries.reshape(tokens * query_heads, head_dim)
    sums, totals, highest = pl.pallas_call(
        functools.partial(local_kernel, **sizes),
        grid_spec=pltpu.PrefetchScalarGridSpec(
            num_scalar_prefetch=2,
            grid=(steps,),
            in_specs=[
                query_spec, table_spec, table_spec,
                pl.BlockSpec(clear.shape, lambda g, *_: (0, 0)),
            ],
            out_specs=[sums_spec, row_spec, row_spec],
            scratch_shapes=[pltpu.VMEM((8, item_rows), jnp.float32)],
        ),
        out_shape=[sums_shape, row_shape, row_shape],
        compiler_params=pltpu.CompilerParams(vmem_limit_bytes=40 * 2**20),
        cost_estimate=pl.CostEstimate(
            flops=3 * tokens * query_heads * picks * block_len * head_dim,
            bytes_accessed=32 * 2**20,
            transcendentals=tokens * query_heads * picks * block_len,
        ),
        name="local_part",
    )(
        table(local_slots), jnp.max(local_count, axis=0), query_rows, key_table, value_table,
        clear,
    )

    remote_rows = shifts * REMOTE_BLOCK_MAX * block_len
    out = pl.pallas_call(
        functools.partial(remote_kernel, shifts=shifts, **sizes),
        grid_spec=pltpu.PrefetchScalarGridSpec(
            num_scalar_prefetch=2,
            grid=(steps,),
            in_specs=[query_spec, sums_spec, row_spec, row_spec]
            + [pl.BlockSpec(memory_space=pl.ANY)] * shifts,
            out_specs=query_spec,
            scratch_shapes=[
                pltpu.VMEM((used, remote_rows, head_dim), jnp.bfloat16),
                pltpu.VMEM((used, remote_rows, head_dim), jnp.bfloat16),
                pltpu.VMEM((8, item_rows), jnp.float32),
                pltpu.SemaphoreType.DMA((2 * used * shifts,)),
            ],
        ),
        out_shape=jax.ShapeDtypeStruct(query_rows.shape, jnp.bfloat16),
        compiler_params=pltpu.CompilerParams(vmem_limit_bytes=40 * 2**20),
        name="remote_part",
    )(
        table(remote_slots), jnp.max(remote_count, axis=0), query_rows,
        sums, totals, highest, *arrived,
    )
    return out.reshape(tokens, query_heads, head_dim)


def solution(mesh):
    return jax.shard_map(
        on_device,
        mesh=mesh,
        in_specs=(
            P(("groups", "ctx"), ("heads", "rep"), None),
            P(("groups", "ctx"), "heads", None),
            P(("groups", "ctx"), "heads", None),
            P("heads", ("groups", "ctx"), None),
        ),
        out_specs=P(("groups", "ctx"), ("heads", "rep"), None),
        check_vma=False,
    )
```

time: 323 us -> 112 us (0.35); the launches traced: 318 us -> 112 us
  other arithmetic: 136 us -> 1.66 us
  Pallas kernels: 0 us -> 85.1 us
  matrix products: 81 us -> 0 us
  local copies, waits for them, and re-layouts: 72.9 us -> 13.7 us
  waiting for transfers between devices: 9.86 us -> 0.02 us
  starting transfers between devices: 17.8 us -> 10.7 us
    sub x7 -> x2, other arithmetic: 119 us -> 0.01 us  [compact(): packed = jnp.sum(jnp.where(here, index[..., :, None] + 1, 0), axis=-2) - 1]
    pallas_call x0 -> x4, Pallas kernels: none -> 85.1 us  [the longest x1 29.8 us: on_device(): pl.pallas_call(functools.partial(local_kernel, **sizes), grid_spec=pltpu....]
    dot_general x12 -> x0, matrix products: 81 us -> none  [the longest x6 48.4 us: attend(): jnp.einsum('gqeah,egkh->egaqk', query_part, key_part, preferred_element_t...]
    gather x17 -> x0, local copies, waits for them, and re-layouts: 34.1 us -> none  [the longest x6 15.3 us: block_group(): key_table[head_index, index_part]]
    all_to_all x3 -> x0, starting transfers between devices: 17.8 us -> none  [the longest x1 7.47 us: on_device(): lax.all_to_all(send_keys, 'ctx', split_axis=1, concat_axis=1, tiled=True)]
    dynamic_update_slice x12 -> x0, local copies, waits for them, and re-layouts: 12.3 us -> none  [on_device(): result = lax.map(block_group, (query_groups, index_groups, chosen_groups))]
    unnamed x5 -> x20, local copies, waits for them, and re-layouts: 1.51 us -> 12.4 us
    ppermute x0 -> x6, starting transfers between devices: none -> 10.7 us  [the longest x3 5.89 us: on_device(): lax.ppermute(parcel, 'ctx', [(i, i + d) for i in range(shards - d)])]
  transfers between devices with their start and end apart: 3 -> 6, of which waited for: 2 -> 0; matrix products, arithmetic and copies ran while one was open for 6% -> 1% of each run, Pallas kernels for 0% -> 28%
where the time goes in v1:
time: 112 us
  Pallas kernels  85.1 us (76%)
  local copies, waits for them, and re-layouts  13.7 us (12%)
  starting transfers between devices  10.7 us (10%)
  other arithmetic  1.66 us (1%)
    pallas_call x1, Pallas kernels, on_device(): pl.pallas_call(functools.partial(local_kernel, **sizes), grid_spec=pltpu....  29.8 us
    pallas_call x1, Pallas kernels, on_device(): pl.pallas_call(functools.partial(remote_kernel, shifts=shifts, **sizes),...  27.2 us
    pallas_call x1, Pallas kernels, pack(): pl.pallas_call(functools.partial(pack_kernel, shifts=shifts, used=used, b...  26.4 us
    unnamed x20, local copies, waits for them, and re-layouts  12.4 us
    ppermute x3, starting transfers between devices, on_device(): lax.ppermute(parcel, 'ctx', [(i, i + d) for i in range(shards - d)])  5.89 us
    ppermute x3, starting transfers between devices, on_device(): lax.ppermute(lists, 'ctx', [(j, j - d) for j in range(d, shards)])  4.81 us
  transfers between devices with their start and end apart: 6, of which 0 were waited for; matrix products, arithmetic and copies ran while one was open for 1% of the time, Pallas kernels for 28%

profile of v1, /device:TPU:18, one launch (start us, length us, event | category | flops | bytes accessed | tf_op | source)
XLA Modules:
  0.0 111.5 jit_solution(2146903253523195442)
XLA Ops:
  0.0 0.8 convert_reduce_fusion.2
  0.8 2.2 %collective-permute-start.1 = (s32[2,24,8]{1,2,0:T(8,128)S(1)}, s32[2,24,8]{1,2,0:T(8,128)S(1)}, u32[]{:S(2)}, u32[]{:S(2)}) collective-permute-start(s32[2,24,8]{1,2,0:T(8,128)S(1)} %get-tuple-element.29), channel_id=1, source_target_pairs={{8,0},{12,4},{9,1},{13,5},{10,2},{14,6},{11,3},{15,7},{24,16},{28,... | collective-permute-start | bytes 4616 | tf_op jit(solution)/shard_map/ppermute | solution.py:393
  3.0 0.7 collective-permute-start.2
  3.7 1.9 %collective-permute-start = (s32[2,24,8]{1,2,0:T(8,128)S(1)}, s32[2,24,8]{1,2,0:T(8,128)S(1)}, u32[]{:S(2)}, u32[]{:S(2)}) collective-permute-start(s32[2,24,8]{1,2,0:T(8,128)S(1)} %get-tuple-element.29), channel_id=1, source_target_pairs={{4,0},{8,4},{12,8},{5,1},{9,5},{13,9},{6,2},{10,6},{14,10},{7,3},{... | collective-permute-start | bytes 4616 | tf_op jit(solution)/shard_map/ppermute | solution.py:393
  5.7 0.2 select_reduce_fusion.2
  6.3 0.1 reshape.55.slots_ref
  6.5 0.1 reshape.57.slots_ref
  6.6 1.9 %copy-done.1 = bf16[3072,4,128]{2,1,0:T(4,128)(2,1)S(1)} copy-done((bf16[3072,4,128]{2,1,0:T(4,128)(2,1)S(1)}, bf16[3072,4,128]{2,1,0:T(4,128)(2,1)}, u32[]{:S(2)}) %copy-start.1) | copy-done | bytes 3145752
  8.5 1.9 %copy-done.2 = bf16[3072,4,128]{2,1,0:T(4,128)(2,1)S(1)} copy-done((bf16[3072,4,128]{2,1,0:T(4,128)(2,1)S(1)}, bf16[3072,4,128]{2,1,0:T(4,128)(2,1)}, u32[]{:S(2)}) %copy-start.2) | copy-done | bytes 3145752
  10.4 1.7 %relayout.1 = (bf16[2,3072,128]{2,1,0:T(8,128)(2,1)S(1)}, bf16[2,3072,128]{2,1,0:T(8,128)(2,1)S(1)}) custom-call(s32[1]{0:T(128)} %bitcast.3.first_ref, bf16[12288,128]{1,0:T(8,128)(2,1)S(1)} %bitcast.18, bf16[12288,128]{1,0:T(8,128)(2,1)S(1)} %bitcast.19), custom_call_target="tpu_custom_call" | custom-call | tf_op jit(solution)/shard_map/relayout/pallas_call | solution.py:45
  12.1 1.1 %copy-done.3 = bf16[2,3072,128]{2,1,0:T(8,128)(2,1)} copy-done((bf16[2,3072,128]{2,1,0:T(8,128)(2,1)}, bf16[2,3072,128]{2,1,0:T(8,128)(2,1)S(1)}, u32[]{:S(2)}) %copy-start.3) | copy-done | bytes 1572888
  13.2 1.2 %copy-done.5 = bf16[2,3072,128]{2,1,0:T(8,128)(2,1)} copy-done((bf16[2,3072,128]{2,1,0:T(8,128)(2,1)}, bf16[2,3072,128]{2,1,0:T(8,128)(2,1)S(1)}, u32[]{:S(2)}) %copy-start.5) | copy-done | bytes 1572888
  14.4 0.3 select_reduce_fusion.4
  15.0 0.7 reshape.61.request
  15.7 26.4 %pack.1 = (bf16[2,2,256,128]{3,2,1,0:T(8,128)(2,1)}, bf16[2,2,256,128]{3,2,1,0:T(8,128)(2,1)}, bf16[2,2,256,128]{3,2,1,0:T(8,128)(2,1)}, f32[8,512]{1,0:T(8,128)}) custom-call(s32[12]{0:T(128)} %reshape.61.request, bf16[2,3072,128]{2,1,0:T(8,128)(2,1)} %copy-done.3, bf16[2,3072,128]{2,1,0:T(8,128)(2,1)} %copy-done.5), custom_call_target="tpu_custom_call" | custom-call | tf_op jit(solution)/shard_map/pack/pallas_call | solution.py:97
  42.1 3.9 %collective-permute-start.3 = (bf16[2,2,256,128]{3,2,1,0:T(8,128)(2,1)}, bf16[2,2,256,128]{3,2,1,0:T(8,128)(2,1)S(1)}, u32[]{:S(2)}, u32[]{:S(2)}) collective-permute-start(bf16[2,2,256,128]{3,2,1,0:T(8,128)(2,1)} %get-tuple-element.20), channel_id=1, source_target_pairs={{0,4},{4,8},{8,12},{1,5},{5,9},{9,13},{2,6},{6,10},{10,14},{3,7},{... | collective-permute-start | bytes 786440 | tf_op jit(solution)/shard_map/ppermute | solution.py:413
  46.0 1.3 %collective-permute-start.4 = (bf16[2,2,256,128]{3,2,1,0:T(8,128)(2,1)}, bf16[2,2,256,128]{3,2,1,0:T(8,128)(2,1)S(1)}, u32[]{:S(2)}, u32[]{:S(2)}) collective-permute-start(bf16[2,2,256,128]{3,2,1,0:T(8,128)(2,1)} %get-tuple-element.21), channel_id=1, source_target_pairs={{0,8},{4,12},{1,9},{5,13},{2,10},{6,14},{3,11},{7,15},{16,24},{20,... | collective-permute-start | bytes 786440 | tf_op jit(solution)/shard_map/ppermute | solution.py:413
  47.3 0.7 collective-permute-start.5
  48.0 2.8 %copy-done = bf16[3072,8,128]{2,1,0:T(8,128)(2,1)S(1)} copy-done((bf16[3072,8,128]{2,1,0:T(8,128)(2,1)S(1)}, bf16[3072,8,128]{2,1,0:T(8,128)(2,1)}, u32[]{:S(2)}) %copy-start) | copy-done | bytes 6291480
  50.8 1.4 %copy-done.4 = bf16[2,3072,128]{2,1,0:T(8,128)(2,1)S(1)} copy-done((bf16[2,3072,128]{2,1,0:T(8,128)(2,1)S(1)}, bf16[2,3072,128]{2,1,0:T(8,128)(2,1)}, u32[]{:S(2)}) %copy-start.4) | copy-done | bytes 1572888
  52.2 1.4 %copy-done.6 = bf16[2,3072,128]{2,1,0:T(8,128)(2,1)S(1)} copy-done((bf16[2,3072,128]{2,1,0:T(8,128)(2,1)S(1)}, bf16[2,3072,128]{2,1,0:T(8,128)(2,1)}, u32[]{:S(2)}) %copy-start.6) | copy-done | bytes 1572888
  53.6 0.7 copy-done.7
  54.3 29.8 %local_part.1 = (f32[48,128,512]{2,1,0:T(8,128)}, f32[48,8,512]{2,1,0:T(8,128)S(1)}, f32[48,8,512]{2,1,0:T(8,128)S(1)}) custom-call(s32[384]{0:T(512)S(1)} %reshape.57.slots_ref, s32[24]{0:T(128)S(1)} %reduce_max.28.counts_ref, bf16[24576,128]{1,0:T(8,128)(2,1)S(1)} %bitcast.14, bf16[2,3072,128]{2,1,0:T(8,128)(2,1)S(1)} %copy-done.4, ...), custom_call_target="tpu_custom_call" | custom-call | flops 9663676416 | bytes 33554432 | tf_op jit(solution)/shard_map/local_part/pallas_call | solution.py:444
  84.2 27.2 %remote_part.1 = bf16[24576,128]{1,0:T(8,128)(2,1)} custom-call(s32[384]{0:T(512)S(1)} %reshape.55.slots_ref, s32[24]{0:T(128)S(1)} %reduce_max.27.counts_ref, bf16[24576,128]{1,0:T(8,128)(2,1)S(1)} %bitcast.17, f32[48,128,512]{2,1,0:T(8,128)} %get-tuple-element.17.sums_ref, f32[48,8,512]{2,1,0:T(8,128)S(1)} %get-tuple-element.18.totals_ref, ...), custom_call_target="tpu_custom_call" | custom-call | tf_op jit(solution)/shard_map/remote_part/pallas_call | solution.py:470
  (38 shorter events, 0.8 us)
Async XLA Ops:
  0.8 13.6 %collective-permute-start.1 = (s32[2,24,8]{1,2,0:T(8,128)S(1)}, s32[2,24,8]{1,2,0:T(8,128)S(1)}, u32[]{:S(2)}, u32[]{:S(2)}) collective-permute-start(s32[2,24,8]{1,2,0:T(8,128)S(1)} %get-tuple-element.29), channel_id=1, source_target_pairs={{8,0},{12,4},{9,1},{13,5},{10,2},{14,6},{11,3},{15,7},{24,16},{28,... | collective-permute-start | bytes 4616 | tf_op jit(solution)/shard_map/ppermute | solution.py:393
  3.0 11.3 %collective-permute-start.2 = (s32[2,24,8]{1,2,0:T(8,128)S(1)}, s32[2,24,8]{1,2,0:T(8,128)S(1)}, u32[]{:S(2)}, u32[]{:S(2)}) collective-permute-start(s32[2,24,8]{1,2,0:T(8,128)S(1)} %get-tuple-element.29), channel_id=1, source_target_pairs={{12,0},{13,1},{14,2},{15,3},{28,16},{29,17},{30,18},{31,19}} | collective-permute-start | bytes 4616 | tf_op jit(solution)/shard_map/ppermute | solution.py:393
  3.7 10.7 %collective-permute-start = (s32[2,24,8]{1,2,0:T(8,128)S(1)}, s32[2,24,8]{1,2,0:T(8,128)S(1)}, u32[]{:S(2)}, u32[]{:S(2)}) collective-permute-start(s32[2,24,8]{1,2,0:T(8,128)S(1)} %get-tuple-element.29), channel_id=1, source_target_pairs={{4,0},{8,4},{12,8},{5,1},{9,5},{13,9},{6,2},{10,6},{14,10},{7,3},{... | collective-permute-start | bytes 4616 | tf_op jit(solution)/shard_map/ppermute | solution.py:393
  6.6 1.9 %copy-start.1 = (bf16[3072,4,128]{2,1,0:T(4,128)(2,1)S(1)}, bf16[3072,4,128]{2,1,0:T(4,128)(2,1)}, u32[]{:S(2)}) copy-start(bf16[3072,4,128]{2,1,0:T(4,128)(2,1)} %param.5) | copy-start | bytes 9437188
  8.5 1.9 %copy-start.2 = (bf16[3072,4,128]{2,1,0:T(4,128)(2,1)S(1)}, bf16[3072,4,128]{2,1,0:T(4,128)(2,1)}, u32[]{:S(2)}) copy-start(bf16[3072,4,128]{2,1,0:T(4,128)(2,1)} %param.6) | copy-start | bytes 9437188
  10.4 73.7 %slice-start = ((s8[6291456]{0:T(1024)(128)(4,1)}), s8[2097152]{0:T(1024)(128)(4,1)S(1)}, s32[]{:S(2)}) async-start(s8[6291456]{0:T(1024)(128)(4,1)} %bitcast.15), calls=%async_computation | async-start | bytes 4194304
  12.1 1.1 %copy-start.3 = (bf16[2,3072,128]{2,1,0:T(8,128)(2,1)}, bf16[2,3072,128]{2,1,0:T(8,128)(2,1)S(1)}, u32[]{:S(2)}) copy-start(bf16[2,3072,128]{2,1,0:T(8,128)(2,1)S(1)} %get-tuple-element.14.keys_ref) | copy-start | bytes 4718596
  13.2 1.2 %copy-start.5 = (bf16[2,3072,128]{2,1,0:T(8,128)(2,1)}, bf16[2,3072,128]{2,1,0:T(8,128)(2,1)S(1)}, u32[]{:S(2)}) copy-start(bf16[2,3072,128]{2,1,0:T(8,128)(2,1)S(1)} %get-tuple-element.15.values_ref) | copy-start | bytes 4718596
  42.1 42.0 %collective-permute-start.3 = (bf16[2,2,256,128]{3,2,1,0:T(8,128)(2,1)}, bf16[2,2,256,128]{3,2,1,0:T(8,128)(2,1)S(1)}, u32[]{:S(2)}, u32[]{:S(2)}) collective-permute-start(bf16[2,2,256,128]{3,2,1,0:T(8,128)(2,1)} %get-tuple-element.20), channel_id=1, source_target_pairs={{0,4},{4,8},{8,12},{1,5},{5,9},{9,13},{2,6},{6,10},{10,14},{3,7},{... | collective-permute-start | bytes 786440 | tf_op jit(solution)/shard_map/ppermute | solution.py:413
  46.0 38.1 %collective-permute-start.4 = (bf16[2,2,256,128]{3,2,1,0:T(8,128)(2,1)}, bf16[2,2,256,128]{3,2,1,0:T(8,128)(2,1)S(1)}, u32[]{:S(2)}, u32[]{:S(2)}) collective-permute-start(bf16[2,2,256,128]{3,2,1,0:T(8,128)(2,1)} %get-tuple-element.21), channel_id=1, source_target_pairs={{0,8},{4,12},{1,9},{5,13},{2,10},{6,14},{3,11},{7,15},{16,24},{20,... | collective-permute-start | bytes 786440 | tf_op jit(solution)/shard_map/ppermute | solution.py:413
  47.3 36.8 %collective-permute-start.5 = (bf16[2,2,256,128]{3,2,1,0:T(8,128)(2,1)}, bf16[2,2,256,128]{3,2,1,0:T(8,128)(2,1)S(1)}, u32[]{:S(2)}, u32[]{:S(2)}) collective-permute-start(bf16[2,2,256,128]{3,2,1,0:T(8,128)(2,1)} %get-tuple-element.22), channel_id=1, source_target_pairs={{0,12},{1,13},{2,14},{3,15},{16,28},{17,29},{18,30},{19,31}} | collective-permute-start | bytes 786440 | tf_op jit(solution)/shard_map/ppermute | solution.py:413
  48.0 2.8 %copy-start = (bf16[3072,8,128]{2,1,0:T(8,128)(2,1)S(1)}, bf16[3072,8,128]{2,1,0:T(8,128)(2,1)}, u32[]{:S(2)}) copy-start(bf16[3072,8,128]{2,1,0:T(8,128)(2,1)} %param.4) | copy-start | bytes 18874372
  50.8 1.4 %copy-start.4 = (bf16[2,3072,128]{2,1,0:T(8,128)(2,1)S(1)}, bf16[2,3072,128]{2,1,0:T(8,128)(2,1)}, u32[]{:S(2)}) copy-start(bf16[2,3072,128]{2,1,0:T(8,128)(2,1)} %copy-done.3) | copy-start | bytes 4718596
  52.2 1.4 %copy-start.6 = (bf16[2,3072,128]{2,1,0:T(8,128)(2,1)S(1)}, bf16[2,3072,128]{2,1,0:T(8,128)(2,1)}, u32[]{:S(2)}) copy-start(bf16[2,3072,128]{2,1,0:T(8,128)(2,1)} %copy-done.5) | copy-start | bytes 4718596
  53.6 0.7 copy-start.7
  54.3 29.8 %slice-start.1 = ((s8[6291456]{0:T(1024)(128)(4,1)}), s8[4194304]{0:T(1024)(128)(4,1)S(1)}, s32[]{:S(2)}) async-start(s8[6291456]{0:T(1024)(128)(4,1)} %bitcast.15), calls=%async_computation.1 | async-start | bytes 8388608

commit v2 on v1

--- a/solution.py
+++ b/solution.py
@@ -15,6 +15,7 @@
 MASKED = -1e30
 CLOSED = 3e38
 SAFE_TOTAL = 2.0**100
+VMEM_BYTES = 60 * 2**20
 
 
 def block_rows(index, block_len):
@@ -55,7 +56,7 @@
             scratch_shapes=[pltpu.VMEM((rows * kv_heads, head_dim), jnp.float32)] * 2,
         ),
         out_shape=[table, table],
-        compiler_params=pltpu.CompilerParams(vmem_limit_bytes=32 * 2**20),
+        compiler_params=pltpu.CompilerParams(vmem_limit_bytes=VMEM_BYTES),
         name="relayout",
     )(
         first,
@@ -64,46 +65,35 @@
     )
 
 
-def pack_kernel(request, keys_ref, values_ref, *rest, shifts, used, block_len):
-    outs, (clear_ref, sems) = rest[:shifts], rest[shifts:]
+def pack_kernel(request, keys_ref, values_ref, *outs, used, block_len):
+    *outs, clear_ref = outs
     clear_ref[...] = jnp.zeros_like(clear_ref)
-    copies = []
-    for shift in range(shifts):
+    for shift, out in enumerate(outs):
         for head in range(used):
             for turn in range(REMOTE_BLOCK_MAX):
                 at = (shift * used + head) * REMOTE_BLOCK_MAX + turn
                 source = block_rows(request[at], block_len)
-                target = pl.ds(turn * block_len, block_len)
-                for kind, table in enumerate((keys_ref, values_ref)):
-                    copies.append(
-                        pltpu.make_async_copy(
-                            table.at[head, source],
-                            outs[shift].at[kind, head, target],
-                            sems.at[2 * at + kind],
-                        )
-                    )
-    for copy in copies:
-        copy.start()
-    for copy in copies:
-        copy.wait()
+                target = slice(turn * block_len, (turn + 1) * block_len)
+                out[0, head, target, :] = keys_ref[head, source, :]
+                out[1, head, target, :] = values_ref[head, source, :]
 
 
 def pack(request, key_table, value_table, shifts, block_len, row_shape):
     used, _, head_dim = key_table.shape
-    anywhere = pl.BlockSpec(memory_space=pl.ANY)
-    parcel = jax.ShapeDtypeStruct(
-        (2, used, REMOTE_BLOCK_MAX * block_len, head_dim), jnp.bfloat16
-    )
+    parcel = (2, used, REMOTE_BLOCK_MAX * block_len, head_dim)
+    whole = pl.BlockSpec(key_table.shape, lambda g, *_: (0, 0, 0))
     return pl.pallas_call(
-        functools.partial(pack_kernel, shifts=shifts, used=used, block_len=block_len),
+        functools.partial(pack_kernel, used=used, block_len=block_len),
         grid_spec=pltpu.PrefetchScalarGridSpec(
             num_scalar_prefetch=1,
             grid=(1,),
-            in_specs=[anywhere, anywhere],
-            out_specs=[anywhere] * shifts + [pl.BlockSpec(row_shape, lambda g, *_: (0, 0))],
-            scratch_shapes=[pltpu.SemaphoreType.DMA((2 * shifts * used * REMOTE_BLOCK_MAX,))],
-        ),
-        out_shape=[parcel] * shifts + [jax.ShapeDtypeStruct(row_shape, jnp.float32)],
+            in_specs=[whole, whole],
+            out_specs=[pl.BlockSpec(parcel, lambda g, *_: (0, 0, 0, 0))] * shifts
+            + [pl.BlockSpec(row_shape, lambda g, *_: (0, 0))],
+        ),
+        out_shape=[jax.ShapeDtypeStruct(parcel, jnp.bfloat16)] * shifts
+        + [jax.ShapeDtypeStruct(row_shape, jnp.float32)],
+        compiler_params=pltpu.CompilerParams(vmem_limit_bytes=VMEM_BYTES),
         name="pack",
     )(request, key_table, value_table)
 
@@ -251,28 +241,16 @@
     slots_ref, counts_ref, queries_ref, sums_ref, totals_ref, highest_ref, *rest,
     shifts, step_blocks, used, picks, block_len, scale,
 ):
-    parcels, (out_ref, keys_ref, values_ref, bad_ref, sems) = rest[:shifts], rest[shifts:]
+    parcels, (out_ref, keys_ref, values_ref, bad_ref) = rest[:shifts], rest[shifts:]
     step = pl.program_id(0)
     parcel_rows = REMOTE_BLOCK_MAX * block_len
 
     @pl.when(step == 0)
     def _():
-        copies = []
-        for shift in range(shifts):
+        for shift, parcel in enumerate(parcels):
             place = pl.ds(shift * parcel_rows, parcel_rows)
-            for head in range(used):
-                for kind, table in enumerate((keys_ref, values_ref)):
-                    copies.append(
-                        pltpu.make_async_copy(
-                            parcels[shift].at[kind, head],
-                            table.at[head, place],
-                            sems.at[(shift * used + head) * 2 + kind],
-                        )
-                    )
-        for copy in copies:
-            copy.start()
-        for copy in copies:
-            copy.wait()
+            keys_ref[:, place, :] = parcel[0]
+            values_ref[:, place, :] = parcel[1]
 
     def gather(ref, head, slots, axis):
         return jnp.concatenate(
@@ -454,7 +432,7 @@
             scratch_shapes=[pltpu.VMEM((8, item_rows), jnp.float32)],
         ),
         out_shape=[sums_shape, row_shape, row_shape],
-        compiler_params=pltpu.CompilerParams(vmem_limit_bytes=40 * 2**20),
+        compiler_params=pltpu.CompilerParams(vmem_limit_bytes=VMEM_BYTES),
         cost_estimate=pl.CostEstimate(
             flops=3 * tokens * query_heads * picks * block_len * head_dim,
             bytes_accessed=32 * 2**20,
@@ -473,17 +451,16 @@
             num_scalar_prefetch=2,
             grid=(steps,),
             in_specs=[query_spec, sums_spec, row_spec, row_spec]
-            + [pl.BlockSpec(memory_space=pl.ANY)] * shifts,
+            + [pl.BlockSpec(arrived[0].shape, lambda g, *_: (0, 0, 0, 0))] * shifts,
             out_specs=query_spec,
             scratch_shapes=[
                 pltpu.VMEM((used, remote_rows, head_dim), jnp.bfloat16),
                 pltpu.VMEM((used, remote_rows, head_dim), jnp.bfloat16),
                 pltpu.VMEM((8, item_rows), jnp.float32),
-                pltpu.SemaphoreType.DMA((2 * used * shifts,)),
             ],
         ),
         out_shape=jax.ShapeDtypeStruct(query_rows.shape, jnp.bfloat16),
-        compiler_params=pltpu.CompilerParams(vmem_limit_bytes=40 * 2**20),
+        compiler_params=pltpu.CompilerParams(vmem_limit_bytes=VMEM_BYTES),
         name="remote_part",
     )(
         table(remote_slots), jnp.max(remote_count, axis=0), query_rows,

time: 112 us -> 86.7 us (0.77)
  Pallas kernels: 85.1 us -> 69.4 us
  local copies, waits for them, and re-layouts: 13.7 us -> 3.3 us
  other arithmetic: 1.66 us -> 2.82 us
    pallas_call x1, Pallas kernels: 26.4 us -> 3.51 us  [pack(): pl.pallas_call(functools.partial(pack_kernel, used=used, block_len=block_...]
    unnamed x20 -> x6, local copies, waits for them, and re-layouts: 12.4 us -> 0.88 us
    pallas_call x1, Pallas kernels: 1.66 us -> 5.51 us  [relayout(): pl.pallas_call(functools.partial(relayout_kernel, step_blocks=step_blocks...]
    pallas_call x1, Pallas kernels: 29.8 us -> 32 us  [on_device(): pl.pallas_call(functools.partial(local_kernel, **sizes), grid_spec=pltpu....]
    pallas_call x1, Pallas kernels: 27.2 us -> 28.4 us  [on_device(): pl.pallas_call(functools.partial(remote_kernel, shifts=shifts, **sizes),...]
    reshape x2, local copies, waits for them, and re-layouts: 0.21 us -> 1.34 us  [table(): return jnp.transpose(slots, (1, 0, 2)).reshape(-1)]
  transfers between devices with their start and end apart: 6 -> 6, of which waited for: 0 -> 0; matrix products, arithmetic and copies ran while one was open for 1% -> 4% of each run, Pallas kernels for 28% -> 43%
where the time goes in v2:
time: 86.7 us; the launch traced here: 86.4 us
  Pallas kernels  69.4 us (80%)
  starting transfers between devices  10.7 us (12%)
  local copies, waits for them, and re-layouts  3.3 us (4%)
  other arithmetic  2.82 us (3%)
    pallas_call x1, Pallas kernels, on_device(): pl.pallas_call(functools.partial(local_kernel, **sizes), grid_spec=pltpu....  32 us
    pallas_call x1, Pallas kernels, on_device(): pl.pallas_call(functools.partial(remote_kernel, shifts=shifts, **sizes),...  28.4 us
    ppermute x3, starting transfers between devices, on_device(): lax.ppermute(parcel, 'ctx', [(i, i + d) for i in range(shards - d)])  5.88 us
    pallas_call x1, Pallas kernels, relayout(): pl.pallas_call(functools.partial(relayout_kernel, step_blocks=step_blocks...  5.51 us
    ppermute x3, starting transfers between devices, on_device(): lax.ppermute(lists, 'ctx', [(j, j - d) for j in range(d, shards)])  4.81 us
    pallas_call x1, Pallas kernels, pack(): pl.pallas_call(functools.partial(pack_kernel, used=used, block_len=block_...  3.51 us
  transfers between devices with their start and end apart: 6, of which 0 were waited for; matrix products, arithmetic and copies ran while one was open for 4% of the time, Pallas kernels for 43%

profile of v2, /device:TPU:18, one launch (start us, length us, event | category | flops | bytes accessed | tf_op | source)
XLA Modules:
  0.0 86.4 jit_solution(7999829912942027112)
XLA Ops:
  0.0 0.8 convert_reduce_fusion.2
  0.8 2.2 %collective-permute-start.1 = (s32[2,24,8]{1,2,0:T(8,128)S(1)}, s32[2,24,8]{1,2,0:T(8,128)S(1)}, u32[]{:S(2)}, u32[]{:S(2)}) collective-permute-start(s32[2,24,8]{1,2,0:T(8,128)S(1)} %get-tuple-element.29), channel_id=1, source_target_pairs={{8,0},{12,4},{9,1},{13,5},{10,2},{14,6},{11,3},{15,7},{24,16},{28,... | collective-permute-start | bytes 4616 | tf_op jit(solution)/shard_map/ppermute | solution.py:371
  3.0 0.7 collective-permute-start.2
  3.7 1.9 %collective-permute-start = (s32[2,24,8]{1,2,0:T(8,128)S(1)}, s32[2,24,8]{1,2,0:T(8,128)S(1)}, u32[]{:S(2)}, u32[]{:S(2)}) collective-permute-start(s32[2,24,8]{1,2,0:T(8,128)S(1)} %get-tuple-element.29), channel_id=1, source_target_pairs={{4,0},{8,4},{12,8},{5,1},{9,5},{13,9},{6,2},{10,6},{14,10},{7,3},{... | collective-permute-start | bytes 4616 | tf_op jit(solution)/shard_map/ppermute | solution.py:371
  5.7 0.2 select_reduce_fusion.2
  6.2 0.6 reduce_max.28.counts_ref
  6.8 0.6 reduce_max.27.counts_ref
  7.5 0.6 reshape.55.slots_ref
  8.2 0.7 reshape.57.slots_ref
  8.9 5.5 %relayout.1 = (bf16[2,3072,128]{2,1,0:T(8,128)(2,1)}, bf16[2,3072,128]{2,1,0:T(8,128)(2,1)}) custom-call(s32[1]{0:T(128)} %bitcast.3.first_ref, bf16[12288,128]{1,0:T(8,128)(2,1)} %bitcast.16, bf16[12288,128]{1,0:T(8,128)(2,1)} %bitcast.17), custom_call_target="tpu_custom_call" | custom-call | tf_op jit(solution)/shard_map/relayout/pallas_call | solution.py:46
  14.4 0.3 select_reduce_fusion.4
  14.8 0.1 copy.34
  14.8 0.1 copy.35
  14.9 0.1 copy.36
  15.0 0.6 reshape.61.request
  15.7 3.5 %pack.1 = (bf16[2,2,256,128]{3,2,1,0:T(8,128)(2,1)}, bf16[2,2,256,128]{3,2,1,0:T(8,128)(2,1)}, bf16[2,2,256,128]{3,2,1,0:T(8,128)(2,1)}, f32[8,512]{1,0:T(8,128)}) custom-call(s32[12]{0:T(128)} %reshape.61.request, bf16[2,3072,128]{2,1,0:T(8,128)(2,1)} %get-tuple-element.14.keys_ref, bf16[2,3072,128]{2,1,0:T(8,128)(2,1)} %get-tuple-element.15.values_ref), custom_call_target="tpu_custom_call" | custom-call | tf_op jit(solution)/shard_map/pack/pallas_call | solution.py:85
  19.2 3.9 %collective-permute-start.3 = (bf16[2,2,256,128]{3,2,1,0:T(8,128)(2,1)}, bf16[2,2,256,128]{3,2,1,0:T(8,128)(2,1)S(1)}, u32[]{:S(2)}, u32[]{:S(2)}) collective-permute-start(bf16[2,2,256,128]{3,2,1,0:T(8,128)(2,1)} %get-tuple-element.20), channel_id=1, source_target_pairs={{0,4},{4,8},{8,12},{1,5},{5,9},{9,13},{2,6},{6,10},{10,14},{3,7},{... | collective-permute-start | bytes 786440 | tf_op jit(solution)/shard_map/ppermute | solution.py:391
  23.1 1.3 %collective-permute-start.4 = (bf16[2,2,256,128]{3,2,1,0:T(8,128)(2,1)}, bf16[2,2,256,128]{3,2,1,0:T(8,128)(2,1)S(1)}, u32[]{:S(2)}, u32[]{:S(2)}) collective-permute-start(bf16[2,2,256,128]{3,2,1,0:T(8,128)(2,1)} %get-tuple-element.21), channel_id=1, source_target_pairs={{0,8},{4,12},{1,9},{5,13},{2,10},{6,14},{3,11},{7,15},{16,24},{20,... | collective-permute-start | bytes 786440 | tf_op jit(solution)/shard_map/ppermute | solution.py:391
  24.4 0.7 collective-permute-start.5
  25.1 32.0 %local_part.1 = (f32[48,128,512]{2,1,0:T(8,128)}, f32[48,8,512]{2,1,0:T(8,128)}, f32[48,8,512]{2,1,0:T(8,128)}) custom-call(s32[384]{0:T(512)} %reshape.57.slots_ref, s32[24]{0:T(128)} %reduce_max.28.counts_ref, bf16[24576,128]{1,0:T(8,128)(2,1)} %bitcast.14, bf16[2,3072,128]{2,1,0:T(8,128)(2,1)} %get-tuple-element.14.keys_ref, ...), custom_call_target="tpu_custom_call" | custom-call | flops 9663676416 | bytes 33554432 | tf_op jit(solution)/shard_map/local_part/pallas_call | solution.py:422
  57.1 0.7 copy-done
  57.8 0.1 copy-done.1
  57.9 0.1 copy-done.2
  58.0 28.4 %remote_part.1 = bf16[24576,128]{1,0:T(8,128)(2,1)} custom-call(s32[384]{0:T(512)} %reshape.55.slots_ref, s32[24]{0:T(128)} %reduce_max.27.counts_ref, bf16[24576,128]{1,0:T(8,128)(2,1)} %bitcast.15, f32[48,128,512]{2,1,0:T(8,128)} %get-tuple-element.17.sums_ref, f32[48,8,512]{2,1,0:T(8,128)} %get-tuple-element.18.totals_ref, ...), custom_call_target="tpu_custom_call" | custom-call | tf_op jit(solution)/shard_map/remote_part/pallas_call | solution.py:448
  (23 shorter events, 0.5 us)
Async XLA Ops:
  0.8 13.6 %collective-permute-start.1 = (s32[2,24,8]{1,2,0:T(8,128)S(1)}, s32[2,24,8]{1,2,0:T(8,128)S(1)}, u32[]{:S(2)}, u32[]{:S(2)}) collective-permute-start(s32[2,24,8]{1,2,0:T(8,128)S(1)} %get-tuple-element.29), channel_id=1, source_target_pairs={{8,0},{12,4},{9,1},{13,5},{10,2},{14,6},{11,3},{15,7},{24,16},{28,... | collective-permute-start | bytes 4616 | tf_op jit(solution)/shard_map/ppermute | solution.py:371
  3.0 11.4 %collective-permute-start.2 = (s32[2,24,8]{1,2,0:T(8,128)S(1)}, s32[2,24,8]{1,2,0:T(8,128)S(1)}, u32[]{:S(2)}, u32[]{:S(2)}) collective-permute-start(s32[2,24,8]{1,2,0:T(8,128)S(1)} %get-tuple-element.29), channel_id=1, source_target_pairs={{12,0},{13,1},{14,2},{15,3},{28,16},{29,17},{30,18},{31,19}} | collective-permute-start | bytes 4616 | tf_op jit(solution)/shard_map/ppermute | solution.py:371
  3.7 10.7 %collective-permute-start = (s32[2,24,8]{1,2,0:T(8,128)S(1)}, s32[2,24,8]{1,2,0:T(8,128)S(1)}, u32[]{:S(2)}, u32[]{:S(2)}) collective-permute-start(s32[2,24,8]{1,2,0:T(8,128)S(1)} %get-tuple-element.29), channel_id=1, source_target_pairs={{4,0},{8,4},{12,8},{5,1},{9,5},{13,9},{6,2},{10,6},{14,10},{7,3},{... | collective-permute-start | bytes 4616 | tf_op jit(solution)/shard_map/ppermute | solution.py:371
  19.2 37.9 %collective-permute-start.3 = (bf16[2,2,256,128]{3,2,1,0:T(8,128)(2,1)}, bf16[2,2,256,128]{3,2,1,0:T(8,128)(2,1)S(1)}, u32[]{:S(2)}, u32[]{:S(2)}) collective-permute-start(bf16[2,2,256,128]{3,2,1,0:T(8,128)(2,1)} %get-tuple-element.20), channel_id=1, source_target_pairs={{0,4},{4,8},{8,12},{1,5},{5,9},{9,13},{2,6},{6,10},{10,14},{3,7},{... | collective-permute-start | bytes 786440 | tf_op jit(solution)/shard_map/ppermute | solution.py:391
  23.1 34.0 %collective-permute-start.4 = (bf16[2,2,256,128]{3,2,1,0:T(8,128)(2,1)}, bf16[2,2,256,128]{3,2,1,0:T(8,128)(2,1)S(1)}, u32[]{:S(2)}, u32[]{:S(2)}) collective-permute-start(bf16[2,2,256,128]{3,2,1,0:T(8,128)(2,1)} %get-tuple-element.21), channel_id=1, source_target_pairs={{0,8},{4,12},{1,9},{5,13},{2,10},{6,14},{3,11},{7,15},{16,24},{20,... | collective-permute-start | bytes 786440 | tf_op jit(solution)/shard_map/ppermute | solution.py:391
  24.4 32.7 %collective-permute-start.5 = (bf16[2,2,256,128]{3,2,1,0:T(8,128)(2,1)}, bf16[2,2,256,128]{3,2,1,0:T(8,128)(2,1)S(1)}, u32[]{:S(2)}, u32[]{:S(2)}) collective-permute-start(bf16[2,2,256,128]{3,2,1,0:T(8,128)(2,1)} %get-tuple-element.22), channel_id=1, source_target_pairs={{0,12},{1,13},{2,14},{3,15},{16,28},{17,29},{18,30},{19,31}} | collective-permute-start | bytes 786440 | tf_op jit(solution)/shard_map/ppermute | solution.py:391
  57.1 0.7 copy-start
  57.1 0.8 copy-start.1
  57.1 0.9 %copy-start.2 = (bf16[2,2,256,128]{3,2,1,0:T(8,128)(2,1)}, bf16[2,2,256,128]{3,2,1,0:T(8,128)(2,1)S(1)}, u32[]{:S(2)}) copy-start(bf16[2,2,256,128]{3,2,1,0:T(8,128)(2,1)S(1)} %collective-permute-done.5.rest_2_) | copy-start | bytes 786436

commit v3 on v2

v3 whole, which is shorter than its diff:
```python
import functools

import jax
import jax.numpy as jnp
from jax import lax
from jax.experimental import pallas as pl
from jax.experimental.pallas import tpu as pltpu
from jax.sharding import PartitionSpec as P

QUERY_HEADS = 32
KEY_VALUE_HEADS = 8
REMOTE_BLOCK_MAX = 2
GROUP = QUERY_HEADS // KEY_VALUE_HEADS
LOG2E = 1.4426950408889634
MASKED = -1e30
CLOSED = 3e38
SAFE_TOTAL = 2.0**100
VMEM_BYTES = 60 * 2**20
UNITS_AT_ONCE = 8
FIELD = 10


def block_rows(index, block_len):
    return pl.ds(pl.multiple_of(index * block_len, block_len), block_len)


def pack_kernel(
    request, keys_ref, values_ref, *rest, shifts, used, kv_heads, block_len
):
    first_ref, outs = rest[0], rest[1 : shifts + 1]
    clear_ref, blocks_ref, wide_ref, sems = rest[shifts + 1 :]
    rows = block_len * kv_heads
    clear_ref[...] = jnp.zeros_like(clear_ref)
    wanted = [
        (shift, head, turn)
        for shift in range(shifts)
        for head in range(used)
        for turn in range(REMOTE_BLOCK_MAX)
    ]
    copies = []
    for at in range(len(wanted)):
        for kind, table in enumerate((keys_ref, values_ref)):
            copies.append(
                pltpu.make_async_copy(
                    table.at[block_rows(request[at], rows)],
                    blocks_ref.at[2 * at + kind],
                    sems.at[2 * at + kind],
                )
            )
    for copy in copies:
        copy.start()
    for at, (shift, head, turn) in enumerate(wanted):
        target = slice(turn * block_len, (turn + 1) * block_len)
        picked = pl.ds(first_ref[0] + head, block_len, stride=kv_heads)
        for kind in range(2):
            place = 2 * at + kind
            copies[place].wait()
            wide_ref[place] = blocks_ref[place].astype(jnp.float32)
            block = wide_ref[place, picked, :]
            outs[shift][kind, head, target, :] = (block.T if kind else block).astype(jnp.bfloat16)


def pack(request, first, keys, values, kv_heads, shifts, used, block_len, row_shape):
    head_dim = keys.shape[-1]
    parcel = (2, used, REMOTE_BLOCK_MAX * block_len, head_dim)
    anywhere = pl.BlockSpec(memory_space=pl.ANY)
    count = 2 * shifts * used * REMOTE_BLOCK_MAX
    rows = block_len * kv_heads
    return pl.pallas_call(
        functools.partial(
            pack_kernel, shifts=shifts, used=used, kv_heads=kv_heads, block_len=block_len
        ),
        grid_spec=pltpu.PrefetchScalarGridSpec(
            num_scalar_prefetch=1,
            grid=(1,),
            in_specs=[anywhere, anywhere, pl.BlockSpec(memory_space=pltpu.SMEM)],
            out_specs=[pl.BlockSpec(parcel, lambda g, *_: (0, 0, 0, 0))] * shifts
            + [pl.BlockSpec(row_shape, lambda g, *_: (0, 0))],
            scratch_shapes=[
                pltpu.VMEM((count, rows, head_dim), jnp.bfloat16),
                pltpu.VMEM((count, rows, head_dim), jnp.float32),
                pltpu.SemaphoreType.DMA((count,)),
            ],
        ),
        out_shape=[jax.ShapeDtypeStruct(parcel, jnp.bfloat16)] * shifts
        + [jax.ShapeDtypeStruct(row_shape, jnp.float32)],
        compiler_params=pltpu.CompilerParams(vmem_limit_bytes=VMEM_BYTES),
        name="pack",
    )(request, keys, values, first)


def split_heads(rows, used):
    count, head_dim = rows.shape
    if used == 1:
        return (rows,)
    wide = rows.astype(jnp.float32).reshape(count // 16, 2, 8, head_dim)
    even, odd = wide[:, 0], wide[:, 1]
    upper = lax.broadcasted_iota(jnp.int32, even.shape, 1) < GROUP
    first = jnp.where(upper, even, pltpu.roll(odd, GROUP, 1))
    second = jnp.where(upper, pltpu.roll(even, GROUP, 1), odd)
    return tuple(x.reshape(count // 2, head_dim).astype(jnp.bfloat16) for x in (first, second))


def join_heads(first, *others):
    count, head_dim = first.shape
    if not others:
        return first.astype(jnp.bfloat16)
    (second,) = others
    first = first.reshape(count // 8, 8, head_dim)
    second = second.reshape(count // 8, 8, head_dim)
    upper = lax.broadcasted_iota(jnp.int32, first.shape, 1) < GROUP
    even = jnp.where(upper, first, pltpu.roll(second, GROUP, 1))
    odd = jnp.where(upper, pltpu.roll(first, GROUP, 1), second)
    return jnp.stack([even, odd], axis=1).reshape(count * 2, head_dim).astype(jnp.bfloat16)


def score(key_rows, query):
    return lax.dot_general(
        key_rows, query, (((1,), (1,)), ((), ())), preferred_element_type=jnp.float32
    )


def causal(scores):
    key = lax.broadcasted_iota(jnp.int32, scores.shape, 0)
    per_head = scores.shape[1] // scores.shape[0]
    token = lax.broadcasted_iota(jnp.int32, scores.shape, 1) // per_head
    return jnp.where(key <= token, scores, MASKED)


def fold(weights):
    return jnp.sum(weights.reshape(weights.shape[0] // 8, 8, weights.shape[1]), axis=0)


def attend_units(
    units_ref, base, queries_ref, keys_ref, values_ref, highest_ref, sums_ref, totals_ref,
    *, used, block_len, scale, units_max,
):
    def read(unit):
        code = units_ref[base + unit]
        mask = (1 << FIELD) - 1
        return code >> (2 * FIELD), ((code >> FIELD) & mask) - 1, (code & mask) - 1

    def block(ref, item, slot):
        head = lax.rem(item, used)
        return ref[head, block_rows(jnp.maximum(slot, 0), block_len), :]

    def scores_of(unit):
        item, *slots = unit
        rows = jnp.concatenate([block(keys_ref, item, slot) for slot in slots], axis=0)
        return score(rows, queries_ref[item])

    def weigh(unit, scores, highest):
        item, *slots = unit
        parts = []
        for turn, slot in enumerate(slots):
            shift = jnp.where(slot < 0, CLOSED, highest)
            part = scores[turn * block_len : (turn + 1) * block_len]
            parts.append(jnp.exp2(part * scale - shift))
        weights = jnp.concatenate(parts, axis=0)
        columns = jnp.concatenate([block(values_ref, item, slot) for slot in slots], axis=1)
        summed = jnp.dot(
            columns, weights.astype(jnp.bfloat16), preferred_element_type=jnp.float32
        )
        return fold(weights), summed

    count = units_ref[base + units_max]

    def some(turn, carry):
        units = [read(turn * UNITS_AT_ONCE + n) for n in range(UNITS_AT_ONCE)]
        scores = [scores_of(unit) for unit in units]
        shares = [weigh(u, s, highest_ref[u[0], :1, :]) for u, s in zip(units, scores)]
        for unit, (total, summed) in zip(units, shares):
            totals_ref[unit[0]] += total
            sums_ref[unit[0]] += summed
        return carry

    lax.fori_loop(0, (count + UNITS_AT_ONCE - 1) // UNITS_AT_ONCE, some, 0)

    def only(unit, item):
        its, first, second = read(unit)
        return item, jnp.where(its == item, first, -1), jnp.where(its == item, second, -1)

    def raise_highest(item, highest):
        def look(turn, highest):
            unit = only(turn, item)
            scores = scores_of(unit)
            for place, slot in enumerate(unit[1:]):
                part = scores[place * block_len : (place + 1) * block_len]
                found = jnp.max(part, axis=0, keepdims=True) * scale
                highest = jnp.where(slot < 0, highest, jnp.maximum(highest, found))
            return highest

        return lax.fori_loop(0, count, look, highest)

    def add_again(item, highest, sums, totals):
        def add(turn, carry):
            unit = only(turn, item)
            total, summed = weigh(unit, scores_of(unit), highest)
            return carry[0] + summed, carry[1] + total

        return lax.fori_loop(0, count, add, (sums, totals))

    return raise_highest, add_again


def unsafe(totals):
    return jnp.max(jnp.where(totals < SAFE_TOTAL, 0.0, 1.0)) > 0.0


def local_kernel(
    units_ref, first_ref, queries_ref, keys_ref, values_ref, clear_ref,
    sums_ref, totals_ref, highest_ref, split_ref,
    key_table, value_table, keys_wide, values_wide,
    *, blocks, step_blocks, used, kv_heads, block_len, scale, units_max, at_once,
):
    step = pl.program_id(0)
    rows = block_len * kv_heads

    @pl.when(step == 0)
    def _():
        def take_apart(turn, carry):
            for n in range(at_once):
                block = turn * at_once + n
                source = block_rows(block, rows)
                keys_wide[n] = keys_ref[source, :].astype(jnp.float32)
                values_wide[n] = values_ref[source, :].astype(jnp.float32)
                for head in range(used):
                    picked = pl.ds(first_ref[0] + head, block_len, stride=kv_heads)
                    target = block_rows(block, block_len)
                    key_table[head, target, :] = keys_wide[n, picked, :].astype(jnp.bfloat16)
                    value_table[head, target, :] = values_wide[n, picked, :].T.astype(
                        jnp.bfloat16
                    )
            return carry

        lax.fori_loop(0, blocks // at_once, take_apart, 0)

    query_rows = queries_ref.shape[0] // step_blocks

    def own_part(item, block, highest=None):
        head = lax.rem(item, used)
        here = block_rows(step * step_blocks + block, block_len)
        scores = causal(score(key_table[head, here, :], split_ref[item]))
        if highest is None:
            highest = jnp.max(scores, axis=0, keepdims=True) * scale
        weights = jnp.exp2(scores * scale - highest)
        summed = jnp.dot(
            value_table[head, here, :], weights.astype(jnp.bfloat16),
            preferred_element_type=jnp.float32,
        )
        return highest, fold(weights), summed

    def own_blocks(turn, carry):
        todo = []
        for n in range(at_once):
            block = turn * at_once + n
            raw = queries_ref[pl.ds(pl.multiple_of(block * query_rows, query_rows), query_rows), :]
            for head, query in enumerate(split_heads(raw, used)):
                split_ref[block * used + head] = query
                todo.append((block * used + head, block))
        for item, (highest, total, summed) in [(item, own_part(item, b)) for item, b in todo]:
            highest_ref[item] = jnp.broadcast_to(highest, total.shape) + clear_ref[...]
            totals_ref[item] = total
            sums_ref[item] = summed
        return carry

    lax.fori_loop(0, step_blocks // at_once, own_blocks, 0)
    raise_highest, add_again = attend_units(
        units_ref, step * (units_max + 1), split_ref, key_table, value_table, highest_ref,
        sums_ref, totals_ref, used=used, block_len=block_len, scale=scale, units_max=units_max,
    )

    @pl.when(unsafe(totals_ref[...]))
    def _():
        def mend(item, carry):
            highest = raise_highest(item, highest_ref[item][:1])
            _, total, summed = own_part(item, item // used, highest)
            sums, totals = add_again(item, highest, summed, total)
            highest_ref[item] = jnp.broadcast_to(highest, totals.shape)
            totals_ref[item] = totals
            sums_ref[item] = sums
            return carry

        lax.fori_loop(0, step_blocks * used, mend, 0)


def remote_kernel(
    units_ref, split_ref, sums_in, totals_in, highest_ref, *rest,
    shifts, step_blocks, used, block_len, scale, units_max, at_once,
):
    parcels, (out_ref, key_table, value_table, sums_ref, totals_ref) = (
        rest[:shifts], rest[shifts:]
    )
    step = pl.program_id(0)
    parcel_rows = REMOTE_BLOCK_MAX * block_len

    @pl.when(step == 0)
    def _():
        for shift, parcel in enumerate(parcels):
            place = pl.ds(shift * parcel_rows, parcel_rows)
            key_table[:, place, :] = parcel[0]
            value_table[:, place, :] = parcel[1]

    sums_ref[...] = sums_in[...]
    totals_ref[...] = totals_in[...]
    raise_highest, add_again = attend_units(
        units_ref, step * (units_max + 1), split_ref, key_table, value_table, highest_ref,
        sums_ref, totals_ref, used=used, block_len=block_len, scale=scale, units_max=units_max,
    )

    @pl.when(unsafe(totals_ref[...] * 0.5))
    def _():
        def mend(item, carry):
            before = highest_ref[item][:1]
            highest = raise_highest(item, before)
            shrink = jnp.exp2(before - highest)
            sums, totals = add_again(
                item, highest, sums_in[item] * shrink, totals_in[item] * shrink
            )
            totals_ref[item] = totals
            sums_ref[item] = sums
            return carry

        lax.fori_loop(0, step_blocks * used, mend, 0)

    query_rows = out_ref.shape[0] // step_blocks

    def finish(turn, carry):
        for n in range(at_once):
            block = turn * at_once + n
            parts = []
            for head in range(used):
                item = block * used + head
                total = jnp.sum(totals_ref[item], axis=0, keepdims=True)
                parts.append((sums_ref[item] * (1.0 / total)).T)
            place = pl.ds(pl.multiple_of(block * query_rows, query_rows), query_rows)
            out_ref[place, :] = join_heads(*parts)
        return carry

    lax.fori_loop(0, step_blocks // at_once, finish, 0)


def list_units(open_slot, index, steps, units_max):
    used, blocks, picks = index.shape
    ahead = jnp.arange(picks)[:, None] < jnp.arange(picks)[None, :]
    place = jnp.sum(open_slot[..., :, None] & ahead, axis=-2)
    here = open_slot[..., :, None] & (place[..., :, None] == jnp.arange(picks))
    packed = jnp.sum(jnp.where(here, index[..., :, None] + 1, 0), axis=-2)
    pairs = jnp.transpose(packed, (1, 0, 2)).reshape(steps, -1, picks // 2, 2)
    item = jnp.arange(pairs.shape[1], dtype=jnp.int32)[None, :, None]
    codes = (item << (2 * FIELD)) + (pairs[..., 0] << FIELD) + pairs[..., 1]
    filled = (pairs[..., 0] > 0).reshape(steps, -1)
    codes = codes.reshape(steps, -1)
    ahead = jnp.arange(codes.shape[1])[:, None] < jnp.arange(codes.shape[1])[None, :]
    place = jnp.sum(filled[:, :, None] & ahead, axis=1)
    here = filled[:, :, None] & (place[:, :, None] == jnp.arange(units_max))
    listed = jnp.sum(jnp.where(here, codes[:, :, None], 0), axis=1)
    count = jnp.sum(filled, axis=1, keepdims=True, dtype=jnp.int32)
    return jnp.concatenate([listed, count], axis=1).reshape(-1).astype(jnp.int32)


def on_device(queries, keys, values, chosen):
    tokens, query_heads, head_dim = queries.shape
    kv_heads = keys.shape[1]
    blocks, picks = chosen.shape[1:]
    block_len = tokens // blocks
    used = max(1, query_heads // GROUP)
    per_head = query_heads // used
    shards = lax.axis_size("ctx")
    shifts = shards - 1
    position = lax.axis_index("ctx")
    base = position * blocks
    first = lax.axis_index("rep") * query_heads // GROUP
    scale = LOG2E * head_dim**-0.5
    step_blocks = next(n for n in (6, 4, 3, 2, 1) if blocks % n == 0)
    at_once = next(n for n in (3, 2, 1) if step_blocks % n == 0)
    steps = blocks // step_blocks
    item_rows = per_head * block_len
    units_max = step_blocks * used * (picks // 2)
    units_max = -(-units_max // UNITS_AT_ONCE) * UNITS_AT_ONCE

    lists = lax.dynamic_slice_in_dim(chosen, first, used, 0)
    wanted = jnp.stack(
        [
            lax.ppermute(lists, "ctx", [(j, j - d) for j in range(d, shards)])
            for d in range(1, shards)
        ]
    )
    within = wanted - base
    mine = (within >= 0) & (within < blocks)
    request = jnp.stack(
        [
            jnp.min(jnp.where(mine, within, blocks - 1), axis=(2, 3)),
            jnp.max(jnp.where(mine, within, 0), axis=(2, 3)),
        ],
        axis=-1,
    )
    first = first.reshape(1)
    query_rows = queries.reshape(tokens * query_heads, head_dim)
    key_rows = keys.reshape(tokens * kv_heads, head_dim)
    value_rows = values.reshape(tokens * kv_heads, head_dim)
    *parcels, clear = pack(
        request.reshape(-1), first, key_rows, value_rows, kv_heads, shifts, used, block_len,
        (8, item_rows),
    )
    arrived = [
        lax.ppermute(parcel, "ctx", [(i, i + d) for i in range(shards - d)])
        for d, parcel in zip(range(1, shards), parcels)
    ]

    local = lists >= base
    own = base + jnp.arange(blocks)
    local_units = list_units(local & (lists != own[None, :, None]), lists - base, steps, units_max)
    shard_of = lists // blocks
    from_shard = shard_of[..., None] == jnp.arange(shards)
    lowest = jnp.min(
        jnp.where(from_shard, lists[..., None], shards * blocks), axis=(1, 2), keepdims=True
    )
    is_lowest = jnp.any(from_shard & (lists[..., None] == lowest), axis=-1)
    remote_index = (position - 1 - shard_of) * REMOTE_BLOCK_MAX + jnp.where(is_lowest, 0, 1)
    remote_units = list_units(~local, remote_index, steps, units_max)

    def stepped(*shape):
        return pl.BlockSpec(shape, lambda g, *_: (g,) + (0,) * (len(shape) - 1))

    def whole(shape):
        return pl.BlockSpec(shape, lambda g, *_: (0,) * len(shape))

    items = step_blocks * used
    query_spec = stepped(step_blocks * block_len * query_heads, head_dim)
    sums_spec = stepped(items, head_dim, item_rows)
    row_spec = stepped(items, 8, item_rows)
    split_spec = stepped(items, item_rows, head_dim)
    sums_shape = jax.ShapeDtypeStruct((blocks * used, head_dim, item_rows), jnp.float32)
    row_shape = jax.ShapeDtypeStruct((blocks * used, 8, item_rows), jnp.float32)
    split_shape = jax.ShapeDtypeStruct((blocks * used, item_rows, head_dim), jnp.bfloat16)
    sizes = dict(
        step_blocks=step_blocks, used=used, block_len=block_len, scale=scale,
        units_max=units_max, at_once=at_once,
    )
    wide = pltpu.VMEM((at_once, block_len * kv_heads, head_dim), jnp.float32)
    table = pltpu.VMEM((used, tokens, head_dim), jnp.bfloat16)
    sums, totals, highest, split = pl.pallas_call(
        functools.partial(local_kernel, blocks=blocks, kv_heads=kv_heads, **sizes),
        grid_spec=pltpu.PrefetchScalarGridSpec(
            num_scalar_prefetch=2,
            grid=(steps,),
            in_specs=[
                query_spec, whole(key_rows.shape), whole(value_rows.shape), whole(clear.shape)
            ],
            out_specs=[sums_spec, row_spec, row_spec, split_spec],
            scratch_shapes=[table, table, wide, wide],
        ),
        out_shape=[sums_shape, row_shape, row_shape, split_shape],
        compiler_params=pltpu.CompilerParams(vmem_limit_bytes=VMEM_BYTES),
        cost_estimate=pl.CostEstimate(
            flops=3 * tokens * query_heads * picks * block_len * head_dim,
            bytes_accessed=32 * 2**20,
            transcendentals=tokens * query_heads * picks * block_len,
        ),
        name="local_part",
    )(local_units, first, query_rows, key_rows, value_rows, clear)

    table = pltpu.VMEM((used, shifts * REMOTE_BLOCK_MAX * block_len, head_dim), jnp.bfloat16)
    out = pl.pallas_call(
        functools.partial(remote_kernel, shifts=shifts, **sizes),
        grid_spec=pltpu.PrefetchScalarGridSpec(
            num_scalar_prefetch=1,
            grid=(steps,),
            in_specs=[split_spec, sums_spec, row_spec, row_spec]
            + [whole(arrived[0].shape)] * shifts,
            out_specs=query_spec,
            scratch_shapes=[
                table,
                table,
                pltpu.VMEM((items, head_dim, item_rows), jnp.float32),
                pltpu.VMEM((items, 8, item_rows), jnp.float32),
            ],
        ),
        out_shape=jax.ShapeDtypeStruct(query_rows.shape, jnp.bfloat16),
        compiler_params=pltpu.CompilerParams(vmem_limit_bytes=VMEM_BYTES),
        name="remote_part",
    )(remote_units, split, sums, totals, highest, *arrived)
    return out.reshape(tokens, query_heads, head_dim)


def solution(mesh):
    return jax.shard_map(
        on_device,
        mesh=mesh,
        in_specs=(
            P(("groups", "ctx"), ("heads", "rep"), None),
            P(("groups", "ctx"), "heads", None),
            P(("groups", "ctx"), "heads", None),
            P("heads", ("groups", "ctx"), None),
        ),
        out_specs=P(("groups", "ctx"), ("heads", "rep"), None),
        check_vma=False,
    )
```

time: 86.7 us -> 87.1 us (level)
  the two profiles are of different devices: /device:TPU:18 before, /device:TPU:0 now
where the time goes in v3:
time: 87.1 us; the launch traced here: 86.8 us
  Pallas kernels  62.4 us (72%)
  starting transfers between devices  13.2 us (15%)
  local copies, waits for them, and re-layouts  5.17 us (6%)
  waiting for transfers between devices  3.39 us (4%)
  other arithmetic  2.38 us (3%)
    pallas_call x1, Pallas kernels, on_device(): pl.pallas_call(functools.partial(local_kernel, blocks=blocks, kv_heads=kv...  45.4 us
    pallas_call x1, Pallas kernels, on_device(): pl.pallas_call(functools.partial(remote_kernel, shifts=shifts, **sizes),...  12.6 us
    ppermute x3, starting transfers between devices, on_device(): lax.ppermute(parcel, 'ctx', [(i, i + d) for i in range(shards - d)])  9.34 us
    pallas_call x1, Pallas kernels, pack(): pl.pallas_call(functools.partial(pack_kernel, shifts=shifts, used=used, k...  4.38 us
    ppermute x3, starting transfers between devices, on_device(): lax.ppermute(lists, 'ctx', [(j, j - d) for j in range(d, shards)])  3.86 us
    ppermute x3, waiting for transfers between devices, on_device(): lax.ppermute(lists, 'ctx', [(j, j - d) for j in range(d, shards)])  3.38 us
  transfers between devices with their start and end apart: 6, of which 2 were waited for; matrix products, arithmetic and copies ran while one was open for 5% of the time, Pallas kernels for 52%

profile of v3, /device:TPU:0, one launch (start us, length us, event | category | flops | bytes accessed | tf_op | source)
XLA Modules:
  0.0 86.8 jit_solution(13708337389649916030)
XLA Ops:
  0.0 0.7 subtract_add_fusion
  0.7 1.3 %collective-permute-start = (s32[2,24,8]{1,2,0:T(8,128)S(1)}, s32[2,24,8]{1,2,0:T(8,128)S(1)}, u32[]{:S(2)}, u32[]{:S(2)}) collective-permute-start(s32[2,24,8]{1,2,0:T(8,128)S(1)} %get-tuple-element.30), channel_id=1, source_target_pairs={{4,0},{8,4},{12,8},{5,1},{9,5},{13,9},{6,2},{10,6},{14,10},{7,3},{... | collective-permute-start | bytes 4616 | tf_op jit(solution)/shard_map/ppermute | solution.py:385
  2.0 1.3 %collective-permute-start.1 = (s32[2,24,8]{1,2,0:T(8,128)S(1)}, s32[2,24,8]{1,2,0:T(8,128)S(1)}, u32[]{:S(2)}, u32[]{:S(2)}) collective-permute-start(s32[2,24,8]{1,2,0:T(8,128)S(1)} %get-tuple-element.30), channel_id=1, source_target_pairs={{8,0},{12,4},{9,1},{13,5},{10,2},{14,6},{11,3},{15,7},{24,16},{28,... | collective-permute-start | bytes 4616 | tf_op jit(solution)/shard_map/ppermute | solution.py:385
  3.3 1.3 %collective-permute-start.2 = (s32[2,24,8]{1,2,0:T(8,128)S(1)}, s32[2,24,8]{1,2,0:T(8,128)S(1)}, u32[]{:S(2)}, u32[]{:S(2)}) collective-permute-start(s32[2,24,8]{1,2,0:T(8,128)S(1)} %get-tuple-element.30), channel_id=1, source_target_pairs={{12,0},{13,1},{14,2},{15,3},{28,16},{29,17},{30,18},{31,19}} | collective-permute-start | bytes 4616 | tf_op jit(solution)/shard_map/ppermute | solution.py:385
  4.8 0.2 select_reduce_fusion.4
  5.3 0.1 copy.46
  5.8 0.1 copy.47
  6.8 0.1 copy.52
  7.5 0.1 convert_reduce_fusion
  7.6 0.2 select_reduce_fusion.1
  7.9 0.2 select_reduce_fusion
  8.1 0.7 reshape.135.units_ref
  8.8 0.6 reshape.137.units_ref
  9.4 0.6 collective-permute-done.1
  10.0 2.8 %collective-permute-done.2 = s32[2,24,8]{1,2,0:T(8,128)S(1)} collective-permute-done((s32[2,24,8]{1,2,0:T(8,128)S(1)}, s32[2,24,8]{1,2,0:T(8,128)S(1)}, u32[]{:S(2)}, u32[]{:S(2)}) %collective-permute-start.2) | collective-permute-done | bytes 1568 | tf_op jit(solution)/shard_map/ppermute | solution.py:385
  12.8 0.3 select_reduce_fusion.6
  13.4 0.7 reshape.142.request
  14.1 4.4 %pack.1 = (bf16[2,2,256,128]{3,2,1,0:T(8,128)(2,1)}, bf16[2,2,256,128]{3,2,1,0:T(8,128)(2,1)}, bf16[2,2,256,128]{3,2,1,0:T(8,128)(2,1)}, f32[8,512]{1,0:T(8,128)}) custom-call(s32[12]{0:T(128)} %reshape.142.request, bf16[12288,128]{1,0:T(8,128)(2,1)} %bitcast.30, bf16[12288,128]{1,0:T(8,128)(2,1)} %bitcast.32, s32[1]{0:T(128)} %bitcast.4.rest_0_.first_ref), custom_call_target="tpu_custom_call" | custom-call | tf_op jit(solution)/shard_map/pack/pallas_call | solution.py:69
  18.5 1.6 %collective-permute-start.3 = (bf16[2,2,256,128]{3,2,1,0:T(8,128)(2,1)}, bf16[2,2,256,128]{3,2,1,0:T(8,128)(2,1)S(1)}, u32[]{:S(2)}, u32[]{:S(2)}) collective-permute-start(bf16[2,2,256,128]{3,2,1,0:T(8,128)(2,1)} %get-tuple-element.18), channel_id=1, source_target_pairs={{0,4},{4,8},{8,12},{1,5},{5,9},{9,13},{2,6},{6,10},{10,14},{3,7},{... | collective-permute-start | bytes 786440 | tf_op jit(solution)/shard_map/ppermute | solution.py:407
  20.1 6.5 %collective-permute-start.4 = (bf16[2,2,256,128]{3,2,1,0:T(8,128)(2,1)}, bf16[2,2,256,128]{3,2,1,0:T(8,128)(2,1)S(1)}, u32[]{:S(2)}, u32[]{:S(2)}) collective-permute-start(bf16[2,2,256,128]{3,2,1,0:T(8,128)(2,1)} %get-tuple-element.19), channel_id=1, source_target_pairs={{0,8},{4,12},{1,9},{5,13},{2,10},{6,14},{3,11},{7,15},{16,24},{20,... | collective-permute-start | bytes 786440 | tf_op jit(solution)/shard_map/ppermute | solution.py:407
  26.5 1.3 %collective-permute-start.5 = (bf16[2,2,256,128]{3,2,1,0:T(8,128)(2,1)}, bf16[2,2,256,128]{3,2,1,0:T(8,128)(2,1)S(1)}, u32[]{:S(2)}, u32[]{:S(2)}) collective-permute-start(bf16[2,2,256,128]{3,2,1,0:T(8,128)(2,1)} %get-tuple-element.20), channel_id=1, source_target_pairs={{0,12},{1,13},{2,14},{3,15},{16,28},{17,29},{18,30},{19,31}} | collective-permute-start | bytes 786440 | tf_op jit(solution)/shard_map/ppermute | solution.py:407
  27.8 45.4 %local_part.1 = (f32[48,128,512]{2,1,0:T(8,128)}, f32[48,8,512]{2,1,0:T(8,128)}, f32[48,8,512]{2,1,0:T(8,128)}, bf16[48,512,128]{2,1,0:T(8,128)(2,1)}) custom-call(s32[196]{0:T(256)} %reshape.137.units_ref, s32[1]{0:T(128)} %bitcast.4.rest_0_.first_ref, bf16[24576,128]{1,0:T(8,128)(2,1)} %bitcast.43, bf16[12288,128]{1,0:T(8,128)(2,1)} %bitcast.31, ...), custom_call_target="tpu_custom_call" | custom-call | flops 9663676416 | bytes 33554432 | tf_op jit(solution)/shard_map/local_part/pallas_call | solution.py:443
  73.3 0.6 copy-done
  74.1 12.6 %remote_part.1 = bf16[24576,128]{1,0:T(8,128)(2,1)} custom-call(s32[196]{0:T(256)} %reshape.135.units_ref, bf16[48,512,128]{2,1,0:T(8,128)(2,1)} %get-tuple-element.14.split_ref, f32[48,128,512]{2,1,0:T(8,128)} %get-tuple-element.15.sums_in, f32[48,8,512]{2,1,0:T(8,128)} %get-tuple-element.16.totals_in, f32[48,8,512]{2,1,0:T(8,128)} %get-tuple-element.17.highest_ref, ...), custom_call_target="tpu_custom_call" | custom-call | tf_op jit(solution)/shard_map/remote_part/pallas_call | solution.py:465
  (45 shorter events, 2.8 us)
Async XLA Ops:
  0.7 8.7 %collective-permute-start = (s32[2,24,8]{1,2,0:T(8,128)S(1)}, s32[2,24,8]{1,2,0:T(8,128)S(1)}, u32[]{:S(2)}, u32[]{:S(2)}) collective-permute-start(s32[2,24,8]{1,2,0:T(8,128)S(1)} %get-tuple-element.30), channel_id=1, source_target_pairs={{4,0},{8,4},{12,8},{5,1},{9,5},{13,9},{6,2},{10,6},{14,10},{7,3},{... | collective-permute-start | bytes 4616 | tf_op jit(solution)/shard_map/ppermute | solution.py:385
  2.0 8.0 %collective-permute-start.1 = (s32[2,24,8]{1,2,0:T(8,128)S(1)}, s32[2,24,8]{1,2,0:T(8,128)S(1)}, u32[]{:S(2)}, u32[]{:S(2)}) collective-permute-start(s32[2,24,8]{1,2,0:T(8,128)S(1)} %get-tuple-element.30), channel_id=1, source_target_pairs={{8,0},{12,4},{9,1},{13,5},{10,2},{14,6},{11,3},{15,7},{24,16},{28,... | collective-permute-start | bytes 4616 | tf_op jit(solution)/shard_map/ppermute | solution.py:385
  3.3 9.5 %collective-permute-start.2 = (s32[2,24,8]{1,2,0:T(8,128)S(1)}, s32[2,24,8]{1,2,0:T(8,128)S(1)}, u32[]{:S(2)}, u32[]{:S(2)}) collective-permute-start(s32[2,24,8]{1,2,0:T(8,128)S(1)} %get-tuple-element.30), channel_id=1, source_target_pairs={{12,0},{13,1},{14,2},{15,3},{28,16},{29,17},{30,18},{31,19}} | collective-permute-start | bytes 4616 | tf_op jit(solution)/shard_map/ppermute | solution.py:385
  18.5 54.8 %collective-permute-start.3 = (bf16[2,2,256,128]{3,2,1,0:T(8,128)(2,1)}, bf16[2,2,256,128]{3,2,1,0:T(8,128)(2,1)S(1)}, u32[]{:S(2)}, u32[]{:S(2)}) collective-permute-start(bf16[2,2,256,128]{3,2,1,0:T(8,128)(2,1)} %get-tuple-element.18), channel_id=1, source_target_pairs={{0,4},{4,8},{8,12},{1,5},{5,9},{9,13},{2,6},{6,10},{10,14},{3,7},{... | collective-permute-start | bytes 786440 | tf_op jit(solution)/shard_map/ppermute | solution.py:407
  20.1 53.2 %collective-permute-start.4 = (bf16[2,2,256,128]{3,2,1,0:T(8,128)(2,1)}, bf16[2,2,256,128]{3,2,1,0:T(8,128)(2,1)S(1)}, u32[]{:S(2)}, u32[]{:S(2)}) collective-permute-start(bf16[2,2,256,128]{3,2,1,0:T(8,128)(2,1)} %get-tuple-element.19), channel_id=1, source_target_pairs={{0,8},{4,12},{1,9},{5,13},{2,10},{6,14},{3,11},{7,15},{16,24},{20,... | collective-permute-start | bytes 786440 | tf_op jit(solution)/shard_map/ppermute | solution.py:407
  26.5 46.7 %collective-permute-start.5 = (bf16[2,2,256,128]{3,2,1,0:T(8,128)(2,1)}, bf16[2,2,256,128]{3,2,1,0:T(8,128)(2,1)S(1)}, u32[]{:S(2)}, u32[]{:S(2)}) collective-permute-start(bf16[2,2,256,128]{3,2,1,0:T(8,128)(2,1)} %get-tuple-element.20), channel_id=1, source_target_pairs={{0,12},{1,13},{2,14},{3,15},{16,28},{17,29},{18,30},{19,31}} | collective-permute-start | bytes 786440 | tf_op jit(solution)/shard_map/ppermute | solution.py:407
  73.2 0.7 copy-start
  73.3 0.8 copy-start.1
  73.3 0.9 copy-start.2

commit v4 on v3

--- a/solution.py
+++ b/solution.py
@@ -16,6 +16,8 @@
 CLOSED = 3e38
 SAFE_TOTAL = 2.0**100
 VMEM_BYTES = 60 * 2**20
+LOCAL_VMEM_BYTES = 20 * 2**20
+REMOTE_VMEM_BYTES = 12 * 2**20
 UNITS_AT_ONCE = 8
 FIELD = 10
 
@@ -120,11 +122,10 @@
     )
 
 
-def causal(scores):
-    key = lax.broadcasted_iota(jnp.int32, scores.shape, 0)
-    per_head = scores.shape[1] // scores.shape[0]
-    token = lax.broadcasted_iota(jnp.int32, scores.shape, 1) // per_head
-    return jnp.where(key <= token, scores, MASKED)
+def causal_mask(shape):
+    key = lax.broadcasted_iota(jnp.int32, shape, 0)
+    token = lax.broadcasted_iota(jnp.int32, shape, 1) // (shape[1] // shape[0])
+    return jnp.where(key <= token, 0.0, MASKED)
 
 
 def fold(weights):
@@ -203,27 +204,53 @@
     return raise_highest, add_again
 
 
+def step_items(ref, step, items):
+    return ref.at[pl.ds(step * items, items)]
+
+
 def unsafe(totals):
     return jnp.max(jnp.where(totals < SAFE_TOTAL, 0.0, 1.0)) > 0.0
 
 
 def local_kernel(
     units_ref, first_ref, queries_ref, keys_ref, values_ref, clear_ref,
-    sums_ref, totals_ref, highest_ref, split_ref,
-    key_table, value_table, keys_wide, values_wide,
+    all_sums, all_totals, all_highest, all_split,
+    key_table, value_table, keys_raw, values_raw, keys_wide, values_wide, mask_ref, sems,
     *, blocks, step_blocks, used, kv_heads, block_len, scale, units_max, at_once,
 ):
     step = pl.program_id(0)
     rows = block_len * kv_heads
+    sums_ref, totals_ref, highest_ref, split_ref = (
+        step_items(ref, step, step_blocks * used)
+        for ref in (all_sums, all_totals, all_highest, all_split)
+    )
 
     @pl.when(step == 0)
     def _():
+        mask_ref[...] = causal_mask(mask_ref.shape)
+        chunk = rows * at_once
+
+        def copies(turn):
+            place = pl.ds(pl.multiple_of(turn * chunk, chunk), chunk)
+            return [
+                pltpu.make_async_copy(source.at[place], raw.at[place], sems.at[kind, turn])
+                for kind, (source, raw) in enumerate(
+                    ((keys_ref, keys_raw), (values_ref, values_raw))
+                )
+            ]
+
+        for turn in range(blocks // at_once):
+            for copy in copies(turn):
+                copy.start()
+
         def take_apart(turn, carry):
+            for copy in copies(turn):
+                copy.wait()
             for n in range(at_once):
                 block = turn * at_once + n
                 source = block_rows(block, rows)
-                keys_wide[n] = keys_ref[source, :].astype(jnp.float32)
-                values_wide[n] = values_ref[source, :].astype(jnp.float32)
+                keys_wide[n] = keys_raw[source, :].astype(jnp.float32)
+                values_wide[n] = values_raw[source, :].astype(jnp.float32)
                 for head in range(used):
                     picked = pl.ds(first_ref[0] + head, block_len, stride=kv_heads)
                     target = block_rows(block, block_len)
@@ -237,18 +264,19 @@
 
     query_rows = queries_ref.shape[0] // step_blocks
 
-    def own_part(item, block, highest=None):
-        head = lax.rem(item, used)
+    def own_scores(item, block, query):
         here = block_rows(step * step_blocks + block, block_len)
-        scores = causal(score(key_table[head, here, :], split_ref[item]))
-        if highest is None:
-            highest = jnp.max(scores, axis=0, keepdims=True) * scale
+        scores = score(key_table[lax.rem(item, used), here, :], query)
+        return scores + mask_ref[...]
+
+    def own_share(item, block, scores, highest):
+        here = block_rows(step * step_blocks + block, block_len)
         weights = jnp.exp2(scores * scale - highest)
         summed = jnp.dot(
-            value_table[head, here, :], weights.astype(jnp.bfloat16),
+            value_table[lax.rem(item, used), here, :], weights.astype(jnp.bfloat16),
             preferred_element_type=jnp.float32,
         )
-        return highest, fold(weights), summed
+        return fold(weights), summed
 
     def own_blocks(turn, carry):
         todo = []
@@ -256,10 +284,15 @@
             block = turn * at_once + n
             raw = queries_ref[pl.ds(pl.multiple_of(block * query_rows, query_rows), query_rows), :]
             for head, query in enumerate(split_heads(raw, used)):
-                split_ref[block * used + head] = query
-                todo.append((block * used + head, block))
-        for item, (highest, total, summed) in [(item, own_part(item, b)) for item, b in todo]:
-            highest_ref[item] = jnp.broadcast_to(highest, total.shape) + clear_ref[...]
+                todo.append((block * used + head, block, query))
+        scores = [own_scores(*each) for each in todo]
+        highest = [jnp.max(each, axis=0, keepdims=True) * scale for each in scores]
+        shares = [
+            own_share(item, block, s, m) for (item, block, _), s, m in zip(todo, scores, highest)
+        ]
+        for (item, _, query), m, (total, summed) in zip(todo, highest, shares):
+            split_ref[item] = query
+            highest_ref[item] = jnp.broadcast_to(m, total.shape) + clear_ref[...]
             totals_ref[item] = total
             sums_ref[item] = summed
         return carry
@@ -274,7 +307,9 @@
     def _():
         def mend(item, carry):
             highest = raise_highest(item, highest_ref[item][:1])
-            _, total, summed = own_part(item, item // used, highest)
+            block = item // used
+            scores = own_scores(item, block, split_ref[item])
+            total, summed = own_share(item, block, scores, highest)
             sums, totals = add_again(item, highest, summed, total)
             highest_ref[item] = jnp.broadcast_to(highest, totals.shape)
             totals_ref[item] = totals
@@ -285,14 +320,18 @@
 
 
 def remote_kernel(
-    units_ref, split_ref, sums_in, totals_in, highest_ref, *rest,
-    shifts, step_blocks, used, block_len, scale, units_max, at_once,
+    units_ref, all_split, all_sums, all_totals, all_highest, *rest,
+    shifts, blocks, step_blocks, used, block_len, scale, units_max, at_once,
 ):
     parcels, (out_ref, key_table, value_table, sums_ref, totals_ref) = (
         rest[:shifts], rest[shifts:]
     )
     step = pl.program_id(0)
     parcel_rows = REMOTE_BLOCK_MAX * block_len
+    split_ref, sums_in, totals_in, highest_ref = (
+        step_items(ref, step, step_blocks * used)
+        for ref in (all_split, all_sums, all_totals, all_highest)
+    )
 
     @pl.when(step == 0)
     def _():
@@ -338,6 +377,87 @@
         return carry
 
     lax.fori_loop(0, step_blocks // at_once, finish, 0)
+
+
+def stepped(*shape):
+    return pl.BlockSpec(shape, lambda g, *_: (g,) + (0,) * (len(shape) - 1))
+
+
+def whole(shape):
+    return pl.BlockSpec(shape, lambda g, *_: (0,) * len(shape))
+
+
+def local_part(units, first, query_rows, key_rows, value_rows, clear, **sizes):
+    blocks, step_blocks, used = sizes["blocks"], sizes["step_blocks"], sizes["used"]
+    head_dim = query_rows.shape[1]
+    item_rows = clear.shape[1]
+    steps = blocks // step_blocks
+    tokens = blocks * sizes["block_len"]
+    kv_heads = key_rows.shape[0] // tokens
+    wide = pltpu.VMEM((sizes["at_once"], sizes["block_len"] * kv_heads, head_dim), jnp.float32)
+    table = pltpu.VMEM((used, tokens, head_dim), jnp.bfloat16)
+    raw = pltpu.VMEM(key_rows.shape, jnp.bfloat16)
+    row_shape = pltpu.VMEM((blocks * used, 8, item_rows), jnp.float32)
+    return pl.pallas_call(
+        functools.partial(local_kernel, kv_heads=kv_heads, **sizes),
+        grid_spec=pltpu.PrefetchScalarGridSpec(
+            num_scalar_prefetch=2,
+            grid=(steps,),
+            in_specs=[
+                stepped(query_rows.shape[0] // steps, head_dim),
+                pl.BlockSpec(memory_space=pl.ANY), pl.BlockSpec(memory_space=pl.ANY),
+                whole(clear.shape),
+            ],
+            out_specs=[pl.BlockSpec(memory_space=pltpu.VMEM)] * 4,
+            scratch_shapes=[
+                table, table, raw, raw, wide, wide,
+                pltpu.VMEM((sizes["block_len"], item_rows), jnp.float32),
+                pltpu.SemaphoreType.DMA((2, blocks // sizes["at_once"])),
+            ],
+        ),
+        out_shape=[
+            pltpu.VMEM((blocks * used, head_dim, item_rows), jnp.float32),
+            row_shape,
+            row_shape,
+            pltpu.VMEM((blocks * used, item_rows, head_dim), jnp.bfloat16),
+        ],
+        compiler_params=pltpu.CompilerParams(vmem_limit_bytes=LOCAL_VMEM_BYTES),
+        cost_estimate=pl.CostEstimate(
+            flops=2**34, bytes_accessed=32 * 2**20, transcendentals=2**25
+        ),
+        name="local_part",
+    )(units, first, query_rows, key_rows, value_rows, clear)
+
+
+def remote_part(units, states, arrived, out_shape, **sizes):
+    sums, totals, highest, split = (
+        pltpu.with_memory_space_constraint(state, pltpu.VMEM) for state in states
+    )
+    shifts = len(arrived)
+    items = sizes["step_blocks"] * sizes["used"]
+    steps = sizes["blocks"] // sizes["step_blocks"]
+    _, item_rows, head_dim = split.shape
+    table = pltpu.VMEM(
+        (sizes["used"], shifts * arrived[0].shape[2], head_dim), jnp.bfloat16
+    )
+    return pl.pallas_call(
+        functools.partial(remote_kernel, shifts=shifts, **sizes),
+        grid_spec=pltpu.PrefetchScalarGridSpec(
+            num_scalar_prefetch=1,
+            grid=(steps,),
+            in_specs=[pl.BlockSpec(memory_space=pltpu.VMEM)] * (4 + shifts),
+            out_specs=stepped(out_shape[0] // steps, head_dim),
+            scratch_shapes=[
+                table,
+                table,
+                pltpu.VMEM((items, head_dim, item_rows), jnp.float32),
+                pltpu.VMEM((items, 8, item_rows), jnp.float32),
+            ],
+        ),
+        out_shape=jax.ShapeDtypeStruct(out_shape, jnp.bfloat16),
+        compiler_params=pltpu.CompilerParams(vmem_limit_bytes=REMOTE_VMEM_BYTES),
+        name="remote_part",
+    )(units, split, sums, totals, highest, *arrived)
 
 
 def list_units(open_slot, index, steps, units_max):
@@ -396,9 +516,10 @@
         axis=-1,
     )
     first = first.reshape(1)
-    query_rows = queries.reshape(tokens * query_heads, head_dim)
-    key_rows = keys.reshape(tokens * kv_heads, head_dim)
-    value_rows = values.reshape(tokens * kv_heads, head_dim)
+    query_rows, key_rows, value_rows = (
+        pltpu.with_memory_space_constraint(rows.reshape(-1, head_dim), pltpu.HBM)
+        for rows in (queries, keys, values)
+    )
     *parcels, clear = pack(
         request.reshape(-1), first, key_rows, value_rows, kv_heads, shifts, used, block_len,
         (8, item_rows),
@@ -420,67 +541,12 @@
     remote_index = (position - 1 - shard_of) * REMOTE_BLOCK_MAX + jnp.where(is_lowest, 0, 1)
     remote_units = list_units(~local, remote_index, steps, units_max)
 
-    def stepped(*shape):
-        return pl.BlockSpec(shape, lambda g, *_: (g,) + (0,) * (len(shape) - 1))
-
-    def whole(shape):
-        return pl.BlockSpec(shape, lambda g, *_: (0,) * len(shape))
-
-    items = step_blocks * used
-    query_spec = stepped(step_blocks * block_len * query_heads, head_dim)
-    sums_spec = stepped(items, head_dim, item_rows)
-    row_spec = stepped(items, 8, item_rows)
-    split_spec = stepped(items, item_rows, head_dim)
-    sums_shape = jax.ShapeDtypeStruct((blocks * used, head_dim, item_rows), jnp.float32)
-    row_shape = jax.ShapeDtypeStruct((blocks * used, 8, item_rows), jnp.float32)
-    split_shape = jax.ShapeDtypeStruct((blocks * used, item_rows, head_dim), jnp.bfloat16)
     sizes = dict(
-        step_blocks=step_blocks, used=used, block_len=block_len, scale=scale,
+        blocks=blocks, step_blocks=step_blocks, used=used, block_len=block_len, scale=scale,
         units_max=units_max, at_once=at_once,
     )
-    wide = pltpu.VMEM((at_once, block_len * kv_heads, head_dim), jnp.float32)
-    table = pltpu.VMEM((used, tokens, head_dim), jnp.bfloat16)
-    sums, totals, highest, split = pl.pallas_call(
-        functools.partial(local_kernel, blocks=blocks, kv_heads=kv_heads, **sizes),
-        grid_spec=pltpu.PrefetchScalarGridSpec(
-            num_scalar_prefetch=2,
-            grid=(steps,),
-            in_specs=[
-                query_spec, whole(key_rows.shape), whole(value_rows.shape), whole(clear.shape)
-            ],
-            out_specs=[sums_spec, row_spec, row_spec, split_spec],
-            scratch_shapes=[table, table, wide, wide],
-        ),
-        out_shape=[sums_shape, row_shape, row_shape, split_shape],
-        compiler_params=pltpu.CompilerParams(vmem_limit_bytes=VMEM_BYTES),
-        cost_estimate=pl.CostEstimate(
-            flops=3 * tokens * query_heads * picks * block_len * head_dim,
-            bytes_accessed=32 * 2**20,
-            transcendentals=tokens * query_heads * picks * block_len,
-        ),
-        name="local_part",
-    )(local_units, first, query_rows, key_rows, value_rows, clear)
-
-    table = pltpu.VMEM((used, shifts * REMOTE_BLOCK_MAX * block_len, head_dim), jnp.bfloat16)
-    out = pl.pallas_call(
-        functools.partial(remote_kernel, shifts=shifts, **sizes),
-        grid_spec=pltpu.PrefetchScalarGridSpec(
-            num_scalar_prefetch=1,
-            grid=(steps,),
-            in_specs=[split_spec, sums_spec, row_spec, row_spec]
-            + [whole(arrived[0].shape)] * shifts,
-            out_specs=query_spec,
-            scratch_shapes=[
-                table,
-                table,
-                pltpu.VMEM((items, head_dim, item_rows), jnp.float32),
-                pltpu.VMEM((items, 8, item_rows), jnp.float32),
-            ],
-        ),
-        out_shape=jax.ShapeDtypeStruct(query_rows.shape, jnp.bfloat16),
-        compiler_params=pltpu.CompilerParams(vmem_limit_bytes=VMEM_BYTES),
-        name="remote_part",
-    )(remote_units, split, sums, totals, highest, *arrived)
+    states = local_part(local_units, first, query_rows, key_rows, value_rows, clear, **sizes)
+    out = remote_part(remote_units, states, arrived, query_rows.shape, **sizes)
     return out.reshape(tokens, query_heads, head_dim)
 
 

time: 87.1 us -> 74.3 us (0.85)
  the two profiles are of different devices: /device:TPU:0 before, /device:TPU:18 now
where the time goes in v4:
time: 74.3 us; the launch traced here: 73.9 us
  Pallas kernels  55.9 us (75%)
  starting transfers between devices  11.4 us (15%)
  local copies, waits for them, and re-layouts  3.86 us (5%)
  other arithmetic  2.38 us (3%)
    pallas_call x1, Pallas kernels, local_part(): pl.pallas_call(functools.partial(local_kernel, kv_heads=kv_heads, **sizes...  34.4 us
    pallas_call x1, Pallas kernels, remote_part(): pl.pallas_call(functools.partial(remote_kernel, shifts=shifts, **sizes),...  17.2 us
    ppermute x3, starting transfers between devices, on_device(): lax.ppermute(parcel, 'ctx', [(i, i + d) for i in range(shards - d)])  7.14 us
    pallas_call x1, Pallas kernels, pack(): pl.pallas_call(functools.partial(pack_kernel, shifts=shifts, used=used, k...  4.39 us
    ppermute x3, starting transfers between devices, on_device(): lax.ppermute(lists, 'ctx', [(j, j - d) for j in range(d, shards)])  4.3 us
  transfers between devices with their start and end apart: 6, of which 0 were waited for; matrix products, arithmetic and copies ran while one was open for 5% of the time, Pallas kernels for 46%

profile of v4, /device:TPU:18, one launch (start us, length us, event | category | flops | bytes accessed | tf_op | source)
XLA Modules:
  0.0 73.9 jit_solution(4032229317081845554)
XLA Ops:
  0.0 0.7 subtract_add_fusion
  0.7 2.3 %collective-permute-start = (s32[2,24,8]{1,2,0:T(8,128)S(1)}, s32[2,24,8]{1,2,0:T(8,128)S(1)}, u32[]{:S(2)}, u32[]{:S(2)}) collective-permute-start(s32[2,24,8]{1,2,0:T(8,128)S(1)} %get-tuple-element.30), channel_id=1, source_target_pairs={{4,0},{8,4},{12,8},{5,1},{9,5},{13,9},{6,2},{10,6},{14,10},{7,3},{... | collective-permute-start | bytes 4616 | tf_op jit(solution)/shard_map/ppermute | solution.py:505
  3.1 1.3 %collective-permute-start.1 = (s32[2,24,8]{1,2,0:T(8,128)S(1)}, s32[2,24,8]{1,2,0:T(8,128)S(1)}, u32[]{:S(2)}, u32[]{:S(2)}) collective-permute-start(s32[2,24,8]{1,2,0:T(8,128)S(1)} %get-tuple-element.30), channel_id=1, source_target_pairs={{8,0},{12,4},{9,1},{13,5},{10,2},{14,6},{11,3},{15,7},{24,16},{28,... | collective-permute-start | bytes 4616 | tf_op jit(solution)/shard_map/ppermute | solution.py:505
  4.4 0.7 collective-permute-start.2
  5.3 0.2 select_reduce_fusion.4
  5.8 0.1 copy.46
  6.0 0.1 slice_shift-left_fusion.1
  6.2 0.1 copy.47
  6.8 0.1 copy.51
  7.1 0.1 slice_shift-left_fusion
  7.3 0.1 copy.52
  7.7 0.1 copy.54
  7.9 0.1 convert_reduce_fusion
  8.1 0.2 select_reduce_fusion.1
  8.3 0.2 select_reduce_fusion
  8.7 0.3 select_reduce_fusion.6
  9.3 0.7 reshape.142.request
  10.0 4.4 %pack.1 = (bf16[2,2,256,128]{3,2,1,0:T(8,128)(2,1)}, bf16[2,2,256,128]{3,2,1,0:T(8,128)(2,1)}, bf16[2,2,256,128]{3,2,1,0:T(8,128)(2,1)}, f32[8,512]{1,0:T(8,128)}) custom-call(s32[12]{0:T(128)} %reshape.142.request, bf16[12288,128]{1,0:T(8,128)(2,1)} %bitcast.30, bf16[12288,128]{1,0:T(8,128)(2,1)} %bitcast.32, s32[1]{0:T(128)} %bitcast.4.rest_0_.first_ref), custom_call_target="tpu_custom_call" | custom-call | tf_op jit(solution)/shard_map/pack/pallas_call | solution.py:71
  14.4 5.2 %collective-permute-start.3 = (bf16[2,2,256,128]{3,2,1,0:T(8,128)(2,1)}, bf16[2,2,256,128]{3,2,1,0:T(8,128)(2,1)S(1)}, u32[]{:S(2)}, u32[]{:S(2)}) collective-permute-start(bf16[2,2,256,128]{3,2,1,0:T(8,128)(2,1)} %get-tuple-element.18), channel_id=1, source_target_pairs={{0,4},{4,8},{8,12},{1,5},{5,9},{9,13},{2,6},{6,10},{10,14},{3,7},{... | collective-permute-start | bytes 786440 | tf_op jit(solution)/shard_map/ppermute | solution.py:528
  19.6 1.3 %collective-permute-start.4 = (bf16[2,2,256,128]{3,2,1,0:T(8,128)(2,1)}, bf16[2,2,256,128]{3,2,1,0:T(8,128)(2,1)S(1)}, u32[]{:S(2)}, u32[]{:S(2)}) collective-permute-start(bf16[2,2,256,128]{3,2,1,0:T(8,128)(2,1)} %get-tuple-element.19), channel_id=1, source_target_pairs={{0,8},{4,12},{1,9},{5,13},{2,10},{6,14},{3,11},{7,15},{16,24},{20,... | collective-permute-start | bytes 786440 | tf_op jit(solution)/shard_map/ppermute | solution.py:528
  20.9 0.7 collective-permute-start.5
  21.6 0.7 copy-done
  22.3 34.4 %local_part.1 = (f32[48,128,512]{2,1,0:T(8,128)S(1)}, f32[48,8,512]{2,1,0:T(8,128)S(1)}, f32[48,8,512]{2,1,0:T(8,128)S(1)}, bf16[48,512,128]{2,1,0:T(8,128)(2,1)S(1)}) custom-call(s32[196]{0:T(256)S(1)} %reshape.137.units_ref, s32[1]{0:T(128)} %bitcast.4.rest_0_.first_ref, bf16[24576,128]{1,0:T(8,128)(2,1)} %bitcast.43, bf16[12288,128]{1,0:T(8,128)(2,1)} %bitcast.31, ...), custom_call_target="tpu_custom_call" | custom-call | flops 17179869184 | bytes 33554432 | tf_op jit(solution)/shard_map/local_part/pallas_call | solution.py:401
  56.7 17.2 %remote_part.1 = bf16[24576,128]{1,0:T(8,128)(2,1)} custom-call(s32[196]{0:T(256)S(1)} %reshape.135.units_ref, bf16[48,512,128]{2,1,0:T(8,128)(2,1)S(1)} %get-tuple-element.14.all_split, f32[48,128,512]{2,1,0:T(8,128)S(1)} %get-tuple-element.15.all_sums, f32[48,8,512]{2,1,0:T(8,128)S(1)} %get-tuple-element.16.all_totals, ...), custom_call_target="tpu_custom_call" | custom-call | tf_op jit(solution)/shard_map/remote_part/pallas_call | solution.py:443
  (41 shorter events, 2.3 us)
Async XLA Ops:
  0.7 8.0 %collective-permute-start = (s32[2,24,8]{1,2,0:T(8,128)S(1)}, s32[2,24,8]{1,2,0:T(8,128)S(1)}, u32[]{:S(2)}, u32[]{:S(2)}) collective-permute-start(s32[2,24,8]{1,2,0:T(8,128)S(1)} %get-tuple-element.30), channel_id=1, source_target_pairs={{4,0},{8,4},{12,8},{5,1},{9,5},{13,9},{6,2},{10,6},{14,10},{7,3},{... | collective-permute-start | bytes 4616 | tf_op jit(solution)/shard_map/ppermute | solution.py:505
  3.1 5.7 %collective-permute-start.1 = (s32[2,24,8]{1,2,0:T(8,128)S(1)}, s32[2,24,8]{1,2,0:T(8,128)S(1)}, u32[]{:S(2)}, u32[]{:S(2)}) collective-permute-start(s32[2,24,8]{1,2,0:T(8,128)S(1)} %get-tuple-element.30), channel_id=1, source_target_pairs={{8,0},{12,4},{9,1},{13,5},{10,2},{14,6},{11,3},{15,7},{24,16},{28,... | collective-permute-start | bytes 4616 | tf_op jit(solution)/shard_map/ppermute | solution.py:505
  4.4 4.4 %collective-permute-start.2 = (s32[2,24,8]{1,2,0:T(8,128)S(1)}, s32[2,24,8]{1,2,0:T(8,128)S(1)}, u32[]{:S(2)}, u32[]{:S(2)}) collective-permute-start(s32[2,24,8]{1,2,0:T(8,128)S(1)} %get-tuple-element.30), channel_id=1, source_target_pairs={{12,0},{13,1},{14,2},{15,3},{28,16},{29,17},{30,18},{31,19}} | collective-permute-start | bytes 4616 | tf_op jit(solution)/shard_map/ppermute | solution.py:505
  14.4 42.3 %collective-permute-start.3 = (bf16[2,2,256,128]{3,2,1,0:T(8,128)(2,1)}, bf16[2,2,256,128]{3,2,1,0:T(8,128)(2,1)S(1)}, u32[]{:S(2)}, u32[]{:S(2)}) collective-permute-start(bf16[2,2,256,128]{3,2,1,0:T(8,128)(2,1)} %get-tuple-element.18), channel_id=1, source_target_pairs={{0,4},{4,8},{8,12},{1,5},{5,9},{9,13},{2,6},{6,10},{10,14},{3,7},{... | collective-permute-start | bytes 786440 | tf_op jit(solution)/shard_map/ppermute | solution.py:528
  19.6 37.1 %collective-permute-start.4 = (bf16[2,2,256,128]{3,2,1,0:T(8,128)(2,1)}, bf16[2,2,256,128]{3,2,1,0:T(8,128)(2,1)S(1)}, u32[]{:S(2)}, u32[]{:S(2)}) collective-permute-start(bf16[2,2,256,128]{3,2,1,0:T(8,128)(2,1)} %get-tuple-element.19), channel_id=1, source_target_pairs={{0,8},{4,12},{1,9},{5,13},{2,10},{6,14},{3,11},{7,15},{16,24},{20,... | collective-permute-start | bytes 786440 | tf_op jit(solution)/shard_map/ppermute | solution.py:528
  20.9 35.8 %collective-permute-start.5 = (bf16[2,2,256,128]{3,2,1,0:T(8,128)(2,1)}, bf16[2,2,256,128]{3,2,1,0:T(8,128)(2,1)S(1)}, u32[]{:S(2)}, u32[]{:S(2)}) collective-permute-start(bf16[2,2,256,128]{3,2,1,0:T(8,128)(2,1)} %get-tuple-element.20), channel_id=1, source_target_pairs={{0,12},{1,13},{2,14},{3,15},{16,28},{17,29},{18,30},{19,31}} | collective-permute-start | bytes 786440 | tf_op jit(solution)/shard_map/ppermute | solution.py:528
  21.6 0.7 copy-start

commit v5 on v4

v5 whole, which is shorter than its diff:
```python
import functools

import jax
import jax.numpy as jnp
from jax import lax
from jax.experimental import pallas as pl
from jax.experimental.pallas import tpu as pltpu
from jax.sharding import PartitionSpec as P

QUERY_HEADS = 32
KEY_VALUE_HEADS = 8
REMOTE_BLOCK_MAX = 2
GROUP = QUERY_HEADS // KEY_VALUE_HEADS
LOG2E = 1.4426950408889634
MASKED = -1e30
CLOSED = 3e38
SAFE_TOTAL = 2.0**100
VMEM_BYTES = 60 * 2**20
LOCAL_VMEM_BYTES = 22 * 2**20
REMOTE_VMEM_BYTES = 22 * 2**20
UNITS_AT_ONCE = 8
FIELD = 10
ONES_ROWS = 16


def block_rows(index, block_len):
    return pl.ds(pl.multiple_of(index * block_len, block_len), block_len)


def pack_kernel(
    request, keys_ref, values_ref, *rest, shifts, used, kv_heads, block_len
):
    first_ref, outs = rest[0], rest[1 : shifts + 1]
    clear_ref, blocks_ref, wide_ref, sems = rest[shifts + 1 :]
    rows = block_len * kv_heads
    clear_ref[...] = jnp.zeros_like(clear_ref)
    wanted = [
        (shift, head, turn)
        for shift in range(shifts)
        for head in range(used)
        for turn in range(REMOTE_BLOCK_MAX)
    ]
    copies = []
    for at in range(len(wanted)):
        for kind, table in enumerate((keys_ref, values_ref)):
            copies.append(
                pltpu.make_async_copy(
                    table.at[block_rows(request[at], rows)],
                    blocks_ref.at[2 * at + kind],
                    sems.at[2 * at + kind],
                )
            )
    for copy in copies:
        copy.start()
    for at, (shift, head, turn) in enumerate(wanted):
        target = slice(turn * block_len, (turn + 1) * block_len)
        picked = pl.ds(first_ref[0] + head, block_len, stride=kv_heads)
        for kind in range(2):
            place = 2 * at + kind
            copies[place].wait()
            wide_ref[place] = blocks_ref[place].astype(jnp.float32)
            block = wide_ref[place, picked, :]
            outs[shift][kind, head, target, :] = (block.T if kind else block).astype(jnp.bfloat16)


def pack(request, first, keys, values, kv_heads, shifts, used, block_len, row_shape):
    head_dim = keys.shape[-1]
    parcel = (2, used, REMOTE_BLOCK_MAX * block_len, head_dim)
    anywhere = pl.BlockSpec(memory_space=pl.ANY)
    count = 2 * shifts * used * REMOTE_BLOCK_MAX
    rows = block_len * kv_heads
    return pl.pallas_call(
        functools.partial(
            pack_kernel, shifts=shifts, used=used, kv_heads=kv_heads, block_len=block_len
        ),
        grid_spec=pltpu.PrefetchScalarGridSpec(
            num_scalar_prefetch=1,
            grid=(1,),
            in_specs=[anywhere, anywhere, pl.BlockSpec(memory_space=pltpu.SMEM)],
            out_specs=[pl.BlockSpec(parcel, lambda g, *_: (0, 0, 0, 0))] * shifts
            + [pl.BlockSpec(memory_space=pltpu.VMEM)],
            scratch_shapes=[
                pltpu.VMEM((count, rows, head_dim), jnp.bfloat16),
                pltpu.VMEM((count, rows, head_dim), jnp.float32),
                pltpu.SemaphoreType.DMA((count,)),
            ],
        ),
        out_shape=[jax.ShapeDtypeStruct(parcel, jnp.bfloat16)] * shifts
        + [pltpu.VMEM(row_shape, jnp.float32)],
        compiler_params=pltpu.CompilerParams(vmem_limit_bytes=VMEM_BYTES),
        name="pack",
    )(request, keys, values, first)


def split_heads(rows, used):
    count, head_dim = rows.shape
    wide = rows.astype(jnp.float32)
    if used == 1:
        return (wide,)
    wide = wide.reshape(count // 16, 2, 8, head_dim)
    even, odd = wide[:, 0], wide[:, 1]
    upper = lax.broadcasted_iota(jnp.int32, even.shape, 1) < GROUP
    first = jnp.where(upper, even, pltpu.roll(odd, GROUP, 1))
    second = jnp.where(upper, pltpu.roll(even, GROUP, 1), odd)
    return tuple(part.reshape(count // 2, head_dim) for part in (first, second))


def join_heads(first, *others):
    count, head_dim = first.shape
    if not others:
        return first.astype(jnp.bfloat16)
    (second,) = others
    first = first.reshape(count // 8, 8, head_dim)
    second = second.reshape(count // 8, 8, head_dim)
    upper = lax.broadcasted_iota(jnp.int32, first.shape, 1) < GROUP
    even = jnp.where(upper, first, pltpu.roll(second, GROUP, 1))
    odd = jnp.where(upper, pltpu.roll(first, GROUP, 1), second)
    return jnp.stack([even, odd], axis=1).reshape(count * 2, head_dim).astype(jnp.bfloat16)


def score(key_rows, query):
    return lax.dot_general(
        key_rows, query, (((1,), (1,)), ((), ())), preferred_element_type=jnp.float32
    )


def causal_mask(shape):
    key = lax.broadcasted_iota(jnp.int32, shape, 0)
    token = lax.broadcasted_iota(jnp.int32, shape, 1) // (shape[1] // shape[0])
    return jnp.where(key <= token, 0.0, MASKED)


def two_parts(values):
    high = values.astype(jnp.bfloat16)
    low = (values - high.astype(jnp.float32)).astype(jnp.bfloat16)
    return jnp.concatenate([high, low], axis=-1)


def doubled(key_rows):
    return jnp.concatenate([key_rows, key_rows], axis=-1)


def attend_units(
    units_ref, queries_ref, keys_ref, values_ref, highest_ref, sums_ref,
    *, used, block_len, units_max,
):
    def read(unit):
        code = units_ref[unit]
        mask = (1 << FIELD) - 1
        return code >> (2 * FIELD), ((code >> FIELD) & mask) - 1, (code & mask) - 1

    def rows_of(ref, item, slot):
        height = ref.shape[1] // (keys_ref.shape[1] // block_len)
        return ref[lax.rem(item, used), block_rows(jnp.maximum(slot, 0), height), :]

    def scores_of(unit):
        item, *slots = unit
        rows = jnp.concatenate([rows_of(keys_ref, item, slot) for slot in slots], axis=0)
        return score(doubled(rows), queries_ref[item])

    def weigh(unit, scores, highest):
        item, *slots = unit
        parts = []
        for turn, slot in enumerate(slots):
            shift = jnp.where(slot < 0, CLOSED, highest)
            parts.append(jnp.exp2(scores[turn * block_len : (turn + 1) * block_len] - shift))
        weights = jnp.concatenate(parts, axis=0).astype(jnp.bfloat16)
        columns = jnp.concatenate([rows_of(values_ref, item, slot) for slot in slots], axis=1)
        return jnp.dot(columns, weights, preferred_element_type=jnp.float32)

    count = units_ref[units_max]

    def some(turn, carry):
        units = [read(turn * UNITS_AT_ONCE + n) for n in range(UNITS_AT_ONCE)]
        scores = [scores_of(unit) for unit in units]
        for unit, its_scores in zip(units, scores):
            sums_ref[unit[0]] += weigh(unit, its_scores, highest_ref[unit[0], :1, :])
        return carry

    lax.fori_loop(0, (count + UNITS_AT_ONCE - 1) // UNITS_AT_ONCE, some, 0)

    def only(unit, item):
        its, first, second = read(unit)
        return item, jnp.where(its == item, first, -1), jnp.where(its == item, second, -1)

    def raise_highest(item, highest):
        def look(turn, highest):
            unit = only(turn, item)
            scores = scores_of(unit)
            for place, slot in enumerate(unit[1:]):
                part = scores[place * block_len : (place + 1) * block_len]
                found = jnp.max(part, axis=0, keepdims=True)
                highest = jnp.where(slot < 0, highest, jnp.maximum(highest, found))
            return highest

        return lax.fori_loop(0, count, look, highest)

    def add_again(item, highest):
        def add(turn, carry):
            unit = only(turn, item)
            sums_ref[item] += weigh(unit, scores_of(unit), highest)
            return carry

        lax.fori_loop(0, count, add, 0)

    return raise_highest, add_again


def unsafe(sums_ref, height):
    totals = sums_ref[:, height : height + 8, :]
    return jnp.max(jnp.where(totals < SAFE_TOTAL, 0.0, 1.0)) > 0.0


def local_kernel(
    units_ref, first_ref, queries_ref, keys_ref, values_ref, clear_ref,
    sums_ref, highest_ref, split_ref,
    key_table, value_table, queries_raw, keys_raw, values_raw, keys_wide, values_wide, mask_ref,
    sems,
    *, blocks, used, kv_heads, block_len, scale, units_max, at_once,
):
    rows = block_len * kv_heads
    query_rows = queries_ref.shape[0] // blocks
    height = value_table.shape[1] // blocks
    head_dim = keys_ref.shape[1]

    def copies(turn):
        found = []
        for kind, (source, raw) in enumerate(
            ((keys_ref, keys_raw), (values_ref, values_raw), (queries_ref, queries_raw))
        ):
            chunk = source.shape[0] // blocks * at_once
            place = pl.ds(pl.multiple_of(turn * chunk, chunk), chunk)
            found.append(pltpu.make_async_copy(source.at[place], raw.at[place], sems.at[kind, turn]))
        return found

    for turn in range(blocks // at_once):
        for copy in copies(turn):
            copy.start()
    mask_ref[...] = causal_mask(mask_ref.shape) + clear_ref[:1, :1]
    ones = jnp.ones((height - head_dim, block_len), jnp.bfloat16)

    def own_scores(item, block, query):
        here = key_table[lax.rem(item, used), block_rows(block, block_len), :]
        return score(doubled(here), query) + mask_ref[...]

    def own_sum(item, block, scores, highest):
        weights = jnp.exp2(scores - highest).astype(jnp.bfloat16)
        columns = value_table[lax.rem(item, used), block_rows(block, height), :]
        return jnp.dot(columns, weights, preferred_element_type=jnp.float32)

    def chunk(turn, carry):
        for copy in copies(turn):
            copy.wait()
        todo = []
        for n in range(at_once):
            block = turn * at_once + n
            source = block_rows(block, rows)
            keys_wide[n] = keys_raw[source, :].astype(jnp.float32)
            values_wide[n] = values_raw[source, :].astype(jnp.float32)
            raw = queries_raw[block_rows(block, query_rows), :]
            for head, query in enumerate(split_heads(raw, used)):
                picked = pl.ds(first_ref[0] + head, block_len, stride=kv_heads)
                key_rows = keys_wide[n, picked, :].astype(jnp.bfloat16)
                columns = jnp.concatenate(
                    [values_wide[n, picked, :].T.astype(jnp.bfloat16), ones], axis=0
                )
                key_table[head, block_rows(block, block_len), :] = key_rows
                value_table[head, block_rows(block, height), :] = columns
                query = two_parts(query * scale)
                split_ref[block * used + head] = query
                todo.append((block * used + head, query, key_rows, columns))
        scores = [score(doubled(k), query) + mask_ref[...] for _, query, k, _ in todo]
        for (item, _, _, columns), its_scores in zip(todo, scores):
            highest = jnp.max(its_scores, axis=0, keepdims=True)
            weights = jnp.exp2(its_scores - highest).astype(jnp.bfloat16)
            highest_ref[item] = jnp.broadcast_to(highest, highest_ref.shape[1:])
            sums_ref[item] = jnp.dot(columns, weights, preferred_element_type=jnp.float32)
        return carry

    lax.fori_loop(0, blocks // at_once, chunk, 0)
    raise_highest, add_again = attend_units(
        units_ref, split_ref, key_table, value_table, highest_ref, sums_ref,
        used=used, block_len=block_len, units_max=units_max,
    )

    @pl.when(unsafe(sums_ref, head_dim))
    def _():
        def mend(item, carry):
            highest = raise_highest(item, highest_ref[item][:1])
            block = item // used
            scores = own_scores(item, block, split_ref[item])
            highest_ref[item] = jnp.broadcast_to(highest, highest_ref.shape[1:])
            sums_ref[item] = own_sum(item, block, scores, highest)
            add_again(item, highest)
            return carry

        lax.fori_loop(0, blocks * used, mend, 0)


def remote_kernel(
    units_ref, split_ref, sums_in, highest_ref, *rest,
    shifts, blocks, used, block_len, units_max, at_once,
):
    parcels, (out_ref, key_table, value_table, sums_ref, staged, sems) = (
        rest[:shifts], rest[shifts:]
    )
    head_dim = out_ref.shape[1]
    height = sums_in.shape[1]
    query_rows = out_ref.shape[0] // blocks
    ones = jnp.ones((height - head_dim, block_len), jnp.bfloat16)

    for shift, parcel in enumerate(parcels):
        for turn in range(REMOTE_BLOCK_MAX):
            at = shift * REMOTE_BLOCK_MAX + turn
            source = slice(turn * block_len, (turn + 1) * block_len)
            for head in range(used):
                key_table[head, at * block_len : (at + 1) * block_len, :] = parcel[0, head, source, :]
                value_table[head, at * height : at * height + head_dim, :] = parcel[
                    1, head, source, :
                ]
                value_table[head, at * height + head_dim : (at + 1) * height, :] = ones

    def take(item, carry):
        sums_ref[item] = sums_in[item]
        return carry

    lax.fori_loop(0, blocks * used, take, 0)
    raise_highest, add_again = attend_units(
        units_ref, split_ref, key_table, value_table, highest_ref, sums_ref,
        used=used, block_len=block_len, units_max=units_max,
    )

    @pl.when(unsafe(sums_ref, head_dim))
    def _():
        def mend(item, carry):
            before = highest_ref[item][:1]
            highest = raise_highest(item, before)
            sums_ref[item] = sums_in[item] * jnp.exp2(before - highest)
            add_again(item, highest)
            return carry

        lax.fori_loop(0, blocks * used, mend, 0)

    rows = at_once * query_rows

    def give(turn):
        slot = lax.rem(turn, 2)
        place = pl.ds(pl.multiple_of(turn * rows, rows), rows)
        return pltpu.make_async_copy(staged.at[slot], out_ref.at[place], sems.at[slot])

    def finish(turn, carry):
        slot = lax.rem(turn, 2)

        @pl.when(turn >= 2)
        def _():
            give(turn - 2).wait()

        for n in range(at_once):
            parts = []
            for head in range(used):
                item = (turn * at_once + n) * used + head
                total = sums_ref[item, head_dim : head_dim + 1, :]
                parts.append((sums_ref[item, :head_dim, :] * (1.0 / total)).T)
            staged[slot, n * query_rows : (n + 1) * query_rows, :] = join_heads(*parts)
        give(turn).start()
        return carry

    turns = blocks // at_once
    lax.fori_loop(0, turns, finish, 0)
    for turn in range(max(0, turns - 2), turns):
        give(turn).wait()


def local_part(units, first, query_rows, key_rows, value_rows, clear, **sizes):
    blocks, used, block_len = sizes["blocks"], sizes["used"], sizes["block_len"]
    at_once = sizes["at_once"]
    head_dim = query_rows.shape[1]
    item_rows = query_rows.shape[0] // (blocks * used)
    kv_heads = key_rows.shape[0] // (blocks * block_len)
    anywhere = pl.BlockSpec(memory_space=pl.ANY)
    in_vmem = pl.BlockSpec(memory_space=pltpu.VMEM)
    wide = pltpu.VMEM((at_once, block_len * kv_heads, head_dim), jnp.float32)
    height = head_dim + ONES_ROWS
    return pl.pallas_call(
        functools.partial(local_kernel, kv_heads=kv_heads, **sizes),
        grid_spec=pltpu.PrefetchScalarGridSpec(
            num_scalar_prefetch=2,
            grid=(1,),
            in_specs=[anywhere, anywhere, anywhere, in_vmem],
            out_specs=[in_vmem] * 3,
            scratch_shapes=[
                pltpu.VMEM((used, blocks * block_len, head_dim), jnp.bfloat16),
                pltpu.VMEM((used, blocks * height, block_len), jnp.bfloat16),
                pltpu.VMEM(query_rows.shape, jnp.bfloat16),
                pltpu.VMEM(key_rows.shape, jnp.bfloat16),
                pltpu.VMEM(key_rows.shape, jnp.bfloat16),
                wide,
                wide,
                pltpu.VMEM((block_len, item_rows), jnp.float32),
                pltpu.SemaphoreType.DMA((3, blocks // at_once)),
            ],
        ),
        out_shape=[
            pltpu.VMEM((blocks * used, height, item_rows), jnp.float32),
            pltpu.VMEM((blocks * used, 8, item_rows), jnp.float32),
            pltpu.VMEM((blocks * used, item_rows, 2 * head_dim), jnp.bfloat16),
        ],
        compiler_params=pltpu.CompilerParams(vmem_limit_bytes=LOCAL_VMEM_BYTES),
        cost_estimate=pl.CostEstimate(
            flops=2**34, bytes_accessed=32 * 2**20, transcendentals=2**25
        ),
        name="local_part",
    )(units, first, query_rows, key_rows, value_rows, in_place(clear))


def in_place(array):
    return pltpu.with_memory_space_constraint(array, pltpu.VMEM)


def remote_part(units, states, arrived, out_shape, **sizes):
    sums, highest, split = (in_place(state) for state in states)
    shifts = len(arrived)
    blocks, used, block_len = sizes["blocks"], sizes["used"], sizes["block_len"]
    height = sums.shape[1]
    head_dim = out_shape[1]
    slots = shifts * REMOTE_BLOCK_MAX
    sizes.pop("scale")
    return pl.pallas_call(
        functools.partial(remote_kernel, shifts=shifts, **sizes),
        grid_spec=pltpu.PrefetchScalarGridSpec(
            num_scalar_prefetch=1,
            grid=(1,),
            in_specs=[pl.BlockSpec(memory_space=pltpu.VMEM)] * (3 + shifts),
            out_specs=pl.BlockSpec(memory_space=pl.ANY),
            scratch_shapes=[
                pltpu.VMEM((used, slots * block_len, head_dim), jnp.bfloat16),
                pltpu.VMEM((used, slots * height, block_len), jnp.bfloat16),
                pltpu.VMEM(sums.shape, jnp.float32),
                pltpu.VMEM(
                    (2, sizes["at_once"] * out_shape[0] // blocks, head_dim), jnp.bfloat16
                ),
                pltpu.SemaphoreType.DMA((2,)),
            ],
        ),
        out_shape=jax.ShapeDtypeStruct(out_shape, jnp.bfloat16),
        compiler_params=pltpu.CompilerParams(vmem_limit_bytes=REMOTE_VMEM_BYTES),
        name="remote_part",
    )(units, split, sums, highest, *arrived)


def list_units(open_slots, index, units_max):
    lists, items, picks = index.shape
    ahead = jnp.arange(picks)[:, None] < jnp.arange(picks)[None, :]
    place = jnp.sum(open_slots[..., :, None] & ahead, axis=-2)
    half = jnp.arange(0, picks, 2)
    hit = open_slots[..., :, None]
    even = jnp.sum(
        jnp.where(hit & (place[..., :, None] == half), index[..., :, None] + 1, 0), axis=-2
    )
    odd = jnp.sum(
        jnp.where(hit & (place[..., :, None] == half + 1), index[..., :, None] + 1, 0), axis=-2
    )
    item = jnp.arange(items, dtype=jnp.int32)[None, :, None]
    codes = ((item << (2 * FIELD)) + (even << FIELD) + odd).reshape(lists, -1)
    filled = (even > 0).reshape(lists, -1)
    ahead = jnp.arange(codes.shape[1])[:, None] < jnp.arange(codes.shape[1])[None, :]
    place = jnp.sum(filled[:, :, None] & ahead, axis=1)
    target = jnp.arange(units_max + 1)
    here = filled[:, :, None] & (place[:, :, None] == target)
    count = jnp.sum(filled, axis=1, keepdims=True, dtype=jnp.int32)
    listed = jnp.sum(jnp.where(here, codes[:, :, None], 0), axis=1)
    return jnp.where(target == units_max, count, listed).astype(jnp.int32)


def on_device(queries, keys, values, chosen):
    tokens, query_heads, head_dim = queries.shape
    kv_heads = keys.shape[1]
    blocks, picks = chosen.shape[1:]
    block_len = tokens // blocks
    used = max(1, query_heads // GROUP)
    shards = lax.axis_size("ctx")
    shifts = shards - 1
    position = lax.axis_index("ctx")
    base = position * blocks
    first = lax.axis_index("rep") * query_heads // GROUP
    scale = LOG2E * head_dim**-0.5
    at_once = next(n for n in (3, 2, 1) if blocks % n == 0)
    units_max = blocks * used * ((picks + 1) // 2)
    units_max = -(-units_max // UNITS_AT_ONCE) * UNITS_AT_ONCE

    lists = lax.dynamic_slice_in_dim(chosen, first, used, 0)
    wanted = jnp.stack(
        [
            lax.ppermute(lists, "ctx", [(j, j - d) for j in range(d, shards)])
            for d in range(1, shards)
        ]
    )
    within = wanted - base
    mine = (within >= 0) & (within < blocks)
    request = jnp.stack(
        [
            jnp.min(jnp.where(mine, within, blocks - 1), axis=(2, 3)),
            jnp.max(jnp.where(mine, within, 0), axis=(2, 3)),
        ],
        axis=-1,
    )
    first = first.reshape(1)
    query_rows, key_rows, value_rows = (
        pltpu.with_memory_space_constraint(rows.reshape(-1, head_dim), pltpu.HBM)
        for rows in (queries, keys, values)
    )
    *parcels, clear = pack(
        request.reshape(-1), first, key_rows, value_rows, kv_heads, shifts, used, block_len,
        (8, head_dim),
    )
    arrived = [
        lax.ppermute(parcel, "ctx", [(i, i + d) for i in range(shards - d)])
        for d, parcel in zip(range(1, shards), parcels)
    ]

    by_item = jnp.transpose(lists, (1, 0, 2)).reshape(blocks * used, picks)
    local = by_item >= base
    own = base + jnp.arange(blocks * used) // used
    shard_of = by_item // blocks
    from_shard = shard_of[..., None] == jnp.arange(shards)
    lowest = jnp.min(
        jnp.where(from_shard, by_item[..., None], shards * blocks)
        .reshape(blocks, used, picks, shards),
        axis=(0, 2),
    )
    lowest = jnp.tile(lowest, (blocks, 1))[:, None, :]
    is_lowest = jnp.any(from_shard & (by_item[..., None] == lowest), axis=-1)
    remote_index = (position - 1 - shard_of) * REMOTE_BLOCK_MAX + jnp.where(is_lowest, 0, 1)
    units = list_units(
        jnp.stack([local & (by_item != own[:, None]), ~local]),
        jnp.stack([by_item - base, remote_index]),
        units_max,
    )
    sizes = dict(
        blocks=blocks, used=used, block_len=block_len, scale=scale, units_max=units_max,
        at_once=at_once,
    )
    states = local_part(units[0], first, query_rows, key_rows, value_rows, clear, **sizes)
    out = remote_part(units[1], states, arrived, query_rows.shape, **sizes)
    return out.reshape(tokens, query_heads, head_dim)


def solution(mesh):
    return jax.shard_map(
        on_device,
        mesh=mesh,
        in_specs=(
            P(("groups", "ctx"), ("heads", "rep"), None),
            P(("groups", "ctx"), "heads", None),
            P(("groups", "ctx"), "heads", None),
            P("heads", ("groups", "ctx"), None),
        ),
        out_specs=P(("groups", "ctx"), ("heads", "rep"), None),
        check_vma=False,
    )
```

time: 74.3 us -> 66.8 us (0.90)
  Pallas kernels: 55.9 us -> 50.6 us
  local copies, waits for them, and re-layouts: 3.86 us -> 2.02 us
  starting transfers between devices: 11.4 us -> 10.2 us
  waiting for transfers between devices: 0.02 us -> 1.22 us
    pallas_call x1, Pallas kernels: 34.4 us -> 29.1 us  [local_part(): pl.pallas_call(functools.partial(local_kernel, kv_heads=kv_heads, **sizes...]
    ppermute x3, starting transfers between devices: 7.14 us -> 4.8 us  [on_device(): lax.ppermute(parcel, 'ctx', [(i, i + d) for i in range(shards - d)])]
    ppermute x3, waiting for transfers between devices: 0.01 us -> 1.21 us  [on_device(): lax.ppermute(lists, 'ctx', [(j, j - d) for j in range(d, shards)])]
    ppermute x3, starting transfers between devices: 4.3 us -> 5.45 us  [on_device(): lax.ppermute(lists, 'ctx', [(j, j - d) for j in range(d, shards)])]
    select_n x1 -> x3, other arithmetic: 0.01 us -> 0.8 us  [the longest x2 0.73 us: on_device(): shard_of = by_item // blocks]
  transfers between devices with their start and end apart: 6 -> 6, of which waited for: 0 -> 1; matrix products, arithmetic and copies ran while one was open for 5% -> 3% of each run, Pallas kernels for 46% -> 44%
where the time goes in v5:
time: 66.8 us; the launch traced here: 66.4 us
  Pallas kernels  50.6 us (76%)
  starting transfers between devices  10.2 us (15%)
  other arithmetic  2.14 us (3%)
  local copies, waits for them, and re-layouts  2.02 us (3%)
  waiting for transfers between devices  1.22 us (2%)
    pallas_call x1, Pallas kernels, local_part(): pl.pallas_call(functools.partial(local_kernel, kv_heads=kv_heads, **sizes...  29.1 us
    pallas_call x1, Pallas kernels, remote_part(): pl.pallas_call(functools.partial(remote_kernel, shifts=shifts, **sizes),...  17.1 us
    ppermute x3, starting transfers between devices, on_device(): lax.ppermute(lists, 'ctx', [(j, j - d) for j in range(d, shards)])  5.45 us
    ppermute x3, starting transfers between devices, on_device(): lax.ppermute(parcel, 'ctx', [(i, i + d) for i in range(shards - d)])  4.8 us
    pallas_call x1, Pallas kernels, pack(): pl.pallas_call(functools.partial(pack_kernel, shifts=shifts, used=used, k...  4.38 us
  transfers between devices with their start and end apart: 6, of which 1 were waited for; matrix products, arithmetic and copies ran while one was open for 3% of the time, Pallas kernels for 44%

profile of v5, /device:TPU:18, one launch (start us, length us, event | category | flops | bytes accessed | tf_op | source)
XLA Modules:
  0.0 66.4 jit_solution(125180348674129682)
XLA Ops:
  0.0 0.7 %add_select_fusion = (s32[24,2,8]{0,2,1:T(8,128)S(1)}, s32[2,24,8]{1,2,0:T(8,128)S(1)}) fusion(s32[4,24,8]{1,2,0:T(8,128)} %param.7, s32[]{:T(128)S(6)} %select_n.84), kind=kLoop, calls=%fused_computation.17 | loop fusion | flops 3072 | bytes 4612 | tf_op jit(solution)/shard_map/jit(floor_divide)/jit(_where)/select_n | solution.py:524
  0.7 0.7 collective-permute-start.2
  1.4 2.9 %collective-permute-start.1 = (s32[2,24,8]{1,2,0:T(8,128)S(1)}, s32[2,24,8]{1,2,0:T(8,128)S(1)}, u32[]{:S(2)}, u32[]{:S(2)}) collective-permute-start(s32[2,24,8]{1,2,0:T(8,128)S(1)} %get-tuple-element.26), channel_id=1, source_target_pairs={{8,0},{12,4},{9,1},{13,5},{10,2},{14,6},{11,3},{15,7},{24,16},{28,... | collective-permute-start | bytes 4616 | tf_op jit(solution)/shard_map/ppermute | solution.py:494
  4.2 1.9 %collective-permute-start = (s32[2,24,8]{1,2,0:T(8,128)S(1)}, s32[2,24,8]{1,2,0:T(8,128)S(1)}, u32[]{:S(2)}, u32[]{:S(2)}) collective-permute-start(s32[2,24,8]{1,2,0:T(8,128)S(1)} %get-tuple-element.26), channel_id=1, source_target_pairs={{4,0},{8,4},{12,8},{5,1},{9,5},{13,9},{6,2},{10,6},{14,10},{7,3},{... | collective-permute-start | bytes 4616 | tf_op jit(solution)/shard_map/ppermute | solution.py:494
  6.4 0.2 select_reduce_fusion.3
  6.8 0.1 add.92
  7.2 0.1 select_reduce_fusion.2
  7.3 0.1 convert_reduce_fusion.2
  7.4 0.1 copy.78
  7.6 0.1 gt.17
  7.8 0.1 shift_left.28
  8.0 0.1 reduce_sum.61
  8.1 0.1 convert_reduce_fusion
  8.3 0.2 select_reduce_fusion
  8.6 1.2 %collective-permute-done = s32[2,24,8]{1,2,0:T(8,128)S(1)} collective-permute-done((s32[2,24,8]{1,2,0:T(8,128)S(1)}, s32[2,24,8]{1,2,0:T(8,128)S(1)}, u32[]{:S(2)}, u32[]{:S(2)}) %collective-permute-start) | collective-permute-done | bytes 1568 | tf_op jit(solution)/shard_map/ppermute | solution.py:494
  9.8 0.3 select_reduce_fusion.5
  10.3 0.1 copy.83
  10.4 0.6 reshape.284.request
  11.0 4.4 %pack.1 = (bf16[2,2,256,128]{3,2,1,0:T(8,128)(2,1)}, bf16[2,2,256,128]{3,2,1,0:T(8,128)(2,1)}, bf16[2,2,256,128]{3,2,1,0:T(8,128)(2,1)}, f32[8,128]{1,0:T(8,128)S(1)}) custom-call(s32[12]{0:T(128)} %reshape.284.request, bf16[12288,128]{1,0:T(8,128)(2,1)} %bitcast.21, bf16[12288,128]{1,0:T(8,128)(2,1)} %bitcast.23, s32[1]{0:T(128)} %bitcast.7.rest_0_.first_ref), custom_call_target="tpu_custom_call" | custom-call | tf_op jit(solution)/shard_map/pack/pallas_call | solution.py:72
  15.4 2.8 %collective-permute-start.3 = (bf16[2,2,256,128]{3,2,1,0:T(8,128)(2,1)}, bf16[2,2,256,128]{3,2,1,0:T(8,128)(2,1)S(1)}, u32[]{:S(2)}, u32[]{:S(2)}) collective-permute-start(bf16[2,2,256,128]{3,2,1,0:T(8,128)(2,1)} %get-tuple-element.16), channel_id=1, source_target_pairs={{0,4},{4,8},{8,12},{1,5},{5,9},{9,13},{2,6},{6,10},{10,14},{3,7},{... | collective-permute-start | bytes 786440 | tf_op jit(solution)/shard_map/ppermute | solution.py:517
  18.2 1.3 %collective-permute-start.4 = (bf16[2,2,256,128]{3,2,1,0:T(8,128)(2,1)}, bf16[2,2,256,128]{3,2,1,0:T(8,128)(2,1)S(1)}, u32[]{:S(2)}, u32[]{:S(2)}) collective-permute-start(bf16[2,2,256,128]{3,2,1,0:T(8,128)(2,1)} %get-tuple-element.17), channel_id=1, source_target_pairs={{0,8},{4,12},{1,9},{5,13},{2,10},{6,14},{3,11},{7,15},{16,24},{20,... | collective-permute-start | bytes 786440 | tf_op jit(solution)/shard_map/ppermute | solution.py:517
  19.5 0.7 %collective-permute-start.5 = (bf16[2,2,256,128]{3,2,1,0:T(8,128)(2,1)}, bf16[2,2,256,128]{3,2,1,0:T(8,128)(2,1)S(1)}, u32[]{:S(2)}, u32[]{:S(2)}) collective-permute-start(bf16[2,2,256,128]{3,2,1,0:T(8,128)(2,1)} %get-tuple-element.18), channel_id=1, source_target_pairs={{0,12},{1,13},{2,14},{3,15},{16,28},{17,29},{18,30},{19,31}} | collective-permute-start | bytes 786440 | tf_op jit(solution)/shard_map/ppermute | solution.py:517
  20.2 29.1 %local_part.1 = (f32[48,144,512]{2,1,0:T(8,128)S(1)}, f32[48,8,512]{2,1,0:T(8,128)S(1)}, bf16[48,512,256]{2,1,0:T(8,128)(2,1)S(1)}) custom-call(s32[193]{0:T(256)S(1)} %bitcast.20, s32[1]{0:T(128)} %bitcast.7.rest_0_.first_ref, bf16[24576,128]{1,0:T(8,128)(2,1)} %bitcast.35, bf16[12288,128]{1,0:T(8,128)(2,1)} %bitcast.22, bf16[12288,128]{1,0:T(8,128)(2,1)} %bitcast.24, ...), custom_call_target="tpu_custom_call" | custom-call | flops 17179869184 | bytes 33554432 | tf_op jit(solution)/shard_map/local_part/pallas_call | solution.py:384
  49.4 17.1 %remote_part.1 = bf16[24576,128]{1,0:T(8,128)(2,1)} custom-call(s32[193]{0:T(256)S(1)} %bitcast.19, bf16[48,512,256]{2,1,0:T(8,128)(2,1)S(1)} %get-tuple-element.13.split_ref, f32[48,144,512]{2,1,0:T(8,128)S(1)} %get-tuple-element.14.sums_in, f32[48,8,512]{2,1,0:T(8,128)S(1)} %get-tuple-element.15.highest_ref, ...), custom_call_target="tpu_custom_call" | custom-call | tf_op jit(solution)/shard_map/remote_part/pallas_call | solution.py:428
  (32 shorter events, 1.1 us)
Async XLA Ops:
  0.7 7.9 %collective-permute-start.2 = (s32[2,24,8]{1,2,0:T(8,128)S(1)}, s32[2,24,8]{1,2,0:T(8,128)S(1)}, u32[]{:S(2)}, u32[]{:S(2)}) collective-permute-start(s32[2,24,8]{1,2,0:T(8,128)S(1)} %get-tuple-element.26), channel_id=1, source_target_pairs={{12,0},{13,1},{14,2},{15,3},{28,16},{29,17},{30,18},{31,19}} | collective-permute-start | bytes 4616 | tf_op jit(solution)/shard_map/ppermute | solution.py:494
  1.4 7.2 %collective-permute-start.1 = (s32[2,24,8]{1,2,0:T(8,128)S(1)}, s32[2,24,8]{1,2,0:T(8,128)S(1)}, u32[]{:S(2)}, u32[]{:S(2)}) collective-permute-start(s32[2,24,8]{1,2,0:T(8,128)S(1)} %get-tuple-element.26), channel_id=1, source_target_pairs={{8,0},{12,4},{9,1},{13,5},{10,2},{14,6},{11,3},{15,7},{24,16},{28,... | collective-permute-start | bytes 4616 | tf_op jit(solution)/shard_map/ppermute | solution.py:494
  4.2 5.5 %collective-permute-start = (s32[2,24,8]{1,2,0:T(8,128)S(1)}, s32[2,24,8]{1,2,0:T(8,128)S(1)}, u32[]{:S(2)}, u32[]{:S(2)}) collective-permute-start(s32[2,24,8]{1,2,0:T(8,128)S(1)} %get-tuple-element.26), channel_id=1, source_target_pairs={{4,0},{8,4},{12,8},{5,1},{9,5},{13,9},{6,2},{10,6},{14,10},{7,3},{... | collective-permute-start | bytes 4616 | tf_op jit(solution)/shard_map/ppermute | solution.py:494
  15.4 34.0 %collective-permute-start.3 = (bf16[2,2,256,128]{3,2,1,0:T(8,128)(2,1)}, bf16[2,2,256,128]{3,2,1,0:T(8,128)(2,1)S(1)}, u32[]{:S(2)}, u32[]{:S(2)}) collective-permute-start(bf16[2,2,256,128]{3,2,1,0:T(8,128)(2,1)} %get-tuple-element.16), channel_id=1, source_target_pairs={{0,4},{4,8},{8,12},{1,5},{5,9},{9,13},{2,6},{6,10},{10,14},{3,7},{... | collective-permute-start | bytes 786440 | tf_op jit(solution)/shard_map/ppermute | solution.py:517
  18.2 31.1 %collective-permute-start.4 = (bf16[2,2,256,128]{3,2,1,0:T(8,128)(2,1)}, bf16[2,2,256,128]{3,2,1,0:T(8,128)(2,1)S(1)}, u32[]{:S(2)}, u32[]{:S(2)}) collective-permute-start(bf16[2,2,256,128]{3,2,1,0:T(8,128)(2,1)} %get-tuple-element.17), channel_id=1, source_target_pairs={{0,8},{4,12},{1,9},{5,13},{2,10},{6,14},{3,11},{7,15},{16,24},{20,... | collective-permute-start | bytes 786440 | tf_op jit(solution)/shard_map/ppermute | solution.py:517
  19.5 29.8 %collective-permute-start.5 = (bf16[2,2,256,128]{3,2,1,0:T(8,128)(2,1)}, bf16[2,2,256,128]{3,2,1,0:T(8,128)(2,1)S(1)}, u32[]{:S(2)}, u32[]{:S(2)}) collective-permute-start(bf16[2,2,256,128]{3,2,1,0:T(8,128)(2,1)} %get-tuple-element.18), channel_id=1, source_target_pairs={{0,12},{1,13},{2,14},{3,15},{16,28},{17,29},{18,30},{19,31}} | collective-permute-start | bytes 786440 | tf_op jit(solution)/shard_map/ppermute | solution.py:517

commit v6 on v5

--- a/solution.py
+++ b/solution.py
@@ -130,19 +130,9 @@
     return jnp.where(key <= token, 0.0, MASKED)
 
 
-def two_parts(values):
-    high = values.astype(jnp.bfloat16)
-    low = (values - high.astype(jnp.float32)).astype(jnp.bfloat16)
-    return jnp.concatenate([high, low], axis=-1)
-
-
-def doubled(key_rows):
-    return jnp.concatenate([key_rows, key_rows], axis=-1)
-
-
 def attend_units(
     units_ref, queries_ref, keys_ref, values_ref, highest_ref, sums_ref,
-    *, used, block_len, units_max,
+    *, used, block_len, scale, units_max,
 ):
     def read(unit):
         code = units_ref[unit]
@@ -156,14 +146,15 @@
     def scores_of(unit):
         item, *slots = unit
         rows = jnp.concatenate([rows_of(keys_ref, item, slot) for slot in slots], axis=0)
-        return score(doubled(rows), queries_ref[item])
+        return score(rows, queries_ref[item])
 
     def weigh(unit, scores, highest):
         item, *slots = unit
         parts = []
         for turn, slot in enumerate(slots):
             shift = jnp.where(slot < 0, CLOSED, highest)
-            parts.append(jnp.exp2(scores[turn * block_len : (turn + 1) * block_len] - shift))
+            part = scores[turn * block_len : (turn + 1) * block_len]
+            parts.append(jnp.exp2(part * scale - shift))
         weights = jnp.concatenate(parts, axis=0).astype(jnp.bfloat16)
         columns = jnp.concatenate([rows_of(values_ref, item, slot) for slot in slots], axis=1)
         return jnp.dot(columns, weights, preferred_element_type=jnp.float32)
@@ -189,7 +180,7 @@
             scores = scores_of(unit)
             for place, slot in enumerate(unit[1:]):
                 part = scores[place * block_len : (place + 1) * block_len]
-                found = jnp.max(part, axis=0, keepdims=True)
+                found = jnp.max(part, axis=0, keepdims=True) * scale
                 highest = jnp.where(slot < 0, highest, jnp.maximum(highest, found))
             return highest
 
@@ -241,10 +232,10 @@
 
     def own_scores(item, block, query):
         here = key_table[lax.rem(item, used), block_rows(block, block_len), :]
-        return score(doubled(here), query) + mask_ref[...]
+        return score(here, query) + mask_ref[...]
 
     def own_sum(item, block, scores, highest):
-        weights = jnp.exp2(scores - highest).astype(jnp.bfloat16)
+        weights = jnp.exp2(scores * scale - highest).astype(jnp.bfloat16)
         columns = value_table[lax.rem(item, used), block_rows(block, height), :]
         return jnp.dot(columns, weights, preferred_element_type=jnp.float32)
 
@@ -266,13 +257,13 @@
                 )
                 key_table[head, block_rows(block, block_len), :] = key_rows
                 value_table[head, block_rows(block, height), :] = columns
-                query = two_parts(query * scale)
+                query = query.astype(jnp.bfloat16)
                 split_ref[block * used + head] = query
                 todo.append((block * used + head, query, key_rows, columns))
-        scores = [score(doubled(k), query) + mask_ref[...] for _, query, k, _ in todo]
+        scores = [score(k, query) + mask_ref[...] for _, query, k, _ in todo]
         for (item, _, _, columns), its_scores in zip(todo, scores):
-            highest = jnp.max(its_scores, axis=0, keepdims=True)
-            weights = jnp.exp2(its_scores - highest).astype(jnp.bfloat16)
+            highest = jnp.max(its_scores, axis=0, keepdims=True) * scale
+            weights = jnp.exp2(its_scores * scale - highest).astype(jnp.bfloat16)
             highest_ref[item] = jnp.broadcast_to(highest, highest_ref.shape[1:])
             sums_ref[item] = jnp.dot(columns, weights, preferred_element_type=jnp.float32)
         return carry
@@ -280,7 +271,7 @@
     lax.fori_loop(0, blocks // at_once, chunk, 0)
     raise_highest, add_again = attend_units(
         units_ref, split_ref, key_table, value_table, highest_ref, sums_ref,
-        used=used, block_len=block_len, units_max=units_max,
+        used=used, block_len=block_len, scale=scale, units_max=units_max,
     )
 
     @pl.when(unsafe(sums_ref, head_dim))
@@ -299,7 +290,7 @@
 
 def remote_kernel(
     units_ref, split_ref, sums_in, highest_ref, *rest,
-    shifts, blocks, used, block_len, units_max, at_once,
+    shifts, blocks, used, block_len, scale, units_max, at_once,
 ):
     parcels, (out_ref, key_table, value_table, sums_ref, staged, sems) = (
         rest[:shifts], rest[shifts:]
@@ -327,7 +318,7 @@
     lax.fori_loop(0, blocks * used, take, 0)
     raise_highest, add_again = attend_units(
         units_ref, split_ref, key_table, value_table, highest_ref, sums_ref,
-        used=used, block_len=block_len, units_max=units_max,
+        used=used, block_len=block_len, scale=scale, units_max=units_max,
     )
 
     @pl.when(unsafe(sums_ref, head_dim))
@@ -403,7 +394,7 @@
         out_shape=[
             pltpu.VMEM((blocks * used, height, item_rows), jnp.float32),
             pltpu.VMEM((blocks * used, 8, item_rows), jnp.float32),
-            pltpu.VMEM((blocks * used, item_rows, 2 * head_dim), jnp.bfloat16),
+            pltpu.VMEM((blocks * used, item_rows, head_dim), jnp.bfloat16),
         ],
         compiler_params=pltpu.CompilerParams(vmem_limit_bytes=LOCAL_VMEM_BYTES),
         cost_estimate=pl.CostEstimate(
@@ -424,7 +415,6 @@
     height = sums.shape[1]
     head_dim = out_shape[1]
     slots = shifts * REMOTE_BLOCK_MAX
-    sizes.pop("scale")
     return pl.pallas_call(
         functools.partial(remote_kernel, shifts=shifts, **sizes),
         grid_spec=pltpu.PrefetchScalarGridSpec(
@@ -485,16 +475,18 @@
     first = lax.axis_index("rep") * query_heads // GROUP
     scale = LOG2E * head_dim**-0.5
     at_once = next(n for n in (3, 2, 1) if blocks % n == 0)
+    given_at_once = next(n for n in (6, 4, 3, 2, 1) if blocks % n == 0)
     units_max = blocks * used * ((picks + 1) // 2)
     units_max = -(-units_max // UNITS_AT_ONCE) * UNITS_AT_ONCE
 
     lists = lax.dynamic_slice_in_dim(chosen, first, used, 0)
     wanted = jnp.stack(
         [
-            lax.ppermute(lists, "ctx", [(j, j - d) for j in range(d, shards)])
+            lax.ppermute(chosen, "ctx", [(j, j - d) for j in range(d, shards)])
             for d in range(1, shards)
         ]
     )
+    wanted = lax.dynamic_slice_in_dim(wanted, first, used, 1)
     within = wanted - base
     mine = (within >= 0) & (within < blocks)
     request = jnp.stack(
@@ -537,11 +529,10 @@
         units_max,
     )
     sizes = dict(
-        blocks=blocks, used=used, block_len=block_len, scale=scale, units_max=units_max,
-        at_once=at_once,
-    )
-    states = local_part(units[0], first, query_rows, key_rows, value_rows, clear, **sizes)
-    out = remote_part(units[1], states, arrived, query_rows.shape, **sizes)
+        blocks=blocks, used=used, block_len=block_len, scale=scale, units_max=units_max
+    )
+    states = local_part(units[0], first, query_rows, key_rows, value_rows, clear, at_once=at_once, **sizes)
+    out = remote_part(units[1], states, arrived, query_rows.shape, at_once=given_at_once, **sizes)
     return out.reshape(tokens, query_heads, head_dim)
 
 

time: 66.8 us -> 64.1 us (0.960)
  the two profiles are of different devices: /device:TPU:18 before, /device:TPU:0 now
where the time goes in v6:
time: 64.1 us; the launch traced here: 63.9 us
  Pallas kernels  43.6 us (68%)
  starting transfers between devices  12.2 us (19%)
  waiting for transfers between devices  3.59 us (6%)
  other arithmetic  2.14 us (3%)
  local copies, waits for them, and re-layouts  2.01 us (3%)
    pallas_call x1, Pallas kernels, local_part(): pl.pallas_call(functools.partial(local_kernel, kv_heads=kv_heads, **sizes...  33 us
    ppermute x3, starting transfers between devices, on_device(): lax.ppermute(parcel, 'ctx', [(i, i + d) for i in range(shards - d)])  8.36 us
    pallas_call x1, Pallas kernels, remote_part(): pl.pallas_call(functools.partial(remote_kernel, shifts=shifts, **sizes),...  6.21 us
    pallas_call x1, Pallas kernels, pack(): pl.pallas_call(functools.partial(pack_kernel, shifts=shifts, used=used, k...  4.38 us
    ppermute x3, starting transfers between devices, on_device(): lax.ppermute(chosen, 'ctx', [(j, j - d) for j in range(d, shards)])  3.86 us
    ppermute x3, waiting for transfers between devices, on_device(): lax.ppermute(chosen, 'ctx', [(j, j - d) for j in range(d, shards)])  3.59 us
  transfers between devices with their start and end apart: 6, of which 1 were waited for; matrix products, arithmetic and copies ran while one was open for 5% of the time, Pallas kernels for 52%

profile of v6, /device:TPU:0, one launch (start us, length us, event | category | flops | bytes accessed | tf_op | source)
XLA Modules:
  0.0 63.9 jit_solution(1197387527231905529)
XLA Ops:
  0.0 1.3 %collective-permute-start = (s32[4,24,8]{1,2,0:T(8,128)}, s32[4,24,8]{1,2,0:T(8,128)S(1)}, u32[]{:S(2)}, u32[]{:S(2)}) collective-permute-start(s32[4,24,8]{1,2,0:T(8,128)} %param.7), channel_id=1, source_target_pairs={{4,0},{8,4},{12,8},{5,1},{9,5},{13,9},{6,2},{10,6},{14,10},{7,3},{... | collective-permute-start | bytes 9224 | tf_op jit(solution)/shard_map/ppermute | solution.py:485
  1.3 1.3 %collective-permute-start.2 = (s32[4,24,8]{1,2,0:T(8,128)}, s32[4,24,8]{1,2,0:T(8,128)S(1)}, u32[]{:S(2)}, u32[]{:S(2)}) collective-permute-start(s32[4,24,8]{1,2,0:T(8,128)} %param.7), channel_id=1, source_target_pairs={{12,0},{13,1},{14,2},{15,3},{28,16},{29,17},{30,18},{31,19}} | collective-permute-start | bytes 9224 | tf_op jit(solution)/shard_map/ppermute | solution.py:485
  2.6 1.3 %collective-permute-start.1 = (s32[4,24,8]{1,2,0:T(8,128)}, s32[4,24,8]{1,2,0:T(8,128)S(1)}, u32[]{:S(2)}, u32[]{:S(2)}) collective-permute-start(s32[4,24,8]{1,2,0:T(8,128)} %param.7), channel_id=1, source_target_pairs={{8,0},{12,4},{9,1},{13,5},{10,2},{14,6},{11,3},{15,7},{24,16},{28,... | collective-permute-start | bytes 9224 | tf_op jit(solution)/shard_map/ppermute | solution.py:485
  4.0 0.7 %add_select_fusion = (s32[24,2,8]{0,2,1:T(8,128)S(1)}, s32[24,2,8]{0,2,1:T(8,128)S(1)}) fusion(s32[4,24,8]{1,2,0:T(8,128)} %param.7, s32[]{:T(128)S(6)} %select_n.85), kind=kLoop, calls=%fused_computation.22 | loop fusion | flops 3072 | bytes 4612 | tf_op jit(solution)/shard_map/jit(floor_divide)/jit(_where)/select_n | solution.py:516
  4.8 0.2 select_reduce_fusion.3
  5.5 0.1 select_reduce_fusion.2
  5.6 0.1 convert_reduce_fusion.2
  5.7 0.1 copy.78
  5.8 0.1 gt.17
  6.0 0.1 add.93
  6.2 0.1 shift_left.28
  6.5 0.1 reduce_sum.61
  6.6 0.1 convert_reduce_fusion
  6.7 0.2 select_reduce_fusion
  7.0 3.6 %collective-permute-done.2 = s32[4,24,8]{1,2,0:T(8,128)S(1)} collective-permute-done((s32[4,24,8]{1,2,0:T(8,128)}, s32[4,24,8]{1,2,0:T(8,128)S(1)}, u32[]{:S(2)}, u32[]{:S(2)}) %collective-permute-start.2) | collective-permute-done | bytes 3104 | tf_op jit(solution)/shard_map/ppermute | solution.py:485
  10.6 0.3 select_reduce_fusion.5
  11.1 0.1 copy.83
  11.2 0.6 reshape.284.request
  11.8 4.4 %pack.1 = (bf16[2,2,256,128]{3,2,1,0:T(8,128)(2,1)}, bf16[2,2,256,128]{3,2,1,0:T(8,128)(2,1)}, bf16[2,2,256,128]{3,2,1,0:T(8,128)(2,1)}, f32[8,128]{1,0:T(8,128)S(1)}) custom-call(s32[12]{0:T(128)} %reshape.284.request, bf16[12288,128]{1,0:T(8,128)(2,1)} %bitcast.22, bf16[12288,128]{1,0:T(8,128)(2,1)} %bitcast.24, s32[1]{0:T(128)} %bitcast.7.rest_0_.first_ref), custom_call_target="tpu_custom_call" | custom-call | tf_op jit(solution)/shard_map/pack/pallas_call | solution.py:72
  16.2 3.8 %collective-permute-start.3 = (bf16[2,2,256,128]{3,2,1,0:T(8,128)(2,1)}, bf16[2,2,256,128]{3,2,1,0:T(8,128)(2,1)S(1)}, u32[]{:S(2)}, u32[]{:S(2)}) collective-permute-start(bf16[2,2,256,128]{3,2,1,0:T(8,128)(2,1)} %get-tuple-element.16), channel_id=1, source_target_pairs={{0,4},{4,8},{8,12},{1,5},{5,9},{9,13},{2,6},{6,10},{10,14},{3,7},{... | collective-permute-start | bytes 786440 | tf_op jit(solution)/shard_map/ppermute | solution.py:509
  20.0 3.3 %collective-permute-start.4 = (bf16[2,2,256,128]{3,2,1,0:T(8,128)(2,1)}, bf16[2,2,256,128]{3,2,1,0:T(8,128)(2,1)S(1)}, u32[]{:S(2)}, u32[]{:S(2)}) collective-permute-start(bf16[2,2,256,128]{3,2,1,0:T(8,128)(2,1)} %get-tuple-element.17), channel_id=1, source_target_pairs={{0,8},{4,12},{1,9},{5,13},{2,10},{6,14},{3,11},{7,15},{16,24},{20,... | collective-permute-start | bytes 786440 | tf_op jit(solution)/shard_map/ppermute | solution.py:509
  23.3 1.3 %collective-permute-start.5 = (bf16[2,2,256,128]{3,2,1,0:T(8,128)(2,1)}, bf16[2,2,256,128]{3,2,1,0:T(8,128)(2,1)S(1)}, u32[]{:S(2)}, u32[]{:S(2)}) collective-permute-start(bf16[2,2,256,128]{3,2,1,0:T(8,128)(2,1)} %get-tuple-element.18), channel_id=1, source_target_pairs={{0,12},{1,13},{2,14},{3,15},{16,28},{17,29},{18,30},{19,31}} | collective-permute-start | bytes 786440 | tf_op jit(solution)/shard_map/ppermute | solution.py:509
  24.6 33.0 %local_part.1 = (f32[48,144,512]{2,1,0:T(8,128)S(1)}, f32[48,8,512]{2,1,0:T(8,128)S(1)}, bf16[48,512,128]{2,1,0:T(8,128)(2,1)S(1)}) custom-call(s32[193]{0:T(256)S(1)} %bitcast.21, s32[1]{0:T(128)} %bitcast.7.rest_0_.first_ref, bf16[24576,128]{1,0:T(8,128)(2,1)} %bitcast.34, bf16[12288,128]{1,0:T(8,128)(2,1)} %bitcast.23, bf16[12288,128]{1,0:T(8,128)(2,1)} %bitcast.25, ...), custom_call_target="tpu_custom_call" | custom-call | flops 17179869184 | bytes 33554432 | tf_op jit(solution)/shard_map/local_part/pallas_call | solution.py:375
  57.6 6.2 %remote_part.1 = bf16[24576,128]{1,0:T(8,128)(2,1)} custom-call(s32[193]{0:T(256)S(1)} %bitcast.20, bf16[48,512,128]{2,1,0:T(8,128)(2,1)S(1)} %get-tuple-element.13.split_ref, f32[48,144,512]{2,1,0:T(8,128)S(1)} %get-tuple-element.14.sums_in, f32[48,8,512]{2,1,0:T(8,128)S(1)} %get-tuple-element.15.highest_ref, ...), custom_call_target="tpu_custom_call" | custom-call | tf_op jit(solution)/shard_map/remote_part/pallas_call | solution.py:418
  (32 shorter events, 1.0 us)
Async XLA Ops:
  0.0 7.0 %collective-permute-start = (s32[4,24,8]{1,2,0:T(8,128)}, s32[4,24,8]{1,2,0:T(8,128)S(1)}, u32[]{:S(2)}, u32[]{:S(2)}) collective-permute-start(s32[4,24,8]{1,2,0:T(8,128)} %param.7), channel_id=1, source_target_pairs={{4,0},{8,4},{12,8},{5,1},{9,5},{13,9},{6,2},{10,6},{14,10},{7,3},{... | collective-permute-start | bytes 9224 | tf_op jit(solution)/shard_map/ppermute | solution.py:485
  1.3 9.3 %collective-permute-start.2 = (s32[4,24,8]{1,2,0:T(8,128)}, s32[4,24,8]{1,2,0:T(8,128)S(1)}, u32[]{:S(2)}, u32[]{:S(2)}) collective-permute-start(s32[4,24,8]{1,2,0:T(8,128)} %param.7), channel_id=1, source_target_pairs={{12,0},{13,1},{14,2},{15,3},{28,16},{29,17},{30,18},{31,19}} | collective-permute-start | bytes 9224 | tf_op jit(solution)/shard_map/ppermute | solution.py:485
  2.6 8.0 %collective-permute-start.1 = (s32[4,24,8]{1,2,0:T(8,128)}, s32[4,24,8]{1,2,0:T(8,128)S(1)}, u32[]{:S(2)}, u32[]{:S(2)}) collective-permute-start(s32[4,24,8]{1,2,0:T(8,128)} %param.7), channel_id=1, source_target_pairs={{8,0},{12,4},{9,1},{13,5},{10,2},{14,6},{11,3},{15,7},{24,16},{28,... | collective-permute-start | bytes 9224 | tf_op jit(solution)/shard_map/ppermute | solution.py:485
  16.2 41.4 %collective-permute-start.3 = (bf16[2,2,256,128]{3,2,1,0:T(8,128)(2,1)}, bf16[2,2,256,128]{3,2,1,0:T(8,128)(2,1)S(1)}, u32[]{:S(2)}, u32[]{:S(2)}) collective-permute-start(bf16[2,2,256,128]{3,2,1,0:T(8,128)(2,1)} %get-tuple-element.16), channel_id=1, source_target_pairs={{0,4},{4,8},{8,12},{1,5},{5,9},{9,13},{2,6},{6,10},{10,14},{3,7},{... | collective-permute-start | bytes 786440 | tf_op jit(solution)/shard_map/ppermute | solution.py:509
  20.0 37.7 %collective-permute-start.4 = (bf16[2,2,256,128]{3,2,1,0:T(8,128)(2,1)}, bf16[2,2,256,128]{3,2,1,0:T(8,128)(2,1)S(1)}, u32[]{:S(2)}, u32[]{:S(2)}) collective-permute-start(bf16[2,2,256,128]{3,2,1,0:T(8,128)(2,1)} %get-tuple-element.17), channel_id=1, source_target_pairs={{0,8},{4,12},{1,9},{5,13},{2,10},{6,14},{3,11},{7,15},{16,24},{20,... | collective-permute-start | bytes 786440 | tf_op jit(solution)/shard_map/ppermute | solution.py:509
  23.3 34.4 %collective-permute-start.5 = (bf16[2,2,256,128]{3,2,1,0:T(8,128)(2,1)}, bf16[2,2,256,128]{3,2,1,0:T(8,128)(2,1)S(1)}, u32[]{:S(2)}, u32[]{:S(2)}) collective-permute-start(bf16[2,2,256,128]{3,2,1,0:T(8,128)(2,1)} %get-tuple-element.18), channel_id=1, source_target_pairs={{0,12},{1,13},{2,14},{3,15},{16,28},{17,29},{18,30},{19,31}} | collective-permute-start | bytes 786440 | tf_op jit(solution)/shard_map/ppermute | solution.py:509

commit v7 on v6

--- a/solution.py
+++ b/solution.py
@@ -18,8 +18,9 @@
 VMEM_BYTES = 60 * 2**20
 LOCAL_VMEM_BYTES = 22 * 2**20
 REMOTE_VMEM_BYTES = 22 * 2**20
-UNITS_AT_ONCE = 8
-FIELD = 10
+UNIT_KINDS = ((4, 4), (2, 4))
+WIDEST = 4
+FIELD = 6
 ONES_ROWS = 16
 
 
@@ -77,15 +78,14 @@
             num_scalar_prefetch=1,
             grid=(1,),
             in_specs=[anywhere, anywhere, pl.BlockSpec(memory_space=pltpu.SMEM)],
-            out_specs=[pl.BlockSpec(parcel, lambda g, *_: (0, 0, 0, 0))] * shifts
-            + [pl.BlockSpec(memory_space=pltpu.VMEM)],
+            out_specs=[pl.BlockSpec(memory_space=pltpu.VMEM)] * (shifts + 1),
             scratch_shapes=[
                 pltpu.VMEM((count, rows, head_dim), jnp.bfloat16),
                 pltpu.VMEM((count, rows, head_dim), jnp.float32),
                 pltpu.SemaphoreType.DMA((count,)),
             ],
         ),
-        out_shape=[jax.ShapeDtypeStruct(parcel, jnp.bfloat16)] * shifts
+        out_shape=[pltpu.VMEM(parcel, jnp.bfloat16)] * shifts
         + [pltpu.VMEM(row_shape, jnp.float32)],
         compiler_params=pltpu.CompilerParams(vmem_limit_bytes=VMEM_BYTES),
         name="pack",
@@ -134,10 +134,11 @@
     units_ref, queries_ref, keys_ref, values_ref, highest_ref, sums_ref,
     *, used, block_len, scale, units_max,
 ):
-    def read(unit):
-        code = units_ref[unit]
+    def read(base, unit, width):
+        code = units_ref[base + unit]
         mask = (1 << FIELD) - 1
-        return code >> (2 * FIELD), ((code >> FIELD) & mask) - 1, (code & mask) - 1
+        slots = [((code >> ((WIDEST - 1 - n) * FIELD)) & mask) - 1 for n in range(width)]
+        return code >> (WIDEST * FIELD), *slots
 
     def rows_of(ref, item, slot):
         height = ref.shape[1] // (keys_ref.shape[1] // block_len)
@@ -159,40 +160,46 @@
         columns = jnp.concatenate([rows_of(values_ref, item, slot) for slot in slots], axis=1)
         return jnp.dot(columns, weights, preferred_element_type=jnp.float32)
 
-    count = units_ref[units_max]
-
-    def some(turn, carry):
-        units = [read(turn * UNITS_AT_ONCE + n) for n in range(UNITS_AT_ONCE)]
-        scores = [scores_of(unit) for unit in units]
-        for unit, its_scores in zip(units, scores):
-            sums_ref[unit[0]] += weigh(unit, its_scores, highest_ref[unit[0], :1, :])
-        return carry
-
-    lax.fori_loop(0, (count + UNITS_AT_ONCE - 1) // UNITS_AT_ONCE, some, 0)
-
-    def only(unit, item):
-        its, first, second = read(unit)
-        return item, jnp.where(its == item, first, -1), jnp.where(its == item, second, -1)
+    lists = [(kind * (units_max + 1), *sizes) for kind, sizes in enumerate(UNIT_KINDS)]
+    for base, width, at_once in lists:
+
+        def some(turn, carry, base=base, width=width, at_once=at_once):
+            units = [read(base, turn * at_once + n, width) for n in range(at_once)]
+            scores = [scores_of(unit) for unit in units]
+            for unit, its_scores in zip(units, scores):
+                sums_ref[unit[0]] += weigh(unit, its_scores, highest_ref[unit[0], :1, :])
+            return carry
+
+        lax.fori_loop(0, (units_ref[base + units_max] + at_once - 1) // at_once, some, 0)
+
+    def only(base, unit, width, item):
+        its, *slots = read(base, unit, width)
+        return item, *(jnp.where(its == item, slot, -1) for slot in slots)
 
     def raise_highest(item, highest):
-        def look(turn, highest):
-            unit = only(turn, item)
-            scores = scores_of(unit)
-            for place, slot in enumerate(unit[1:]):
-                part = scores[place * block_len : (place + 1) * block_len]
-                found = jnp.max(part, axis=0, keepdims=True) * scale
-                highest = jnp.where(slot < 0, highest, jnp.maximum(highest, found))
-            return highest
-
-        return lax.fori_loop(0, count, look, highest)
+        for base, width, _ in lists:
+
+            def look(turn, highest, base=base, width=width):
+                unit = only(base, turn, width, item)
+                scores = scores_of(unit)
+                for place, slot in enumerate(unit[1:]):
+                    part = scores[place * block_len : (place + 1) * block_len]
+                    found = jnp.max(part, axis=0, keepdims=True) * scale
+                    highest = jnp.where(slot < 0, highest, jnp.maximum(highest, found))
+                return highest
+
+            highest = lax.fori_loop(0, units_ref[base + units_max], look, highest)
+        return highest
 
     def add_again(item, highest):
-        def add(turn, carry):
-            unit = only(turn, item)
-            sums_ref[item] += weigh(unit, scores_of(unit), highest)
-            return carry
-
-        lax.fori_loop(0, count, add, 0)
+        for base, width, _ in lists:
+
+            def add(turn, carry, base=base, width=width):
+                unit = only(base, turn, width, item)
+                sums_ref[item] += weigh(unit, scores_of(unit), highest)
+                return carry
+
+            lax.fori_loop(0, units_ref[base + units_max], add, 0)
 
     return raise_highest, add_again
 
@@ -439,27 +446,26 @@
 
 
 def list_units(open_slots, index, units_max):
-    lists, items, picks = index.shape
+    parts, items, picks = index.shape
     ahead = jnp.arange(picks)[:, None] < jnp.arange(picks)[None, :]
     place = jnp.sum(open_slots[..., :, None] & ahead, axis=-2)
-    half = jnp.arange(0, picks, 2)
-    hit = open_slots[..., :, None]
-    even = jnp.sum(
-        jnp.where(hit & (place[..., :, None] == half), index[..., :, None] + 1, 0), axis=-2
-    )
-    odd = jnp.sum(
-        jnp.where(hit & (place[..., :, None] == half + 1), index[..., :, None] + 1, 0), axis=-2
-    )
-    item = jnp.arange(items, dtype=jnp.int32)[None, :, None]
-    codes = ((item << (2 * FIELD)) + (even << FIELD) + odd).reshape(lists, -1)
-    filled = (even > 0).reshape(lists, -1)
+    width = -(-picks // WIDEST) * WIDEST
+    here = open_slots[..., :, None] & (place[..., :, None] == jnp.arange(width))
+    packed = jnp.sum(jnp.where(here, index[..., :, None] + 1, 0), axis=-2)
+    groups = packed.reshape(parts, items * (width // WIDEST), WIDEST)
+    shifts = jnp.arange(WIDEST - 1, -1, -1, dtype=jnp.int32) * FIELD
+    item = jnp.arange(groups.shape[1], dtype=jnp.int32) // (width // WIDEST)
+    codes = jnp.sum(groups << shifts, axis=-1) + (item << (WIDEST * FIELD))
+    held = jnp.sum(groups > 0, axis=-1)
+    narrow = UNIT_KINDS[1][0]
+    filled = jnp.stack([held > narrow, (held > 0) & (held <= narrow)], axis=1)
     ahead = jnp.arange(codes.shape[1])[:, None] < jnp.arange(codes.shape[1])[None, :]
-    place = jnp.sum(filled[:, :, None] & ahead, axis=1)
+    place = jnp.sum(filled[..., :, None] & ahead, axis=-2)
     target = jnp.arange(units_max + 1)
-    here = filled[:, :, None] & (place[:, :, None] == target)
-    count = jnp.sum(filled, axis=1, keepdims=True, dtype=jnp.int32)
-    listed = jnp.sum(jnp.where(here, codes[:, :, None], 0), axis=1)
-    return jnp.where(target == units_max, count, listed).astype(jnp.int32)
+    here = filled[..., :, None] & (place[..., :, None] == target)
+    count = jnp.sum(filled, axis=-1, keepdims=True, dtype=jnp.int32)
+    listed = jnp.sum(jnp.where(here, codes[:, None, :, None], 0), axis=-2)
+    return jnp.where(target == units_max, count, listed).astype(jnp.int32).reshape(parts, -1)
 
 
 def on_device(queries, keys, values, chosen):
@@ -474,10 +480,10 @@
     base = position * blocks
     first = lax.axis_index("rep") * query_heads // GROUP
     scale = LOG2E * head_dim**-0.5
-    at_once = next(n for n in (3, 2, 1) if blocks % n == 0)
+    at_once = next(n for n in (4, 3, 2, 1) if blocks % n == 0)
     given_at_once = next(n for n in (6, 4, 3, 2, 1) if blocks % n == 0)
-    units_max = blocks * used * ((picks + 1) // 2)
-    units_max = -(-units_max // UNITS_AT_ONCE) * UNITS_AT_ONCE
+    most = max(at_once for _, at_once in UNIT_KINDS)
+    units_max = -(-blocks * used * -(-picks // WIDEST) // most) * most
 
     lists = lax.dynamic_slice_in_dim(chosen, first, used, 0)
     wanted = jnp.stack(

time: 64.1 us -> 62.8 us (0.980)
  the two profiles are of different devices: /device:TPU:0 before, /device:TPU:18 now
where the time goes in v7:
time: 62.8 us; the launch traced here: 62.5 us
  Pallas kernels  47.5 us (76%)
  starting transfers between devices  10.8 us (17%)
  other arithmetic  2.22 us (4%)
  local copies, waits for them, and re-layouts  1.68 us (3%)
    pallas_call x1, Pallas kernels, local_part(): pl.pallas_call(functools.partial(local_kernel, kv_heads=kv_heads, **sizes...  27 us
    pallas_call x1, Pallas kernels, remote_part(): pl.pallas_call(functools.partial(remote_kernel, shifts=shifts, **sizes),...  16.9 us
    ppermute x3, starting transfers between devices, on_device(): lax.ppermute(parcel, 'ctx', [(i, i + d) for i in range(shards - d)])  6 us
    ppermute x3, starting transfers between devices, on_device(): lax.ppermute(chosen, 'ctx', [(j, j - d) for j in range(d, shards)])  4.81 us
    pallas_call x1, Pallas kernels, pack(): pl.pallas_call(functools.partial(pack_kernel, shifts=shifts, used=used, k...  3.63 us
  transfers between devices with their start and end apart: 6, of which 0 were waited for; matrix products, arithmetic and copies ran while one was open for 4% of the time, Pallas kernels for 43%

profile of v7, /device:TPU:18, one launch (start us, length us, event | category | flops | bytes accessed | tf_op | source)
XLA Modules:
  0.0 62.5 jit_solution(3884575761759863343)
XLA Ops:
  0.0 2.3 %collective-permute-start = (s32[4,24,8]{1,2,0:T(8,128)}, s32[4,24,8]{1,2,0:T(8,128)S(1)}, u32[]{:S(2)}, u32[]{:S(2)}) collective-permute-start(s32[4,24,8]{1,2,0:T(8,128)} %param.7), channel_id=1, source_target_pairs={{4,0},{8,4},{12,8},{5,1},{9,5},{13,9},{6,2},{10,6},{14,10},{7,3},{... | collective-permute-start | bytes 9224 | tf_op jit(solution)/shard_map/ppermute | solution.py:491
  2.4 0.7 %collective-permute-start.2 = (s32[4,24,8]{1,2,0:T(8,128)}, s32[4,24,8]{1,2,0:T(8,128)S(1)}, u32[]{:S(2)}, u32[]{:S(2)}) collective-permute-start(s32[4,24,8]{1,2,0:T(8,128)} %param.7), channel_id=1, source_target_pairs={{12,0},{13,1},{14,2},{15,3},{28,16},{29,17},{30,18},{31,19}} | collective-permute-start | bytes 9224 | tf_op jit(solution)/shard_map/ppermute | solution.py:491
  3.0 1.8 %collective-permute-start.1 = (s32[4,24,8]{1,2,0:T(8,128)}, s32[4,24,8]{1,2,0:T(8,128)S(1)}, u32[]{:S(2)}, u32[]{:S(2)}) collective-permute-start(s32[4,24,8]{1,2,0:T(8,128)} %param.7), channel_id=1, source_target_pairs={{8,0},{12,4},{9,1},{13,5},{10,2},{14,6},{11,3},{15,7},{24,16},{28,... | collective-permute-start | bytes 9224 | tf_op jit(solution)/shard_map/ppermute | solution.py:491
  5.0 0.7 %add_select_fusion = (s32[24,2,8]{0,2,1:T(8,128)S(1)}, s32[24,2,8]{0,2,1:T(8,128)S(1)}) fusion(s32[4,24,8]{1,2,0:T(8,128)} %param.7, s32[]{:T(128)S(6)} %select_n.91), kind=kLoop, calls=%fused_computation.25 | loop fusion | flops 3072 | bytes 4612 | tf_op jit(solution)/shard_map/jit(floor_divide)/jit(_where)/select_n | solution.py:522
  5.7 0.1 copy.70
  5.8 0.2 select_reduce_fusion.2
  6.6 0.2 convert_reduce_fusion.1
  6.8 0.1 convert_reduce_fusion.3
  6.9 0.1 copy.84
  7.0 0.1 convert_reduce_fusion
  7.2 0.2 select_reduce_fusion
  7.5 0.1 squeeze.7.units_ref
  7.5 0.1 squeeze.6.units_ref
  7.6 0.3 select_reduce_fusion.4
  8.0 0.1 copy.87
  8.1 0.1 copy.88
  8.2 0.1 copy.89
  8.3 0.7 %reshape.314.request = s32[12]{0:T(128)} reshape(s32[3,2,2]{2,1,0:T(2,128)S(1)} %copy.89) | data formatting | bytes 96 | tf_op jit(solution)/shard_map/reshape | solution.py:511
  8.9 3.6 %pack.1 = (bf16[2,2,256,128]{3,2,1,0:T(8,128)(2,1)S(1)}, bf16[2,2,256,128]{3,2,1,0:T(8,128)(2,1)S(1)}, bf16[2,2,256,128]{3,2,1,0:T(8,128)(2,1)S(1)}, f32[8,128]{1,0:T(8,128)S(1)}) custom-call(s32[12]{0:T(128)} %reshape.314.request, bf16[12288,128]{1,0:T(8,128)(2,1)} %bitcast.22, bf16[12288,128]{1,0:T(8,128)(2,1)} %bitcast.24, s32[1]{0:T(128)} %bitcast.7.rest_0_.first_ref), custom_call_target="tpu_custom_call" | custom-call | tf_op jit(solution)/shard_map/pack/pallas_call | solution.py:73
  12.6 4.0 %collective-permute-start.3 = (bf16[2,2,256,128]{3,2,1,0:T(8,128)(2,1)S(1)}, bf16[2,2,256,128]{3,2,1,0:T(8,128)(2,1)S(1)}, u32[]{:S(2)}, u32[]{:S(2)}) collective-permute-start(bf16[2,2,256,128]{3,2,1,0:T(8,128)(2,1)S(1)} %get-tuple-element.16), channel_id=1, source_target_pairs={{0,4},{4,8},{8,12},{1,5},{5,9},{9,13},{2,6},{6,10},{10,14},{3,7},{... | collective-permute-start | bytes 786440 | tf_op jit(solution)/shard_map/ppermute | solution.py:515
  16.6 1.3 %collective-permute-start.4 = (bf16[2,2,256,128]{3,2,1,0:T(8,128)(2,1)S(1)}, bf16[2,2,256,128]{3,2,1,0:T(8,128)(2,1)S(1)}, u32[]{:S(2)}, u32[]{:S(2)}) collective-permute-start(bf16[2,2,256,128]{3,2,1,0:T(8,128)(2,1)S(1)} %get-tuple-element.17), channel_id=1, source_target_pairs={{0,8},{4,12},{1,9},{5,13},{2,10},{6,14},{3,11},{7,15},{16,24},{20,... | collective-permute-start | bytes 786440 | tf_op jit(solution)/shard_map/ppermute | solution.py:515
  17.9 0.7 %collective-permute-start.5 = (bf16[2,2,256,128]{3,2,1,0:T(8,128)(2,1)S(1)}, bf16[2,2,256,128]{3,2,1,0:T(8,128)(2,1)S(1)}, u32[]{:S(2)}, u32[]{:S(2)}) collective-permute-start(bf16[2,2,256,128]{3,2,1,0:T(8,128)(2,1)S(1)} %get-tuple-element.18), channel_id=1, source_target_pairs={{0,12},{1,13},{2,14},{3,15},{16,28},{17,29},{18,30},{19,31}} | collective-permute-start | bytes 786440 | tf_op jit(solution)/shard_map/ppermute | solution.py:515
  18.6 27.0 %local_part.1 = (f32[48,144,512]{2,1,0:T(8,128)S(1)}, f32[48,8,512]{2,1,0:T(8,128)S(1)}, bf16[48,512,128]{2,1,0:T(8,128)(2,1)S(1)}) custom-call(s32[194]{0:T(256)S(1)} %squeeze.7.units_ref, s32[1]{0:T(128)} %bitcast.7.rest_0_.first_ref, bf16[24576,128]{1,0:T(8,128)(2,1)} %bitcast.34, bf16[12288,128]{1,0:T(8,128)(2,1)} %bitcast.23, ...), custom_call_target="tpu_custom_call" | custom-call | flops 17179869184 | bytes 33554432 | tf_op jit(solution)/shard_map/local_part/pallas_call | solution.py:382
  45.6 16.9 %remote_part.1 = bf16[24576,128]{1,0:T(8,128)(2,1)} custom-call(s32[194]{0:T(256)S(1)} %squeeze.6.units_ref, bf16[48,512,128]{2,1,0:T(8,128)(2,1)S(1)} %get-tuple-element.13.split_ref, f32[48,144,512]{2,1,0:T(8,128)S(1)} %get-tuple-element.14.sums_in, f32[48,8,512]{2,1,0:T(8,128)S(1)} %get-tuple-element.15.highest_ref, ...), custom_call_target="tpu_custom_call" | custom-call | tf_op jit(solution)/shard_map/remote_part/pallas_call | solution.py:425
  (32 shorter events, 0.7 us)
Async XLA Ops:
  0.0 7.6 %collective-permute-start = (s32[4,24,8]{1,2,0:T(8,128)}, s32[4,24,8]{1,2,0:T(8,128)S(1)}, u32[]{:S(2)}, u32[]{:S(2)}) collective-permute-start(s32[4,24,8]{1,2,0:T(8,128)} %param.7), channel_id=1, source_target_pairs={{4,0},{8,4},{12,8},{5,1},{9,5},{13,9},{6,2},{10,6},{14,10},{7,3},{... | collective-permute-start | bytes 9224 | tf_op jit(solution)/shard_map/ppermute | solution.py:491
  2.4 5.3 %collective-permute-start.2 = (s32[4,24,8]{1,2,0:T(8,128)}, s32[4,24,8]{1,2,0:T(8,128)S(1)}, u32[]{:S(2)}, u32[]{:S(2)}) collective-permute-start(s32[4,24,8]{1,2,0:T(8,128)} %param.7), channel_id=1, source_target_pairs={{12,0},{13,1},{14,2},{15,3},{28,16},{29,17},{30,18},{31,19}} | collective-permute-start | bytes 9224 | tf_op jit(solution)/shard_map/ppermute | solution.py:491
  3.0 4.6 %collective-permute-start.1 = (s32[4,24,8]{1,2,0:T(8,128)}, s32[4,24,8]{1,2,0:T(8,128)S(1)}, u32[]{:S(2)}, u32[]{:S(2)}) collective-permute-start(s32[4,24,8]{1,2,0:T(8,128)} %param.7), channel_id=1, source_target_pairs={{8,0},{12,4},{9,1},{13,5},{10,2},{14,6},{11,3},{15,7},{24,16},{28,... | collective-permute-start | bytes 9224 | tf_op jit(solution)/shard_map/ppermute | solution.py:491
  12.6 33.0 %collective-permute-start.3 = (bf16[2,2,256,128]{3,2,1,0:T(8,128)(2,1)S(1)}, bf16[2,2,256,128]{3,2,1,0:T(8,128)(2,1)S(1)}, u32[]{:S(2)}, u32[]{:S(2)}) collective-permute-start(bf16[2,2,256,128]{3,2,1,0:T(8,128)(2,1)S(1)} %get-tuple-element.16), channel_id=1, source_target_pairs={{0,4},{4,8},{8,12},{1,5},{5,9},{9,13},{2,6},{6,10},{10,14},{3,7},{... | collective-permute-start | bytes 786440 | tf_op jit(solution)/shard_map/ppermute | solution.py:515
  16.6 29.0 %collective-permute-start.4 = (bf16[2,2,256,128]{3,2,1,0:T(8,128)(2,1)S(1)}, bf16[2,2,256,128]{3,2,1,0:T(8,128)(2,1)S(1)}, u32[]{:S(2)}, u32[]{:S(2)}) collective-permute-start(bf16[2,2,256,128]{3,2,1,0:T(8,128)(2,1)S(1)} %get-tuple-element.17), channel_id=1, source_target_pairs={{0,8},{4,12},{1,9},{5,13},{2,10},{6,14},{3,11},{7,15},{16,24},{20,... | collective-permute-start | bytes 786440 | tf_op jit(solution)/shard_map/ppermute | solution.py:515
  17.9 27.7 %collective-permute-start.5 = (bf16[2,2,256,128]{3,2,1,0:T(8,128)(2,1)S(1)}, bf16[2,2,256,128]{3,2,1,0:T(8,128)(2,1)S(1)}, u32[]{:S(2)}, u32[]{:S(2)}) collective-permute-start(bf16[2,2,256,128]{3,2,1,0:T(8,128)(2,1)S(1)} %get-tuple-element.18), channel_id=1, source_target_pairs={{0,12},{1,13},{2,14},{3,15},{16,28},{17,29},{18,30},{19,31}} | collective-permute-start | bytes 786440 | tf_op jit(solution)/shard_map/ppermute | solution.py:515

commit v8 on v7

--- a/solution.py
+++ b/solution.py
@@ -15,10 +15,10 @@
 MASKED = -1e30
 CLOSED = 3e38
 SAFE_TOTAL = 2.0**100
-VMEM_BYTES = 60 * 2**20
-LOCAL_VMEM_BYTES = 22 * 2**20
-REMOTE_VMEM_BYTES = 22 * 2**20
-UNIT_KINDS = ((4, 4), (2, 4))
+PACK_VMEM_BYTES = 24 * 2**20
+LOCAL_VMEM_BYTES = 26 * 2**20
+REMOTE_VMEM_BYTES = 26 * 2**20
+UNIT_KINDS = ((4, 6), (2, 6))
 WIDEST = 4
 FIELD = 6
 ONES_ROWS = 16
@@ -87,7 +87,7 @@
         ),
         out_shape=[pltpu.VMEM(parcel, jnp.bfloat16)] * shifts
         + [pltpu.VMEM(row_shape, jnp.float32)],
-        compiler_params=pltpu.CompilerParams(vmem_limit_bytes=VMEM_BYTES),
+        compiler_params=pltpu.CompilerParams(vmem_limit_bytes=PACK_VMEM_BYTES),
         name="pack",
     )(request, keys, values, first)
 

time: 62.8 us -> 61.4 us (0.978); the launches traced: 62.5 us -> 60.5 us
  Pallas kernels: 47.5 us -> 46.1 us
    pallas_call x1, Pallas kernels: 27 us -> 26.2 us  [local_part(): pl.pallas_call(functools.partial(local_kernel, kv_heads=kv_heads, **sizes...]
where the time goes in v8:
time: 61.4 us; the launch traced here: 60.5 us
  Pallas kernels  46.1 us (75%)
  starting transfers between devices  10.8 us (18%)
  other arithmetic  2.22 us (4%)
  local copies, waits for them, and re-layouts  1.09 us (2%)
    pallas_call x1, Pallas kernels, local_part(): pl.pallas_call(functools.partial(local_kernel, kv_heads=kv_heads, **sizes...  26.2 us
    pallas_call x1, Pallas kernels, remote_part(): pl.pallas_call(functools.partial(remote_kernel, shifts=shifts, **sizes),...  16.4 us
    ppermute x3, starting transfers between devices, on_device(): lax.ppermute(parcel, 'ctx', [(i, i + d) for i in range(shards - d)])  6 us
    ppermute x3, starting transfers between devices, on_device(): lax.ppermute(chosen, 'ctx', [(j, j - d) for j in range(d, shards)])  4.81 us
    pallas_call x1, Pallas kernels, pack(): pl.pallas_call(functools.partial(pack_kernel, shifts=shifts, used=used, k...  3.51 us
  transfers between devices with their start and end apart: 6, of which 0 were waited for; matrix products, arithmetic and copies ran while one was open for 4% of the time, Pallas kernels for 43%

profile of v8, /device:TPU:18, one launch (start us, length us, event | category | flops | bytes accessed | tf_op | source)
XLA Modules:
  0.0 60.5 jit_solution(1571418803283616397)
XLA Ops:
  0.0 2.3 %collective-permute-start = (s32[4,24,8]{1,2,0:T(8,128)}, s32[4,24,8]{1,2,0:T(8,128)S(1)}, u32[]{:S(2)}, u32[]{:S(2)}) collective-permute-start(s32[4,24,8]{1,2,0:T(8,128)} %param.7), channel_id=1, source_target_pairs={{4,0},{8,4},{12,8},{5,1},{9,5},{13,9},{6,2},{10,6},{14,10},{7,3},{... | collective-permute-start | bytes 9224 | tf_op jit(solution)/shard_map/ppermute | solution.py:491
  2.4 0.7 %collective-permute-start.2 = (s32[4,24,8]{1,2,0:T(8,128)}, s32[4,24,8]{1,2,0:T(8,128)S(1)}, u32[]{:S(2)}, u32[]{:S(2)}) collective-permute-start(s32[4,24,8]{1,2,0:T(8,128)} %param.7), channel_id=1, source_target_pairs={{12,0},{13,1},{14,2},{15,3},{28,16},{29,17},{30,18},{31,19}} | collective-permute-start | bytes 9224 | tf_op jit(solution)/shard_map/ppermute | solution.py:491
  3.0 1.8 %collective-permute-start.1 = (s32[4,24,8]{1,2,0:T(8,128)}, s32[4,24,8]{1,2,0:T(8,128)S(1)}, u32[]{:S(2)}, u32[]{:S(2)}) collective-permute-start(s32[4,24,8]{1,2,0:T(8,128)} %param.7), channel_id=1, source_target_pairs={{8,0},{12,4},{9,1},{13,5},{10,2},{14,6},{11,3},{15,7},{24,16},{28,... | collective-permute-start | bytes 9224 | tf_op jit(solution)/shard_map/ppermute | solution.py:491
  5.0 0.7 %add_select_fusion = (s32[24,2,8]{0,2,1:T(8,128)S(1)}, s32[24,2,8]{0,2,1:T(8,128)S(1)}) fusion(s32[4,24,8]{1,2,0:T(8,128)} %param.7, s32[]{:T(128)S(6)} %select_n.91), kind=kLoop, calls=%fused_computation.25 | loop fusion | flops 3072 | bytes 4612 | tf_op jit(solution)/shard_map/jit(floor_divide)/jit(_where)/select_n | solution.py:522
  5.7 0.1 copy.70
  5.8 0.2 select_reduce_fusion.2
  6.6 0.2 convert_reduce_fusion.1
  6.8 0.1 convert_reduce_fusion.3
  6.9 0.1 copy.84
  7.0 0.1 convert_reduce_fusion
  7.2 0.2 select_reduce_fusion
  7.5 0.1 squeeze.7.units_ref
  7.5 0.1 squeeze.6.units_ref
  7.6 0.3 select_reduce_fusion.4
  8.0 0.1 copy.87
  8.1 0.1 copy.88
  8.2 0.1 copy.89
  8.3 0.1 reshape.314.request
  8.3 3.5 %pack.1 = (bf16[2,2,256,128]{3,2,1,0:T(8,128)(2,1)S(1)}, bf16[2,2,256,128]{3,2,1,0:T(8,128)(2,1)S(1)}, bf16[2,2,256,128]{3,2,1,0:T(8,128)(2,1)S(1)}, f32[8,128]{1,0:T(8,128)S(1)}) custom-call(s32[12]{0:T(128)S(1)} %reshape.314.request, bf16[12288,128]{1,0:T(8,128)(2,1)} %bitcast.22, bf16[12288,128]{1,0:T(8,128)(2,1)} %bitcast.24, s32[1]{0:T(128)} %bitcast.7.rest_0_.first_ref), custom_call_target="tpu_custom_call" | custom-call | tf_op jit(solution)/shard_map/pack/pallas_call | solution.py:73
  11.9 4.0 %collective-permute-start.3 = (bf16[2,2,256,128]{3,2,1,0:T(8,128)(2,1)S(1)}, bf16[2,2,256,128]{3,2,1,0:T(8,128)(2,1)S(1)}, u32[]{:S(2)}, u32[]{:S(2)}) collective-permute-start(bf16[2,2,256,128]{3,2,1,0:T(8,128)(2,1)S(1)} %get-tuple-element.16), channel_id=1, source_target_pairs={{0,4},{4,8},{8,12},{1,5},{5,9},{9,13},{2,6},{6,10},{10,14},{3,7},{... | collective-permute-start | bytes 786440 | tf_op jit(solution)/shard_map/ppermute | solution.py:515
  15.9 1.3 %collective-permute-start.4 = (bf16[2,2,256,128]{3,2,1,0:T(8,128)(2,1)S(1)}, bf16[2,2,256,128]{3,2,1,0:T(8,128)(2,1)S(1)}, u32[]{:S(2)}, u32[]{:S(2)}) collective-permute-start(bf16[2,2,256,128]{3,2,1,0:T(8,128)(2,1)S(1)} %get-tuple-element.17), channel_id=1, source_target_pairs={{0,8},{4,12},{1,9},{5,13},{2,10},{6,14},{3,11},{7,15},{16,24},{20,... | collective-permute-start | bytes 786440 | tf_op jit(solution)/shard_map/ppermute | solution.py:515
  17.2 0.7 %collective-permute-start.5 = (bf16[2,2,256,128]{3,2,1,0:T(8,128)(2,1)S(1)}, bf16[2,2,256,128]{3,2,1,0:T(8,128)(2,1)S(1)}, u32[]{:S(2)}, u32[]{:S(2)}) collective-permute-start(bf16[2,2,256,128]{3,2,1,0:T(8,128)(2,1)S(1)} %get-tuple-element.18), channel_id=1, source_target_pairs={{0,12},{1,13},{2,14},{3,15},{16,28},{17,29},{18,30},{19,31}} | collective-permute-start | bytes 786440 | tf_op jit(solution)/shard_map/ppermute | solution.py:515
  17.9 26.2 %local_part.1 = (f32[48,144,512]{2,1,0:T(8,128)S(1)}, f32[48,8,512]{2,1,0:T(8,128)S(1)}, bf16[48,512,128]{2,1,0:T(8,128)(2,1)S(1)}) custom-call(s32[194]{0:T(256)S(1)} %squeeze.7.units_ref, s32[1]{0:T(128)} %bitcast.7.rest_0_.first_ref, bf16[24576,128]{1,0:T(8,128)(2,1)} %bitcast.34, bf16[12288,128]{1,0:T(8,128)(2,1)} %bitcast.23, ...), custom_call_target="tpu_custom_call" | custom-call | flops 17179869184 | bytes 33554432 | tf_op jit(solution)/shard_map/local_part/pallas_call | solution.py:382
  44.1 16.4 %remote_part.1 = bf16[24576,128]{1,0:T(8,128)(2,1)} custom-call(s32[194]{0:T(256)S(1)} %squeeze.6.units_ref, bf16[48,512,128]{2,1,0:T(8,128)(2,1)S(1)} %get-tuple-element.13.split_ref, f32[48,144,512]{2,1,0:T(8,128)S(1)} %get-tuple-element.14.sums_in, f32[48,8,512]{2,1,0:T(8,128)S(1)} %get-tuple-element.15.highest_ref, ...), custom_call_target="tpu_custom_call" | custom-call | tf_op jit(solution)/shard_map/remote_part/pallas_call | solution.py:425
  (32 shorter events, 0.7 us)
Async XLA Ops:
  0.0 7.6 %collective-permute-start = (s32[4,24,8]{1,2,0:T(8,128)}, s32[4,24,8]{1,2,0:T(8,128)S(1)}, u32[]{:S(2)}, u32[]{:S(2)}) collective-permute-start(s32[4,24,8]{1,2,0:T(8,128)} %param.7), channel_id=1, source_target_pairs={{4,0},{8,4},{12,8},{5,1},{9,5},{13,9},{6,2},{10,6},{14,10},{7,3},{... | collective-permute-start | bytes 9224 | tf_op jit(solution)/shard_map/ppermute | solution.py:491
  2.4 5.3 %collective-permute-start.2 = (s32[4,24,8]{1,2,0:T(8,128)}, s32[4,24,8]{1,2,0:T(8,128)S(1)}, u32[]{:S(2)}, u32[]{:S(2)}) collective-permute-start(s32[4,24,8]{1,2,0:T(8,128)} %param.7), channel_id=1, source_target_pairs={{12,0},{13,1},{14,2},{15,3},{28,16},{29,17},{30,18},{31,19}} | collective-permute-start | bytes 9224 | tf_op jit(solution)/shard_map/ppermute | solution.py:491
  3.0 4.6 %collective-permute-start.1 = (s32[4,24,8]{1,2,0:T(8,128)}, s32[4,24,8]{1,2,0:T(8,128)S(1)}, u32[]{:S(2)}, u32[]{:S(2)}) collective-permute-start(s32[4,24,8]{1,2,0:T(8,128)} %param.7), channel_id=1, source_target_pairs={{8,0},{12,4},{9,1},{13,5},{10,2},{14,6},{11,3},{15,7},{24,16},{28,... | collective-permute-start | bytes 9224 | tf_op jit(solution)/shard_map/ppermute | solution.py:491
  11.9 32.2 %collective-permute-start.3 = (bf16[2,2,256,128]{3,2,1,0:T(8,128)(2,1)S(1)}, bf16[2,2,256,128]{3,2,1,0:T(8,128)(2,1)S(1)}, u32[]{:S(2)}, u32[]{:S(2)}) collective-permute-start(bf16[2,2,256,128]{3,2,1,0:T(8,128)(2,1)S(1)} %get-tuple-element.16), channel_id=1, source_target_pairs={{0,4},{4,8},{8,12},{1,5},{5,9},{9,13},{2,6},{6,10},{10,14},{3,7},{... | collective-permute-start | bytes 786440 | tf_op jit(solution)/shard_map/ppermute | solution.py:515
  15.9 28.2 %collective-permute-start.4 = (bf16[2,2,256,128]{3,2,1,0:T(8,128)(2,1)S(1)}, bf16[2,2,256,128]{3,2,1,0:T(8,128)(2,1)S(1)}, u32[]{:S(2)}, u32[]{:S(2)}) collective-permute-start(bf16[2,2,256,128]{3,2,1,0:T(8,128)(2,1)S(1)} %get-tuple-element.17), channel_id=1, source_target_pairs={{0,8},{4,12},{1,9},{5,13},{2,10},{6,14},{3,11},{7,15},{16,24},{20,... | collective-permute-start | bytes 786440 | tf_op jit(solution)/shard_map/ppermute | solution.py:515
  17.2 26.9 %collective-permute-start.5 = (bf16[2,2,256,128]{3,2,1,0:T(8,128)(2,1)S(1)}, bf16[2,2,256,128]{3,2,1,0:T(8,128)(2,1)S(1)}, u32[]{:S(2)}, u32[]{:S(2)}) collective-permute-start(bf16[2,2,256,128]{3,2,1,0:T(8,128)(2,1)S(1)} %get-tuple-element.18), channel_id=1, source_target_pairs={{0,12},{1,13},{2,14},{3,15},{16,28},{17,29},{18,30},{19,31}} | collective-permute-start | bytes 786440 | tf_op jit(solution)/shard_map/ppermute | solution.py:515

commit v9 on v8

--- a/solution.py
+++ b/solution.py
@@ -318,17 +318,21 @@
                 ]
                 value_table[head, at * height + head_dim : (at + 1) * height, :] = ones
 
-    def take(item, carry):
-        sums_ref[item] = sums_in[item]
+    listed = units_ref[units_max] + units_ref[2 * units_max + 1] > 0
+    together = next(n for n in (4, 2, 1) if blocks * used % n == 0)
+
+    def take(turn, carry):
+        for n in range(together):
+            sums_ref[turn * together + n] = sums_in[turn * together + n]
         return carry
 
-    lax.fori_loop(0, blocks * used, take, 0)
+    lax.fori_loop(0, jnp.where(listed, blocks * used // together, 0), take, 0)
     raise_highest, add_again = attend_units(
         units_ref, split_ref, key_table, value_table, highest_ref, sums_ref,
         used=used, block_len=block_len, scale=scale, units_max=units_max,
     )
 
-    @pl.when(unsafe(sums_ref, head_dim))
+    @pl.when(listed & unsafe(sums_ref, head_dim))
     def _():
         def mend(item, carry):
             before = highest_ref[item][:1]
@@ -346,7 +350,7 @@
         place = pl.ds(pl.multiple_of(turn * rows, rows), rows)
         return pltpu.make_async_copy(staged.at[slot], out_ref.at[place], sems.at[slot])
 
-    def finish(turn, carry):
+    def finish(source, turn, carry):
         slot = lax.rem(turn, 2)
 
         @pl.when(turn >= 2)
@@ -357,14 +361,17 @@
             parts = []
             for head in range(used):
                 item = (turn * at_once + n) * used + head
-                total = sums_ref[item, head_dim : head_dim + 1, :]
-                parts.append((sums_ref[item, :head_dim, :] * (1.0 / total)).T)
+                total = source[item, head_dim : head_dim + 1, :]
+                parts.append((source[item, :head_dim, :] * (1.0 / total)).T)
             staged[slot, n * query_rows : (n + 1) * query_rows, :] = join_heads(*parts)
         give(turn).start()
         return carry
 
     turns = blocks // at_once
-    lax.fori_loop(0, turns, finish, 0)
+    for here, source in ((listed, sums_ref), (jnp.logical_not(listed), sums_in)):
+        lax.fori_loop(
+            0, jnp.where(here, turns, 0), functools.partial(finish, source), 0
+        )
     for turn in range(max(0, turns - 2), turns):
         give(turn).wait()
 

time: 61.4 us -> 60.7 us (0.989)
    pallas_call x1, Pallas kernels: 26.2 us -> 25.3 us  [local_part(): pl.pallas_call(functools.partial(local_kernel, kv_heads=kv_heads, **sizes...]
  transfers between devices with their start and end apart: 6 -> 6, of which waited for: 0 -> 0; matrix products, arithmetic and copies ran while one was open for 4% -> 4% of each run, Pallas kernels for 43% -> 42%
where the time goes in v9:
time: 60.7 us; the launch traced here: 60.2 us
  Pallas kernels  45.8 us (75%)
  starting transfers between devices  10.8 us (18%)
  other arithmetic  2.22 us (4%)
  local copies, waits for them, and re-layouts  1.09 us (2%)
    pallas_call x1, Pallas kernels, local_part(): pl.pallas_call(functools.partial(local_kernel, kv_heads=kv_heads, **sizes...  25.3 us
    pallas_call x1, Pallas kernels, remote_part(): pl.pallas_call(functools.partial(remote_kernel, shifts=shifts, **sizes),...  17 us
    ppermute x3, starting transfers between devices, on_device(): lax.ppermute(parcel, 'ctx', [(i, i + d) for i in range(shards - d)])  6 us
    ppermute x3, starting transfers between devices, on_device(): lax.ppermute(chosen, 'ctx', [(j, j - d) for j in range(d, shards)])  4.81 us
    pallas_call x1, Pallas kernels, pack(): pl.pallas_call(functools.partial(pack_kernel, shifts=shifts, used=used, k...  3.51 us
  transfers between devices with their start and end apart: 6, of which 0 were waited for; matrix products, arithmetic and copies ran while one was open for 4% of the time, Pallas kernels for 42%

profile of v9, /device:TPU:18, one launch (start us, length us, event | category | flops | bytes accessed | tf_op | source)
XLA Modules:
  0.0 60.2 jit_solution(4896846091256709383)
XLA Ops:
  0.0 2.3 %collective-permute-start = (s32[4,24,8]{1,2,0:T(8,128)}, s32[4,24,8]{1,2,0:T(8,128)S(1)}, u32[]{:S(2)}, u32[]{:S(2)}) collective-permute-start(s32[4,24,8]{1,2,0:T(8,128)} %param.7), channel_id=1, source_target_pairs={{4,0},{8,4},{12,8},{5,1},{9,5},{13,9},{6,2},{10,6},{14,10},{7,3},{... | collective-permute-start | bytes 9224 | tf_op jit(solution)/shard_map/ppermute | solution.py:498
  2.4 0.7 %collective-permute-start.2 = (s32[4,24,8]{1,2,0:T(8,128)}, s32[4,24,8]{1,2,0:T(8,128)S(1)}, u32[]{:S(2)}, u32[]{:S(2)}) collective-permute-start(s32[4,24,8]{1,2,0:T(8,128)} %param.7), channel_id=1, source_target_pairs={{12,0},{13,1},{14,2},{15,3},{28,16},{29,17},{30,18},{31,19}} | collective-permute-start | bytes 9224 | tf_op jit(solution)/shard_map/ppermute | solution.py:498
  3.0 1.8 %collective-permute-start.1 = (s32[4,24,8]{1,2,0:T(8,128)}, s32[4,24,8]{1,2,0:T(8,128)S(1)}, u32[]{:S(2)}, u32[]{:S(2)}) collective-permute-start(s32[4,24,8]{1,2,0:T(8,128)} %param.7), channel_id=1, source_target_pairs={{8,0},{12,4},{9,1},{13,5},{10,2},{14,6},{11,3},{15,7},{24,16},{28,... | collective-permute-start | bytes 9224 | tf_op jit(solution)/shard_map/ppermute | solution.py:498
  5.0 0.7 %add_select_fusion = (s32[24,2,8]{0,2,1:T(8,128)S(1)}, s32[24,2,8]{0,2,1:T(8,128)S(1)}) fusion(s32[4,24,8]{1,2,0:T(8,128)} %param.7, s32[]{:T(128)S(6)} %select_n.91), kind=kLoop, calls=%fused_computation.25 | loop fusion | flops 3072 | bytes 4612 | tf_op jit(solution)/shard_map/jit(floor_divide)/jit(_where)/select_n | solution.py:529
  5.7 0.1 copy.70
  5.8 0.2 select_reduce_fusion.2
  6.6 0.2 convert_reduce_fusion.1
  6.8 0.1 convert_reduce_fusion.3
  6.9 0.1 copy.84
  7.0 0.1 convert_reduce_fusion
  7.2 0.2 select_reduce_fusion
  7.5 0.1 squeeze.7.units_ref
  7.5 0.1 squeeze.6.units_ref
  7.6 0.3 select_reduce_fusion.4
  8.0 0.1 copy.87
  8.1 0.1 copy.88
  8.2 0.1 copy.89
  8.3 0.1 reshape.314.request
  8.3 3.5 %pack.1 = (bf16[2,2,256,128]{3,2,1,0:T(8,128)(2,1)S(1)}, bf16[2,2,256,128]{3,2,1,0:T(8,128)(2,1)S(1)}, bf16[2,2,256,128]{3,2,1,0:T(8,128)(2,1)S(1)}, f32[8,128]{1,0:T(8,128)S(1)}) custom-call(s32[12]{0:T(128)S(1)} %reshape.314.request, bf16[12288,128]{1,0:T(8,128)(2,1)} %bitcast.22, bf16[12288,128]{1,0:T(8,128)(2,1)} %bitcast.24, s32[1]{0:T(128)} %bitcast.7.rest_0_.first_ref), custom_call_target="tpu_custom_call" | custom-call | tf_op jit(solution)/shard_map/pack/pallas_call | solution.py:73
  11.9 4.0 %collective-permute-start.3 = (bf16[2,2,256,128]{3,2,1,0:T(8,128)(2,1)S(1)}, bf16[2,2,256,128]{3,2,1,0:T(8,128)(2,1)S(1)}, u32[]{:S(2)}, u32[]{:S(2)}) collective-permute-start(bf16[2,2,256,128]{3,2,1,0:T(8,128)(2,1)S(1)} %get-tuple-element.16), channel_id=1, source_target_pairs={{0,4},{4,8},{8,12},{1,5},{5,9},{9,13},{2,6},{6,10},{10,14},{3,7},{... | collective-permute-start | bytes 786440 | tf_op jit(solution)/shard_map/ppermute | solution.py:522
  15.9 1.3 %collective-permute-start.4 = (bf16[2,2,256,128]{3,2,1,0:T(8,128)(2,1)S(1)}, bf16[2,2,256,128]{3,2,1,0:T(8,128)(2,1)S(1)}, u32[]{:S(2)}, u32[]{:S(2)}) collective-permute-start(bf16[2,2,256,128]{3,2,1,0:T(8,128)(2,1)S(1)} %get-tuple-element.17), channel_id=1, source_target_pairs={{0,8},{4,12},{1,9},{5,13},{2,10},{6,14},{3,11},{7,15},{16,24},{20,... | collective-permute-start | bytes 786440 | tf_op jit(solution)/shard_map/ppermute | solution.py:522
  17.2 0.7 %collective-permute-start.5 = (bf16[2,2,256,128]{3,2,1,0:T(8,128)(2,1)S(1)}, bf16[2,2,256,128]{3,2,1,0:T(8,128)(2,1)S(1)}, u32[]{:S(2)}, u32[]{:S(2)}) collective-permute-start(bf16[2,2,256,128]{3,2,1,0:T(8,128)(2,1)S(1)} %get-tuple-element.18), channel_id=1, source_target_pairs={{0,12},{1,13},{2,14},{3,15},{16,28},{17,29},{18,30},{19,31}} | collective-permute-start | bytes 786440 | tf_op jit(solution)/shard_map/ppermute | solution.py:522
  17.9 25.3 %local_part.1 = (f32[48,144,512]{2,1,0:T(8,128)S(1)}, f32[48,8,512]{2,1,0:T(8,128)S(1)}, bf16[48,512,128]{2,1,0:T(8,128)(2,1)S(1)}) custom-call(s32[194]{0:T(256)S(1)} %squeeze.7.units_ref, s32[1]{0:T(128)} %bitcast.7.rest_0_.first_ref, bf16[24576,128]{1,0:T(8,128)(2,1)} %bitcast.34, bf16[12288,128]{1,0:T(8,128)(2,1)} %bitcast.23, ...), custom_call_target="tpu_custom_call" | custom-call | flops 17179869184 | bytes 33554432 | tf_op jit(solution)/shard_map/local_part/pallas_call | solution.py:389
  43.2 17.0 %remote_part.1 = bf16[24576,128]{1,0:T(8,128)(2,1)} custom-call(s32[194]{0:T(256)S(1)} %squeeze.6.units_ref, bf16[48,512,128]{2,1,0:T(8,128)(2,1)S(1)} %get-tuple-element.13.split_ref, f32[48,144,512]{2,1,0:T(8,128)S(1)} %get-tuple-element.14.sums_in, f32[48,8,512]{2,1,0:T(8,128)S(1)} %get-tuple-element.15.highest_ref, ...), custom_call_target="tpu_custom_call" | custom-call | tf_op jit(solution)/shard_map/remote_part/pallas_call | solution.py:432
  (32 shorter events, 0.7 us)
Async XLA Ops:
  0.0 7.6 %collective-permute-start = (s32[4,24,8]{1,2,0:T(8,128)}, s32[4,24,8]{1,2,0:T(8,128)S(1)}, u32[]{:S(2)}, u32[]{:S(2)}) collective-permute-start(s32[4,24,8]{1,2,0:T(8,128)} %param.7), channel_id=1, source_target_pairs={{4,0},{8,4},{12,8},{5,1},{9,5},{13,9},{6,2},{10,6},{14,10},{7,3},{... | collective-permute-start | bytes 9224 | tf_op jit(solution)/shard_map/ppermute | solution.py:498
  2.4 5.3 %collective-permute-start.2 = (s32[4,24,8]{1,2,0:T(8,128)}, s32[4,24,8]{1,2,0:T(8,128)S(1)}, u32[]{:S(2)}, u32[]{:S(2)}) collective-permute-start(s32[4,24,8]{1,2,0:T(8,128)} %param.7), channel_id=1, source_target_pairs={{12,0},{13,1},{14,2},{15,3},{28,16},{29,17},{30,18},{31,19}} | collective-permute-start | bytes 9224 | tf_op jit(solution)/shard_map/ppermute | solution.py:498
  3.0 4.6 %collective-permute-start.1 = (s32[4,24,8]{1,2,0:T(8,128)}, s32[4,24,8]{1,2,0:T(8,128)S(1)}, u32[]{:S(2)}, u32[]{:S(2)}) collective-permute-start(s32[4,24,8]{1,2,0:T(8,128)} %param.7), channel_id=1, source_target_pairs={{8,0},{12,4},{9,1},{13,5},{10,2},{14,6},{11,3},{15,7},{24,16},{28,... | collective-permute-start | bytes 9224 | tf_op jit(solution)/shard_map/ppermute | solution.py:498
  11.9 31.3 %collective-permute-start.3 = (bf16[2,2,256,128]{3,2,1,0:T(8,128)(2,1)S(1)}, bf16[2,2,256,128]{3,2,1,0:T(8,128)(2,1)S(1)}, u32[]{:S(2)}, u32[]{:S(2)}) collective-permute-start(bf16[2,2,256,128]{3,2,1,0:T(8,128)(2,1)S(1)} %get-tuple-element.16), channel_id=1, source_target_pairs={{0,4},{4,8},{8,12},{1,5},{5,9},{9,13},{2,6},{6,10},{10,14},{3,7},{... | collective-permute-start | bytes 786440 | tf_op jit(solution)/shard_map/ppermute | solution.py:522
  15.9 27.3 %collective-permute-start.4 = (bf16[2,2,256,128]{3,2,1,0:T(8,128)(2,1)S(1)}, bf16[2,2,256,128]{3,2,1,0:T(8,128)(2,1)S(1)}, u32[]{:S(2)}, u32[]{:S(2)}) collective-permute-start(bf16[2,2,256,128]{3,2,1,0:T(8,128)(2,1)S(1)} %get-tuple-element.17), channel_id=1, source_target_pairs={{0,8},{4,12},{1,9},{5,13},{2,10},{6,14},{3,11},{7,15},{16,24},{20,... | collective-permute-start | bytes 786440 | tf_op jit(solution)/shard_map/ppermute | solution.py:522
  17.2 26.0 %collective-permute-start.5 = (bf16[2,2,256,128]{3,2,1,0:T(8,128)(2,1)S(1)}, bf16[2,2,256,128]{3,2,1,0:T(8,128)(2,1)S(1)}, u32[]{:S(2)}, u32[]{:S(2)}) collective-permute-start(bf16[2,2,256,128]{3,2,1,0:T(8,128)(2,1)S(1)} %get-tuple-element.18), channel_id=1, source_target_pairs={{0,12},{1,13},{2,14},{3,15},{16,28},{17,29},{18,30},{19,31}} | collective-permute-start | bytes 786440 | tf_op jit(solution)/shard_map/ppermute | solution.py:522
